TPU v7x, 512 devices: a whole 4x4x16 slice. The times are simulated.
512 devices in a mesh: sx: 32 (over z, x_lo), sy: 16 (over x_hi, y, core).
Axes of the slice: x: 4 (x_hi: 2, x_lo: 2; x = x_hi * 2 + x_lo), y: 4, z: 16, core: 2. Of those that a mesh axis runs over, the one named last changes fastest.
Arguments:
- gap: float32 [32, 16, 384], P('sx', 'sy')
- kinv: float32 [32, 16, 768, 768], P('sx', 'sy')
- schur: float32 [32, 16, 768, 768], P('sx', 'sy')
- corner_modes: float32 [32, 16, 24, 768], P('sx', 'sy'), may hold values from -0.4375 to 0.4375
- coarse_inverse: float32 [3072, 3072], P(('sx', 'sy'))
- edge_map: int32 [32, 16, 768], P('sx', 'sy'), may hold values from 0 to 767, each once within a row
- corner_map: int32 [32, 16, 24], P('sx', 'sy'), may hold values from 0 to 3072, as said below
- links: int32 [32, 16, 2], P('sx', 'sy'), may hold values 0 or 1
Outputs:
- multipliers: float32 [32, 16, 384], P('sx', 'sy')
- residual: float32 [32, 16, 384], P('sx', 'sy')
Inputs may be any that keep to these rules, and one draw needn't show every extreme that they name: `corner_map`: each coarse degree of freedom is named by the corners of at most four subdomains; corners in the last row or column of the slab's node grid are clamped and hold 3072; the coarse index of a node's dof d is its node number times 6 plus d.
All inputs are finite; a program needn't handle non-finite values. No bound on the sum of `links` on one device may be relied on, other than what follows from the above.
Results may differ from a plain program's by a relative error of at most 0.0003.
Values sent between devices are 32-bit elements; how exact they have to be, the bound alone decides.
No kernel may reach another device: no remote copies, remote signals or barrier semaphores. Data moves between devices by JAX's collectives and lax.ppermute only.
A program may use at most 64 MiB of HBM per device.

v0:
```python
import jax
import jax.numpy as jnp
from jax import lax
from jax.sharding import PartitionSpec as P

ITERS = 3


def shifted(block, axis, distance):
    devices = range(lax.axis_size(axis))
    route = [(i - distance, i) for i in devices if i - distance in devices]
    return lax.ppermute(block, axis, route)


def on_device(gap, kinv, schur, corner_modes, coarse_inverse, edge_map, corner_map, links):
    width = kinv.shape[-1]
    edge = width // 4
    highest = lax.Precision.HIGHEST
    row_here = lax.axis_index("sx")
    col_here = lax.axis_index("sy")
    nrows = lax.axis_size("sx")
    ncols = lax.axis_size("sy")
    link_here = links.reshape(2)
    east_ok = ((col_here < ncols - 1) & (link_here[0] == 1)).astype(jnp.float32)
    south_ok = ((row_here < nrows - 1) & (link_here[1] == 1)).astype(jnp.float32)
    mask = jnp.concatenate(
        [
            jnp.full((edge,), 1.0, jnp.float32) * east_ok,
            jnp.full((edge,), 1.0, jnp.float32) * south_ok,
        ]
    )
    local_map = edge_map.reshape(width)
    kinv_perm = jnp.take(jnp.take(kinv.reshape(width, width), local_map, axis=0), local_map, axis=1)
    schur_perm = jnp.take(
        jnp.take(schur.reshape(width, width), local_map, axis=0), local_map, axis=1
    )
    modes_perm = jnp.take(corner_modes.reshape(-1, width), local_map, axis=1)
    cmap = corner_map.reshape(-1)
    ncoarse = coarse_inverse.shape[1]

    def spread(field):
        east = field[:edge]
        south = field[edge:]
        from_west = shifted(east, "sy", 1)
        from_north = shifted(south, "sx", 1)
        return jnp.concatenate([east, south, -from_west, -from_north])

    def jump(iface):
        from_east = shifted(iface[2 * edge : 3 * edge], "sy", -1)
        from_south = shifted(iface[3 * edge :], "sx", -1)
        return (
            jnp.concatenate([iface[:edge] - from_east, iface[edge : 2 * edge] - from_south]) * mask
        )

    def precondition(field):
        return 0.25 * jump(jnp.dot(schur_perm, spread(field), precision=highest))

    multipliers = jnp.zeros((2 * edge,), jnp.float32)
    residual = mask * gap.reshape(2 * edge)

    def residual_dot(field, precond_field):
        return lax.psum(jnp.sum(field * precond_field), ("sx", "sy"))

    precond = precondition(residual)
    direction = precond
    norm_now = residual_dot(residual, precond)
    for step in range(ITERS):
        operator_iface = spread(direction)
        inner = jnp.dot(kinv_perm, operator_iface, precision=highest)
        operator_loads = jnp.dot(modes_perm, operator_iface, precision=highest)
        onehot = (cmap[:, None] == jnp.arange(ncoarse, dtype=jnp.int32)[None, :]).astype(
            jnp.float32
        )
        partial_load = jnp.dot(operator_loads, onehot, precision=highest)
        coarse = lax.psum(partial_load, ("sx", "sy"))
        owned = jnp.dot(coarse_inverse, coarse, precision=highest)
        solved = lax.all_gather(owned, ("sx", "sy"), axis=0, tiled=True)
        corner_vals = jnp.concatenate([solved, jnp.zeros((1,), jnp.float32)])[cmap]
        image = jump(inner + jnp.dot(corner_vals, modes_perm, precision=highest))
        alpha = norm_now / lax.psum(jnp.sum(direction * image), ("sx", "sy"))
        multipliers = multipliers + alpha * direction
        residual = residual - alpha * image
        if step + 1 < ITERS:
            precond = precondition(residual)
            norm_next = residual_dot(residual, precond)
            direction = precond + norm_next / norm_now * direction
            norm_now = norm_next
    return (multipliers.reshape(gap.shape), residual.reshape(gap.shape))


def solution(mesh):
    placed = (
        P("sx", "sy", None),
        P("sx", "sy", None, None),
        P("sx", "sy", None, None),
        P("sx", "sy", None, None),
        P(("sx", "sy"), None),
        P("sx", "sy", None),
        P("sx", "sy", None),
        P("sx", "sy", None),
    )
    return jax.shard_map(
        on_device,
        mesh=mesh,
        in_specs=placed,
        out_specs=(P("sx", "sy", None), P("sx", "sy", None)),
        check_vma=False,
    )
```

profile of v0, /device:TPU:1, one launch (start us, length us, event | category | flops | bytes accessed | tf_op | source)
XLA Modules:
  0.0 1323.9 jit_solution(4170784154035818391)
XLA Ops:
  4.2 4.6 collective-permute-start
  8.8 3.1 collective-permute-start.1
  12.6 3.5 gather_fusion.6
  16.1 5.8 gather_fusion.4
  21.9 4.9 broadcast_select_fusion
  26.8 3.1 copy.13
  29.9 5.8 gather_fusion.5
  35.7 3.2 fusion.30
  38.9 3.7 collective-permute-start.2
  45.2 3.2 collective-permute-done.3
  48.6 2.9 collective-permute-start.4
  51.5 4.4 collective-permute-start.5
  55.9 3.1 copy.14
  59.0 5.8 gather_fusion.7
  66.7 3.2 fusion.39
  70.6 113.0 %psum.64 = f32[3072]{0:T(1024)S(1)} all-reduce(f32[3072]{0:T(1024)S(1)} %bitcast.105), channel_id=1, replica_groups=mesh['sx'=32,'sy'=16] {'sx','sy'}, use_global_device_ids=true, to_apply=%region_2.5 | all-reduce | flops 3072 | bytes 24576 | tf_op jit(solution)/shard_map/psum | solution.py:75
  184.2 99.7 %all-reduce.1 = f32[3072]{0:T(1024)S(1)} all-reduce(f32[3072]{0:T(1024)S(1)} %dynamic-update-slice), channel_id=1, replica_groups=mesh['sx'=32,'sy'=16] {'sx','sy'}, use_global_device_ids=true, to_apply=%add.1 | all-reduce | flops 3072 | bytes 24576
  285.2 2.6 collective-permute-start.6
  287.8 2.3 collective-permute-done.6
  291.4 3.0 collective-permute-done.7
  295.2 104.9 %all-reduce.4 = (f32[]{:T(128)}, f32[]{:T(128)}) all-reduce(f32[]{:T(128)} %get-tuple-element.5, f32[]{:T(128)} %get-tuple-element.4), channel_id=1, replica_groups=mesh['sx'=32,'sy'=16] {'sx','sy'}, use_global_device_ids=true, to_apply=%region_1.0 | all-reduce | flops 2 | bytes 16 | tf_op jit(solution)/shard_map/psum | solution.py:62
  401.6 2.7 collective-permute-start.8
  406.7 3.2 fusion.33
  409.9 3.0 collective-permute-start.10
  416.2 3.9 collective-permute-done.11
  420.8 108.6 %psum.66 = f32[]{:T(128)} all-reduce(f32[]{:T(128)} %multiply_reduce_fusion.3), channel_id=1, replica_groups=mesh['sx'=32,'sy'=16] {'sx','sy'}, use_global_device_ids=true, to_apply=%region_6.9 | all-reduce | flops 1 | bytes 8 | tf_op jit(solution)/shard_map/psum | solution.py:62
  532.8 2.4 collective-permute-start.13
  536.4 3.2 fusion.42
  539.8 103.4 %psum.67 = f32[3072]{0:T(1024)S(1)} all-reduce(f32[3072]{0:T(1024)S(1)} %bitcast.106), channel_id=1, replica_groups=mesh['sx'=32,'sy'=16] {'sx','sy'}, use_global_device_ids=true, to_apply=%region_7.10 | all-reduce | flops 3072 | bytes 24576 | tf_op jit(solution)/shard_map/psum | solution.py:75
  643.8 101.6 %all-reduce.2 = f32[3072]{0:T(1024)S(1)} all-reduce(f32[3072]{0:T(1024)S(1)} %dynamic-update-slice.1), channel_id=1, replica_groups=mesh['sx'=32,'sy'=16] {'sx','sy'}, use_global_device_ids=true, to_apply=%add.2 | all-reduce | flops 3072 | bytes 24576
  746.7 2.6 collective-permute-start.14
  749.3 2.3 collective-permute-done.14
  753.0 3.0 collective-permute-done.15
  756.7 104.0 %psum.68 = f32[]{:T(128)} all-reduce(f32[]{:T(128)} %multiply_reduce_fusion.2), channel_id=1, replica_groups=mesh['sx'=32,'sy'=16] {'sx','sy'}, use_global_device_ids=true, to_apply=%region_9.12 | all-reduce | flops 1 | bytes 8 | tf_op jit(solution)/shard_map/psum | solution.py:80
  862.3 2.5 collective-permute-start.16
  867.4 3.2 fusion.36
  870.5 2.8 collective-permute-start.18
  873.3 2.1 collective-permute-done.18
  876.8 4.5 collective-permute-done.19
  882.1 107.9 %psum.69 = f32[]{:T(128)} all-reduce(f32[]{:T(128)} %multiply_reduce_fusion.1), channel_id=1, replica_groups=mesh['sx'=32,'sy'=16] {'sx','sy'}, use_global_device_ids=true, to_apply=%region_11.14 | all-reduce | flops 1 | bytes 8 | tf_op jit(solution)/shard_map/psum | solution.py:62
  993.4 2.6 collective-permute-start.21
  997.0 3.2 fusion.45
  1000.5 103.4 %psum.70 = f32[3072]{0:T(1024)S(1)} all-reduce(f32[3072]{0:T(1024)S(1)} %bitcast.107), channel_id=1, replica_groups=mesh['sx'=32,'sy'=16] {'sx','sy'}, use_global_device_ids=true, to_apply=%region_12.15 | all-reduce | flops 3072 | bytes 24576 | tf_op jit(solution)/shard_map/psum | solution.py:75
  1104.5 101.6 %all-reduce.3 = f32[3072]{0:T(1024)S(1)} all-reduce(f32[3072]{0:T(1024)S(1)} %dynamic-update-slice.2), channel_id=1, replica_groups=mesh['sx'=32,'sy'=16] {'sx','sy'}, use_global_device_ids=true, to_apply=%add.3 | all-reduce | flops 3072 | bytes 24576
  1207.3 2.6 collective-permute-start.22
  1209.9 2.3 collective-permute-done.22
  1213.6 3.0 collective-permute-done.23
  1217.4 104.0 %psum.71 = f32[]{:T(128)} all-reduce(f32[]{:T(128)} %multiply_reduce_fusion), channel_id=1, replica_groups=mesh['sx'=32,'sy'=16] {'sx','sy'}, use_global_device_ids=true, to_apply=%region_14.17 | all-reduce | flops 1 | bytes 8 | tf_op jit(solution)/shard_map/psum | solution.py:80
  (136 shorter events, 39.5 us)
Async XLA Ops:
  0.6 12.0 copy-start
  4.2 31.4 %collective-permute-start = (f32[192]{0:T(256)S(1)}, f32[192]{0:T(256)S(1)}, u32[]{:S(2)}, u32[]{:S(2)}) collective-permute-start(f32[192]{0:T(256)S(1)} %get-tuple-element.30), channel_id=1, source_target_pairs={{0,1},{1,2},{2,3},{3,4},{4,5},{5,6},{6,7},{7,8},{8,9},{9,10},{10,1... | collective-permute-start | bytes 2312 | tf_op jit(solution)/shard_map/ppermute | solution.py:12
  8.8 26.9 %collective-permute-start.1 = (f32[192]{0:T(256)S(1)}, f32[192]{0:T(256)S(1)}, u32[]{:S(2)}, u32[]{:S(2)}) collective-permute-start(f32[192]{0:T(256)S(1)} %get-tuple-element.31), channel_id=1, source_target_pairs={{0,16},{16,32},{32,48},{48,64},{64,80},{80,96},{96,112},{112,128},... | collective-permute-start | bytes 2312 | tf_op jit(solution)/shard_map/ppermute | solution.py:12
  16.1 5.8 copy-start.4
  21.9 4.9 copy-start.3
  38.9 4.9 collective-permute-start.2
  43.9 4.5 collective-permute-start.3
  48.6 18.0 %collective-permute-start.4 = (f32[192]{0:T(256)S(1)}, f32[192]{0:T(256)S(1)}, u32[]{:S(2)}, u32[]{:S(2)}) collective-permute-start(f32[192]{0:T(256)S(1)} %get-tuple-element.28), channel_id=1, source_target_pairs={{0,1},{1,2},{2,3},{3,4},{4,5},{5,6},{6,7},{7,8},{8,9},{9,10},{10,1... | collective-permute-start | bytes 2312 | tf_op jit(solution)/shard_map/ppermute | solution.py:12
  51.5 15.1 %collective-permute-start.5 = (f32[192]{0:T(256)S(1)}, f32[192]{0:T(256)S(1)}, u32[]{:S(2)}, u32[]{:S(2)}) collective-permute-start(f32[192]{0:T(256)S(1)} %get-tuple-element.29), channel_id=1, source_target_pairs={{0,16},{16,32},{32,48},{48,64},{64,80},{80,96},{96,112},{112,128},... | collective-permute-start | bytes 2312 | tf_op jit(solution)/shard_map/ppermute | solution.py:12
  59.0 5.8 copy-start.2
  64.8 118.8 %copy-start.1 = (f32[6,3072]{1,0:T(8,128)S(1)}, f32[6,3072]{1,0:T(8,128)}, u32[]{:S(2)}) copy-start(f32[6,3072]{1,0:T(8,128)} %param.16) | copy-start | bytes 221188
  285.2 4.9 collective-permute-start.6
  290.1 4.3 collective-permute-start.7
  401.6 4.3 collective-permute-start.8
  404.3 2.3 collective-permute-start.9
  409.9 4.9 collective-permute-start.10
  414.9 5.2 collective-permute-start.11
  530.9 4.3 collective-permute-start.12
  532.8 3.1 collective-permute-start.13
  746.7 4.9 collective-permute-start.14
  751.7 4.3 collective-permute-start.15
  862.3 4.3 collective-permute-start.16
  864.7 2.5 collective-permute-start.17
  870.5 4.9 collective-permute-start.18
  875.5 5.8 collective-permute-start.19
  991.5 4.5 collective-permute-start.20
  993.4 3.1 collective-permute-start.21
  1207.3 4.9 collective-permute-start.22
  1212.3 4.3 collective-permute-start.23
where the time goes:
time: 1330 us; the launch traced here: 1320 us
  blocking collectives  1150 us (86%)
  starting transfers between devices  57.4 us (4%)
  waiting for transfers between devices  35.2 us (3%)
  local copies, waits for them, and re-layouts  34.7 us (3%)
  matrix products  23.5 us (2%)
    psum x3, blocking collectives, residual_dot(): return lax.psum(jnp.sum(field * precond_field), ('sx', 'sy'))  321 us
    psum x3, blocking collectives, on_device(): coarse = lax.psum(partial_load, ('sx', 'sy'))  320 us
    unnamed x3, blocking collectives  303 us
    psum x2, blocking collectives, on_device(): alpha = norm_now / lax.psum(jnp.sum(direction * image), ('sx', 'sy'))  208 us
    ppermute x24, starting transfers between devices, shifted(): return lax.ppermute(block, axis, route)  57.4 us
    ppermute x24, waiting for transfers between devices, shifted(): return lax.ppermute(block, axis, route)  35.2 us
  transfers between devices with their start and end apart: 24, of which 16 were waited for; matrix products, arithmetic and copies ran while one was open for 3% of the time, Pallas kernels for 0%

commit v1 on v0

v1 whole, which is shorter than its diff:
```python
import jax
import jax.numpy as jnp
from jax import lax
from jax.experimental import pallas as pl
from jax.experimental.pallas import tpu as pltpu
from jax.sharding import PartitionSpec as P

ITERS = 3
LANES = 128
SLOT = 256
TILE = 8
CORNERS = 24
HIGHEST = lax.Precision.HIGHEST
VMEM = pl.BlockSpec(memory_space=pltpu.VMEM)
SMEM = pl.BlockSpec(memory_space=pltpu.SMEM)
LIMIT = 40 * 1024 * 1024

RES, MUL, DIR, IFACE, PARTNER, MASK, SCAL, NSTATE = 0, 8, 16, 24, 32, 40, 48, 56
GAMMA, LOAD = 48, 49


def call(kernel, inputs, outputs, specs=None, name=None):
    return pl.pallas_call(
        kernel,
        out_shape=[jax.ShapeDtypeStruct(shape, jnp.float32) for shape in outputs],
        in_specs=specs or [VMEM] * len(inputs),
        out_specs=[VMEM] * len(outputs),
        compiler_params=pltpu.CompilerParams(vmem_limit_bytes=LIMIT),
        name=name,
    )(*inputs)


def iota(shape, dim):
    return lax.broadcasted_iota(jnp.int32, shape, dim)


def as_tile(row):
    return jnp.concatenate([row[:, LANES * c : LANES * (c + 1)] for c in range(TILE)], axis=0)


def as_row(tile):
    return jnp.concatenate([tile[c : c + 1, :] for c in range(TILE)], axis=1)


def total(value):
    return jnp.sum(jnp.sum(value, axis=1, keepdims=True), axis=0, keepdims=True)


def apply_matrix(tile, map_tile, map_row, matrix_ref):
    width = matrix_ref.shape[0]
    values = jnp.transpose(tile)
    places = jnp.transpose(map_tile)
    lanes = iota((LANES, LANES), 1)
    pieces = []
    for t in range(width // LANES):
        acc = jnp.zeros((LANES, LANES), jnp.float32)
        for c in range(TILE):
            hit = places[:, c : c + 1] == lanes + t * LANES
            acc = acc + jnp.where(hit, values[:, c : c + 1], 0.0)
        pieces.append(jnp.sum(acc, axis=0, keepdims=True))
    out = jnp.zeros((TILE, TILE * LANES), jnp.float32)
    for b in range(width // LANES):
        rows = slice(b * LANES, (b + 1) * LANES)
        acc = matrix_ref[rows, 0:LANES] * pieces[0]
        for t in range(1, width // LANES):
            acc = acc + matrix_ref[rows, t * LANES : (t + 1) * LANES] * pieces[t]
        column = jnp.sum(acc, axis=1, keepdims=True)
        for s in range(LANES // TILE):
            index = iota((TILE, TILE * LANES), 0) + (b * LANES + s * TILE)
            out = out + jnp.where(map_row == index, column[s * TILE : (s + 1) * TILE, :], 0.0)
    return jnp.sum(out, axis=0, keepdims=True)


def coarse_load(weighted, modes_ref, near_ref, rt_ref, l_ref, nrows):
    own = jnp.sum(modes_ref[...] * weighted, axis=1, keepdims=True)
    near = near_ref[...] * weighted
    loads = [own]
    for q in range(4):
        loads.append(-jnp.sum(near[:, SLOT * q : SLOT * (q + 1)], axis=1, keepdims=True))
    loads.append(jnp.zeros((LANES - 5 * CORNERS, 1), jnp.float32))
    column = jnp.concatenate(loads, axis=0)
    return jnp.dot(rt_ref[0:nrows, :], column * l_ref[...], precision=HIGHEST)


def apply_schur(tile, map_tile, map_row, mask_row, schur_ref, modes_ref, near_ref, rt_ref, l_ref, out_ref, nrows, ncols):
    y_row = apply_matrix(tile, map_tile, map_row, schur_ref)
    load = coarse_load(0.25 * mask_row * y_row, modes_ref, near_ref, rt_ref, l_ref, nrows)
    y = as_tile(y_row)
    gamma = jnp.broadcast_to(0.25 * total(tile * y), (1, LANES))
    here = lax.axis_index("sy")
    rest = jnp.zeros((3, LANES), jnp.float32)
    for j in range(ncols):
        edge = jnp.where(here + 1 == j, y[0:2], jnp.where(here - 1 == j, y[4:6], 0.0))
        out_ref[j, 0:TILE, :] = jnp.concatenate([load[2 * j : 2 * j + 2], edge, gamma, rest], axis=0)
    return y


def pack_kernel(links_ref, modes_ref, map_ref, gap_ref, cmap_ref, out_modes, to_east, to_south, to_west, to_north):
    nrows, ncols = lax.axis_size("sx"), lax.axis_size("sy")
    modes = jnp.concatenate([modes_ref[...], jnp.zeros((8, modes_ref.shape[1]), jnp.float32)], axis=0)
    first = modes.astype(jnp.bfloat16)
    left = modes - first.astype(jnp.float32)
    second = left.astype(jnp.bfloat16)
    third = (left - second.astype(jnp.float32)).astype(jnp.bfloat16)
    map_row = map_ref[...]
    acc = jnp.zeros((CORNERS + 8, TILE * LANES), jnp.float32)
    for b in range(modes_ref.shape[1] // LANES):
        cols = slice(b * LANES, (b + 1) * LANES)
        index = iota((LANES, TILE * LANES), 0) + b * LANES
        hit = jnp.where(map_row == index, 1.0, 0.0).astype(jnp.bfloat16)
        for part in (first, second, third):
            acc = acc + jnp.dot(part[:, cols], hit, preferred_element_type=jnp.float32)
    acc = acc[0:CORNERS]
    out_modes[...] = acc
    east = ((lax.axis_index("sy") < ncols - 1) & (links_ref[0, 0] == 1)).astype(jnp.float32)
    south = ((lax.axis_index("sx") < nrows - 1) & (links_ref[0, 1] == 1)).astype(jnp.float32)
    gap = gap_ref[...]
    cmap = jnp.concatenate([cmap_ref[...], jnp.zeros((1, LANES), jnp.float32)], axis=1)
    rest = jnp.zeros((5, SLOT), jnp.float32)
    none = jnp.zeros((1, SLOT), jnp.float32)
    for q, ref in enumerate((to_east, to_south, to_west, to_north)):
        ref[0:CORNERS, :] = acc[:, SLOT * q : SLOT * (q + 1)]
        if q < 2:
            scale = (east, south)[q]
            values = jnp.concatenate([gap[2 * q : 2 * q + 1], gap[2 * q + 1 : 2 * q + 2]], axis=1) * scale
            mask = jnp.full((1, SLOT), 1.0, jnp.float32) * scale
        else:
            values, mask = none, none
        ref[CORNERS : CORNERS + 8, :] = jnp.concatenate([values, mask, cmap, rest], axis=0)


def start_kernel(
    own_east, own_south, from_east, from_south, from_west, from_north, cmap_ref, map_ref, map_tile_ref, schur_ref, modes_ref,
    blocks_ref, out_ref, state, near, r_ref, rt_ref, l_ref, mask_row_ref,
):
    nrows, ncols = lax.axis_size("sx"), lax.axis_size("sy")
    block = CORNERS // 4 * ncols
    row, cm = CORNERS, CORNERS + 2
    sources = (from_east, from_south, from_west, from_north)
    for q, ref in enumerate(sources):
        near[:, SLOT * q : SLOT * (q + 1)] = ref[0:CORNERS, :]
    values = [own_east[row : row + 1], own_south[row : row + 1], -from_west[row : row + 1], -from_north[row : row + 1]]
    masks = [ref[row + 1 : row + 2] for ref in (own_east, own_south, from_west, from_north)]
    residual = as_tile(jnp.concatenate(values, axis=1))
    mask_row = jnp.concatenate(masks, axis=1)
    mask_row_ref[...] = mask_row
    maps = [cmap_ref[...]] + [ref[cm : cm + 1, 0:LANES] for ref in sources]
    columns = jnp.transpose(jnp.concatenate(maps + [jnp.zeros((3, LANES), jnp.float32)], axis=0))
    column = [columns[0:CORNERS, g : g + 1] for g in range(5)]
    column.append(jnp.full((LANES - 5 * CORNERS, 1), float(block * nrows), jnp.float32))
    column = jnp.concatenate(column, axis=0)
    group = jnp.floor((column + 0.5) * (1.0 / block))
    inside = column - group * block
    lanes = iota((LANES, LANES), 1).astype(jnp.float32)
    hit_row = jnp.where((group == lanes) & (lanes < nrows), 1.0, 0.0)
    r_ref[...] = hit_row
    rt_ref[...] = jnp.transpose(hit_row)
    l_ref[...] = jnp.where(inside == lanes, 1.0, 0.0)
    y = apply_schur(
        residual, map_tile_ref[...], map_ref[...], mask_row, schur_ref, modes_ref, near, rt_ref, l_ref, out_ref, nrows, ncols
    )
    for j in range(ncols):
        out_ref[j, TILE : 3 * TILE, :] = blocks_ref[j]
    state[...] = jnp.zeros(state.shape, jnp.float32)
    state[RES : RES + TILE, :] = residual
    state[IFACE : IFACE + TILE, :] = y
    state[MASK : MASK + TILE, :] = as_tile(mask_row)


def rows_kernel(arrived, state_in, out_ref, state):
    nrows, ncols = lax.axis_size("sx"), lax.axis_size("sy")
    here, above = lax.axis_index("sy"), lax.axis_index("sx")
    summed = arrived[0, 0:TILE, :]
    for j in range(1, ncols):
        summed = summed + arrived[j, 0:TILE, :]
    west = arrived[jnp.maximum(here - 1, 0), 2:4, :]
    east = arrived[jnp.minimum(here + 1, ncols - 1), 2:4, :]
    state[...] = state_in[...]
    none = jnp.zeros((2, LANES), jnp.float32)
    state[PARTNER : PARTNER + TILE, :] = jnp.concatenate([east, none, west, none], axis=0)
    y = state_in[IFACE : IFACE + TILE, :]
    for i in range(nrows):
        edge = jnp.where(above + 1 == i, y[2:4], jnp.where(above - 1 == i, y[6:8], 0.0))
        out_ref[i, :, :] = jnp.concatenate([summed[0:2], edge, summed[4:8]], axis=0)


def direction_kernel(step, arrived, state_in, map_ref, map_tile_ref, kinv_ref, blocks_ref, out_ref, state):
    nrows, ncols = lax.axis_size("sx"), lax.axis_size("sy")
    here, above = lax.axis_index("sy"), lax.axis_index("sx")
    summed = arrived[0]
    for i in range(1, nrows):
        summed = summed + arrived[i]
    north = arrived[jnp.maximum(above - 1, 0), 2:4, :]
    south = arrived[jnp.minimum(above + 1, nrows - 1), 2:4, :]
    partner = state_in[PARTNER : PARTNER + TILE, :]
    partner = jnp.concatenate([partner[0:2], south, partner[4:6], north], axis=0)
    direction = 0.25 * state_in[MASK : MASK + TILE, :] * (state_in[IFACE : IFACE + TILE, :] - partner)
    load = summed[0:2]
    gamma = summed[4:5]
    if step:
        beta = gamma / state_in[GAMMA : GAMMA + 1, :]
        direction = direction + beta * state_in[DIR : DIR + TILE, :]
        load = load + beta * state_in[LOAD : LOAD + 2, :]
    inner = as_tile(apply_matrix(direction, map_tile_ref[...], map_ref[...], kinv_ref))
    energy = jnp.broadcast_to(total(direction * inner), (1, LANES))
    ndof = CORNERS // 4
    solved = jnp.zeros((2 * TILE, LANES), jnp.float32)
    pattern = jnp.concatenate([load] * TILE, axis=0)
    lanes = iota((2 * TILE, LANES), 1)
    halves = iota((2 * TILE, LANES), 0) // 2
    valid = iota((2 * TILE, LANES), 0) < 2 * ndof
    for j in range(ncols):
        column = jnp.sum(blocks_ref[j, TILE : 3 * TILE, :] * pattern, axis=1, keepdims=True)
        solved = solved + jnp.where((lanes == halves + j * ndof) & valid, column, 0.0)
    solved = jnp.sum(solved, axis=0, keepdims=True)
    rest = jnp.zeros((2, LANES), jnp.float32)
    for j in range(ncols):
        edge = jnp.where(here + 1 == j, inner[0:2], jnp.where(here - 1 == j, inner[4:6], 0.0))
        out_ref[j, :, :] = jnp.concatenate([solved, load, edge, energy, rest], axis=0)
    state[...] = state_in[...]
    state[DIR : DIR + TILE, :] = direction
    state[IFACE : IFACE + TILE, :] = inner
    state[SCAL : SCAL + TILE, :] = jnp.concatenate([gamma, load, jnp.zeros((5, LANES), jnp.float32)], axis=0)


def solve_kernel(arrived, state_in, out_ref, state, whole_load):
    nrows, ncols = lax.axis_size("sx"), lax.axis_size("sy")
    here, above = lax.axis_index("sy"), lax.axis_index("sx")
    summed = arrived[0]
    for j in range(1, ncols):
        summed = summed + arrived[j]
    whole_load[...] = jnp.concatenate([arrived[j, 1:3, :] for j in range(ncols)], axis=0)
    west = arrived[jnp.maximum(here - 1, 0), 3:5, :]
    east = arrived[jnp.minimum(here + 1, ncols - 1), 3:5, :]
    state[...] = state_in[...]
    none = jnp.zeros((2, LANES), jnp.float32)
    state[PARTNER : PARTNER + TILE, :] = jnp.concatenate([east, none, west, none], axis=0)
    inner = state_in[IFACE : IFACE + TILE, :]
    rest = jnp.zeros((4, LANES), jnp.float32)
    for i in range(nrows):
        edge = jnp.where(above + 1 == i, inner[2:4], jnp.where(above - 1 == i, inner[6:8], 0.0))
        out_ref[i, :, :] = jnp.concatenate([summed[0:1], edge, summed[5:6], rest], axis=0)


def advance(arrived, state_in, whole_load, modes_ref, near_ref, r_ref, l_ref):
    nrows = lax.axis_size("sx")
    above = lax.axis_index("sx")
    energy = arrived[0]
    for i in range(1, nrows):
        energy = energy + arrived[i]
    energy = energy[3:4]
    north = arrived[jnp.maximum(above - 1, 0), 1:3, :]
    south = arrived[jnp.minimum(above + 1, nrows - 1), 1:3, :]
    solved = jnp.concatenate([arrived[i, 0:1, :] for i in range(nrows)], axis=0)
    energy = energy + total(whole_load[...] * solved)
    alpha = state_in[GAMMA : GAMMA + 1, :] / energy
    found = jnp.dot(r_ref[:, 0:nrows], solved, precision=HIGHEST)
    corners = jnp.sum(found * l_ref[...], axis=1, keepdims=True)
    coarse = jnp.sum(corners[0:CORNERS] * modes_ref[...], axis=0, keepdims=True)
    near = []
    for q in range(4):
        values = corners[CORNERS * (q + 1) : CORNERS * (q + 2)]
        near.append(jnp.sum(values * near_ref[:, SLOT * q : SLOT * (q + 1)], axis=0, keepdims=True))
    coarse = as_tile(coarse - jnp.concatenate(near, axis=1))
    partner = state_in[PARTNER : PARTNER + TILE, :]
    partner = jnp.concatenate([partner[0:2], south, partner[4:6], north], axis=0)
    image = state_in[MASK : MASK + TILE, :] * (state_in[IFACE : IFACE + TILE, :] - partner + coarse)
    multipliers = state_in[MUL : MUL + TILE, :] + alpha * state_in[DIR : DIR + TILE, :]
    residual = state_in[RES : RES + TILE, :] - alpha * image
    return multipliers, residual


def next_kernel(
    arrived, state_in, whole_load, modes_ref, near_ref, r_ref, rt_ref, l_ref, mask_row_ref, map_ref, map_tile_ref, schur_ref,
    out_ref, state,
):
    nrows, ncols = lax.axis_size("sx"), lax.axis_size("sy")
    multipliers, residual = advance(arrived, state_in, whole_load, modes_ref, near_ref, r_ref, l_ref)
    y = apply_schur(
        residual, map_tile_ref[...], map_ref[...], mask_row_ref[...], schur_ref, modes_ref, near_ref, rt_ref, l_ref, out_ref,
        nrows, ncols,
    )
    state[...] = state_in[...]
    state[RES : RES + TILE, :] = residual
    state[MUL : MUL + TILE, :] = multipliers
    state[IFACE : IFACE + TILE, :] = y


def last_kernel(arrived, state_in, whole_load, modes_ref, near_ref, r_ref, l_ref, out_multipliers, out_residual):
    multipliers, residual = advance(arrived, state_in, whole_load, modes_ref, near_ref, r_ref, l_ref)
    out_multipliers[...] = multipliers
    out_residual[...] = residual


def shifted(block, axis, distance):
    devices = range(lax.axis_size(axis))
    route = [(i - distance, i) for i in devices if i - distance in devices]
    return lax.ppermute(block, axis, route)


def on_device(gap, kinv, schur, corner_modes, coarse_inverse, edge_map, corner_map, links):
    nrows, ncols = lax.axis_size("sx"), lax.axis_size("sy")
    width = kinv.shape[-1]
    edge = width // 4
    ndof = coarse_inverse.shape[0]
    block = coarse_inverse.shape[1] // nrows
    kinv = kinv.reshape(width, width)
    schur = schur.reshape(width, width)
    modes = corner_modes.reshape(-1, width)
    map_pad = jnp.pad(edge_map.reshape(4, edge), ((0, 0), (0, SLOT - edge)), constant_values=-1)
    map_tile = map_pad.reshape(TILE, LANES)
    map_row = map_pad.reshape(1, TILE * LANES)
    gap_pad = jnp.pad(gap.reshape(2, edge), ((0, 0), (0, SLOT - edge))).reshape(4, LANES)
    cmap = jnp.pad(corner_map.reshape(1, -1).astype(jnp.float32), ((0, 0), (0, LANES - CORNERS)))
    blocks = coarse_inverse.reshape(ndof, ncols, 2, block).transpose(1, 0, 2, 3).reshape(ncols, 2 * ndof, block)
    blocks = jnp.pad(blocks, ((0, 0), (0, 2 * TILE - 2 * ndof), (0, LANES - block)))

    own_modes, east, south, west, north = call(
        pack_kernel,
        (links.reshape(1, 2), modes, map_row, gap_pad, cmap),
        [(CORNERS, TILE * LANES)] + [(CORNERS + 8, SLOT)] * 4,
        [SMEM] + [VMEM] * 4,
        name="pack",
    )
    from_west = shifted(east, "sy", 1)
    from_east = shifted(west, "sy", -1)
    from_north = shifted(south, "sx", 1)
    from_south = shifted(north, "sx", -1)
    square = (LANES, LANES)
    out, state, near, r, rt, l, mask_row = call(
        start_kernel,
        (
            east, south, from_east, from_south, from_west, from_north, cmap, map_row, map_tile, schur, own_modes, blocks,
        ),
        [
            (ncols, 3 * TILE, LANES), (NSTATE, LANES), (CORNERS, TILE * LANES), square, square, square, (1, TILE * LANES),
        ],
        name="start",
    )
    to_sy, to_sx = (ncols, TILE, LANES), (nrows, TILE, LANES)
    state_shape = (NSTATE, LANES)
    for step in range(ITERS):
        arrived = lax.all_to_all(out, "sy", 0, 0, tiled=True)
        if step == 0:
            solver = arrived
        out, state = call(rows_kernel, (arrived, state), [to_sx, state_shape], name="rows")
        arrived = lax.all_to_all(out, "sx", 0, 0, tiled=True)

        def kernel(*refs, step=step):
            direction_kernel(step, *refs)

        out, state = call(
            kernel, (arrived, state, map_row, map_tile, kinv, solver), [to_sy, state_shape], name="direction"
        )
        arrived = lax.all_to_all(out, "sy", 0, 0, tiled=True)
        out, state, load = call(
            solve_kernel, (arrived, state), [to_sx, state_shape, (nrows, LANES)], name="solve"
        )
        arrived = lax.all_to_all(out, "sx", 0, 0, tiled=True)
        common = (arrived, state, load, own_modes, near, r)
        if step + 1 < ITERS:
            out, state = call(
                next_kernel, common + (rt, l, mask_row, map_row, map_tile, schur), [to_sy, state_shape], name="next"
            )
        else:
            results = call(last_kernel, common + (l,), [(TILE, LANES)] * 2, name="last")
    return tuple(value.reshape(4, SLOT)[:2, :edge].reshape(gap.shape) for value in results)


def solution(mesh):
    placed = (
        P("sx", "sy", None),
        P("sx", "sy", None, None),
        P("sx", "sy", None, None),
        P("sx", "sy", None, None),
        P(("sx", "sy"), None),
        P("sx", "sy", None),
        P("sx", "sy", None),
        P("sx", "sy", None),
    )
    return jax.shard_map(
        on_device,
        mesh=mesh,
        in_specs=placed,
        out_specs=(P("sx", "sy", None), P("sx", "sy", None)),
        check_vma=False,
    )
```

time: 1330 us -> 235 us (0.18)
  blocking collectives: 1150 us -> 197 us
  starting transfers between devices: 57.4 us -> 16 us
  waiting for transfers between devices: 35.2 us -> 0.01 us
  local copies, waits for them, and re-layouts: 34.7 us -> 5.84 us
  matrix products: 23.5 us -> 0 us
    psum x8 -> x0, blocking collectives: 849 us -> none  [the longest x3 321 us: residual_dot(): return lax.psum(jnp.sum(field * precond_field), ('sx', 'sy'))]
    unnamed x3 -> x0, blocking collectives: 303 us -> none
    all_to_all x0 -> x12, blocking collectives: none -> 197 us  [the longest x6 123 us: on_device(): arrived = lax.all_to_all(out, 'sx', 0, 0, tiled=True)]
    ppermute x24 -> x4, starting transfers between devices: 57.4 us -> 16 us  [shifted(): return lax.ppermute(block, axis, route)]
    ppermute x24 -> x4, waiting for transfers between devices: 35.2 us -> 0.01 us  [shifted(): return lax.ppermute(block, axis, route)]
    gather x8 -> x0, local copies, waits for them, and re-layouts: 24.4 us -> none  [the longest x1 5.77 us: on_device(): jnp.take(jnp.take(kinv.reshape(width, width), local_map, axis=0), local_m...]
    dot_general x18 -> x0, matrix products: 23.5 us -> none  [the longest x3 9.53 us: on_device(): inner = jnp.dot(kinv_perm, operator_iface, precision=highest)]
  transfers between devices with their start and end apart: 24 -> 4, of which waited for: 16 -> 0; matrix products, arithmetic and copies ran while one was open for 3% -> 0% of each run, Pallas kernels for 0% -> 0%
where the time goes in v1:
time: 235 us; the launch traced here: 233 us
  blocking collectives  197 us (84%)
  starting transfers between devices  16 us (7%)
  Pallas kernels  12 us (5%)
  local copies, waits for them, and re-layouts  5.84 us (2%)
    all_to_all x6, blocking collectives, on_device(): arrived = lax.all_to_all(out, 'sx', 0, 0, tiled=True)  123 us
    all_to_all x6, blocking collectives, on_device(): arrived = lax.all_to_all(out, 'sy', 0, 0, tiled=True)  73.3 us
    ppermute x4, starting transfers between devices, shifted(): return lax.ppermute(block, axis, route)  16 us
    pallas_call x14, Pallas kernels, call(): pl.pallas_call(kernel, out_shape=[jax.ShapeDtypeStruct(shape, jnp.float32...  12 us
  transfers between devices with their start and end apart: 4, of which 0 were waited for; matrix products, arithmetic and copies ran while one was open for 0% of the time, Pallas kernels for 0%

profile of v1, /device:TPU:1, one launch (start us, length us, event | category | flops | bytes accessed | tf_op | source)
XLA Modules:
  0.0 233.4 jit_solution(16602176410489847085)
XLA Ops:
  0.6 0.7 convert_bitcast_fusion
  1.3 0.7 reduce.1
  2.0 0.1 reshape.67
  2.1 0.7 reduce
  2.8 0.1 reshape.65
  2.9 0.9 copy-done.3
  3.8 0.7 copy-done.4
  4.4 1.3 pack.1
  5.7 8.8 %collective-permute-start = (f32[32,256]{1,0:T(8,128)S(1)}, f32[32,256]{1,0:T(8,128)S(1)}, u32[]{:S(2)}, u32[]{:S(2)}) collective-permute-start(f32[32,256]{1,0:T(8,128)S(1)} %get-tuple-element.43), channel_id=1, source_target_pairs={{1,0},{2,1},{3,2},{4,3},{5,4},{6,5},{7,6},{8,7},{9,8},{10,9},{11,1... | collective-permute-start | bytes 98312 | tf_op jit(solution)/shard_map/ppermute | solution.py:298
  14.5 1.3 collective-permute-start.1
  15.8 1.9 collective-permute-start.2
  17.8 4.0 %collective-permute-start.3 = (f32[32,256]{1,0:T(8,128)S(1)}, f32[32,256]{1,0:T(8,128)S(1)}, u32[]{:S(2)}, u32[]{:S(2)}) collective-permute-start(f32[32,256]{1,0:T(8,128)S(1)} %get-tuple-element.42.own_south), channel_id=1, source_target_pairs={{0,16},{16,32},{32,48},{48,64},{64,80},{80,96},{96,112},{112,128},... | collective-permute-start | bytes 98312 | tf_op jit(solution)/shard_map/ppermute | solution.py:298
  21.8 1.1 reshape.71
  22.9 0.0 collective-permute-done.from_east
  22.9 0.0 collective-permute-done.1.from_south
  22.9 0.0 collective-permute-done.2.from_west
  22.9 0.0 collective-permute-done.3.from_north
  22.9 0.0 copy-start
  23.0 1.7 copy-done
  24.6 1.8 start.1
  26.4 0.0 copy-start.1
  26.4 11.9 %all_to_all.60.arrived.refs_5_ = f32[16,24,128]{2,1,0:T(8,128)S(1)} all-to-all(f32[16,24,128]{2,1,0:T(8,128)S(1)} %get-tuple-element.46), channel_id=1, replica_groups=mesh['sx'=32,'sy'=16] {'sy'}, dimensions={0} | all-to-all | bytes 393216 | tf_op jit(solution)/shard_map/all_to_all | solution.py:343
  38.4 0.1 rows.3
  38.5 32.9 %all_to_all.61.refs_0_ = f32[32,8,128]{2,1,0:T(8,128)S(1)} all-to-all(f32[32,8,128]{2,1,0:T(8,128)S(1)} %get-tuple-element.48), channel_id=1, replica_groups=mesh['sx'=32,'sy'=16] {'sx'}, dimensions={0} | all-to-all | bytes 262144 | tf_op jit(solution)/shard_map/all_to_all | solution.py:347
  71.3 0.0 copy-done.2
  71.3 1.5 direction.3
  72.8 13.1 %all_to_all.62.arrived = f32[16,8,128]{2,1,0:T(8,128)S(1)} all-to-all(f32[16,8,128]{2,1,0:T(8,128)S(1)} %get-tuple-element.50), channel_id=1, replica_groups=mesh['sx'=32,'sy'=16] {'sy'}, dimensions={0} | all-to-all | bytes 131072 | tf_op jit(solution)/shard_map/all_to_all | solution.py:355
  85.9 0.1 solve.3
  86.0 18.1 %all_to_all.63.arrived = f32[32,8,128]{2,1,0:T(8,128)S(1)} all-to-all(f32[32,8,128]{2,1,0:T(8,128)S(1)} %get-tuple-element.52), channel_id=1, replica_groups=mesh['sx'=32,'sy'=16] {'sx'}, dimensions={0} | all-to-all | bytes 262144 | tf_op jit(solution)/shard_map/all_to_all | solution.py:359
  104.0 1.9 next.2
  106.0 12.2 %all_to_all.64.arrived = f32[16,8,128]{2,1,0:T(8,128)S(1)} all-to-all(f32[16,8,128]{2,1,0:T(8,128)S(1)} %get-tuple-element.60), channel_id=1, replica_groups=mesh['sx'=32,'sy'=16] {'sy'}, dimensions={0} | all-to-all | bytes 131072 | tf_op jit(solution)/shard_map/all_to_all | solution.py:343
  118.2 0.1 rows.4
  118.3 18.1 %all_to_all.65.refs_0_ = f32[32,8,128]{2,1,0:T(8,128)S(1)} all-to-all(f32[32,8,128]{2,1,0:T(8,128)S(1)} %get-tuple-element.62), channel_id=1, replica_groups=mesh['sx'=32,'sy'=16] {'sx'}, dimensions={0} | all-to-all | bytes 262144 | tf_op jit(solution)/shard_map/all_to_all | solution.py:347
  136.4 1.4 direction.4
  137.8 11.9 %all_to_all.66.arrived = f32[16,8,128]{2,1,0:T(8,128)S(1)} all-to-all(f32[16,8,128]{2,1,0:T(8,128)S(1)} %get-tuple-element.64), channel_id=1, replica_groups=mesh['sx'=32,'sy'=16] {'sy'}, dimensions={0} | all-to-all | bytes 131072 | tf_op jit(solution)/shard_map/all_to_all | solution.py:355
  149.8 0.1 solve.4
  149.8 18.1 %all_to_all.67.arrived = f32[32,8,128]{2,1,0:T(8,128)S(1)} all-to-all(f32[32,8,128]{2,1,0:T(8,128)S(1)} %get-tuple-element.66), channel_id=1, replica_groups=mesh['sx'=32,'sy'=16] {'sx'}, dimensions={0} | all-to-all | bytes 262144 | tf_op jit(solution)/shard_map/all_to_all | solution.py:359
  167.9 1.9 next.3
  169.9 12.1 %all_to_all.68.arrived = f32[16,8,128]{2,1,0:T(8,128)S(1)} all-to-all(f32[16,8,128]{2,1,0:T(8,128)S(1)} %get-tuple-element.69), channel_id=1, replica_groups=mesh['sx'=32,'sy'=16] {'sy'}, dimensions={0} | all-to-all | bytes 131072 | tf_op jit(solution)/shard_map/all_to_all | solution.py:343
  182.0 0.1 rows.5
  182.1 18.1 %all_to_all.69.refs_0_ = f32[32,8,128]{2,1,0:T(8,128)S(1)} all-to-all(f32[32,8,128]{2,1,0:T(8,128)S(1)} %get-tuple-element.71), channel_id=1, replica_groups=mesh['sx'=32,'sy'=16] {'sx'}, dimensions={0} | all-to-all | bytes 262144 | tf_op jit(solution)/shard_map/all_to_all | solution.py:347
  200.2 1.4 direction.5
  201.6 12.0 %all_to_all.70.arrived = f32[16,8,128]{2,1,0:T(8,128)S(1)} all-to-all(f32[16,8,128]{2,1,0:T(8,128)S(1)} %get-tuple-element.73), channel_id=1, replica_groups=mesh['sx'=32,'sy'=16] {'sy'}, dimensions={0} | all-to-all | bytes 131072 | tf_op jit(solution)/shard_map/all_to_all | solution.py:355
  213.6 0.1 solve.5
  213.6 18.1 %all_to_all.71.arrived = f32[32,8,128]{2,1,0:T(8,128)S(1)} all-to-all(f32[32,8,128]{2,1,0:T(8,128)S(1)} %get-tuple-element.75), channel_id=1, replica_groups=mesh['sx'=32,'sy'=16] {'sx'}, dimensions={0} | all-to-all | bytes 262144 | tf_op jit(solution)/shard_map/all_to_all | solution.py:359
  231.7 0.3 last.1
  232.0 0.6 reshape.75
  232.7 0.6 reshape.77
  (17 shorter events, 0.1 us)
Async XLA Ops:
  2.9 0.9 copy-start.3
  3.8 0.7 copy-start.4
  5.7 17.2 %collective-permute-start = (f32[32,256]{1,0:T(8,128)S(1)}, f32[32,256]{1,0:T(8,128)S(1)}, u32[]{:S(2)}, u32[]{:S(2)}) collective-permute-start(f32[32,256]{1,0:T(8,128)S(1)} %get-tuple-element.43), channel_id=1, source_target_pairs={{1,0},{2,1},{3,2},{4,3},{5,4},{6,5},{7,6},{8,7},{9,8},{10,9},{11,1... | collective-permute-start | bytes 98312 | tf_op jit(solution)/shard_map/ppermute | solution.py:298
  14.5 8.4 %collective-permute-start.1 = (f32[32,256]{1,0:T(8,128)S(1)}, f32[32,256]{1,0:T(8,128)S(1)}, u32[]{:S(2)}, u32[]{:S(2)}) collective-permute-start(f32[32,256]{1,0:T(8,128)S(1)} %get-tuple-element.44), channel_id=1, source_target_pairs={{16,0},{32,16},{48,32},{64,48},{80,64},{96,80},{112,96},{128,112},... | collective-permute-start | bytes 98312 | tf_op jit(solution)/shard_map/ppermute | solution.py:298
  15.8 7.1 %collective-permute-start.2 = (f32[32,256]{1,0:T(8,128)S(1)}, f32[32,256]{1,0:T(8,128)S(1)}, u32[]{:S(2)}, u32[]{:S(2)}) collective-permute-start(f32[32,256]{1,0:T(8,128)S(1)} %get-tuple-element.41.own_east), channel_id=1, source_target_pairs={{0,1},{1,2},{2,3},{3,4},{4,5},{5,6},{6,7},{7,8},{8,9},{9,10},{10,1... | collective-permute-start | bytes 98312 | tf_op jit(solution)/shard_map/ppermute | solution.py:298
  17.8 5.2 %collective-permute-start.3 = (f32[32,256]{1,0:T(8,128)S(1)}, f32[32,256]{1,0:T(8,128)S(1)}, u32[]{:S(2)}, u32[]{:S(2)}) collective-permute-start(f32[32,256]{1,0:T(8,128)S(1)} %get-tuple-element.42.own_south), channel_id=1, source_target_pairs={{0,16},{16,32},{32,48},{48,64},{64,80},{80,96},{96,112},{112,128},... | collective-permute-start | bytes 98312 | tf_op jit(solution)/shard_map/ppermute | solution.py:298
  22.9 1.7 copy-start
  24.6 46.7 %copy-start.2 = (f32[1,1,768,768]{3,2,1,0:T(8,128)S(1)}, f32[1,1,768,768]{3,2,1,0:T(8,128)}, u32[]{:S(2)}) copy-start(f32[1,1,768,768]{3,2,1,0:T(8,128)} %param.9) | copy-start | bytes 7077892
  26.4 77.6 %copy-start.1 = (f32[1,1,768,768]{3,2,1,0:T(8,128)S(1)}, f32[1,1,768,768]{3,2,1,0:T(8,128)}, u32[]{:S(2)}) copy-start(f32[1,1,768,768]{3,2,1,0:T(8,128)} %param.10) | copy-start | bytes 7077892

commit v2 on v1

v2 whole, which is shorter than its diff:
```python
import jax
import jax.numpy as jnp
from jax import lax
from jax.experimental import pallas as pl
from jax.experimental.pallas import tpu as pltpu
from jax.sharding import Mesh
from jax.sharding import PartitionSpec as P

ITERS = 3
LANES = 128
SLOT = 256
TILE = 8
CORNERS = 24
NDOF = 6
HIGHEST = lax.Precision.HIGHEST
VMEM = pl.BlockSpec(memory_space=pltpu.VMEM)
ANY = pl.BlockSpec(memory_space=pl.ANY)
LIMIT = 40 * 1024 * 1024

ROWS_AXES = ("z", "xl")
PLANE = ("xl", "sy")

RES, MUL, DIR, IFACE, PARTNER, MASK, SCAL, NSTATE = 0, 8, 16, 24, 32, 40, 48, 56
GAMMA, LOAD = 48, 49


def call(kernel, inputs, outputs, in_specs=None, out_specs=None, scratch=(), name=None):
    shapes = [shape if hasattr(shape, "dtype") else jax.ShapeDtypeStruct(shape, jnp.float32) for shape in outputs]
    return pl.pallas_call(
        kernel,
        out_shape=shapes,
        in_specs=in_specs or [VMEM] * len(inputs),
        out_specs=out_specs or [VMEM] * len(outputs),
        scratch_shapes=list(scratch),
        compiler_params=pltpu.CompilerParams(vmem_limit_bytes=LIMIT),
        name=name,
    )(*inputs)


def iota(shape, dim):
    return lax.broadcasted_iota(jnp.int32, shape, dim)


def as_tile(row):
    return jnp.concatenate([row[:, LANES * c : LANES * (c + 1)] for c in range(TILE)], axis=0)


def total(value):
    return jnp.sum(jnp.sum(value, axis=1, keepdims=True), axis=0, keepdims=True)


def slots(row, count, fill):
    width = row.shape[1]
    wide = jnp.broadcast_to(row, (TILE, width))
    lanes = iota((1, SLOT), 1)
    edge = SLOT * 3 // 4
    pieces = []
    for q in range(count):
        moved = wide if q == 0 else pltpu.roll(wide, width - edge * q, 1)
        pieces.append(jnp.where(lanes < edge, moved[0:1, 0:SLOT], fill))
    return pieces


def apply_matrix(tile, map_tile, map_row, matrix_ref):
    width = matrix_ref.shape[0]
    values = jnp.transpose(tile)
    places = jnp.transpose(map_tile)
    lanes = iota((LANES, LANES), 1)
    pieces = []
    for t in range(width // LANES):
        acc = jnp.zeros((LANES, LANES), jnp.float32)
        for c in range(TILE):
            hit = places[:, c : c + 1] == lanes + t * LANES
            acc = acc + jnp.where(hit, values[:, c : c + 1], 0.0)
        pieces.append(jnp.sum(acc, axis=0, keepdims=True))
    out = jnp.zeros((TILE, TILE * LANES), jnp.float32)
    for b in range(width // LANES):
        rows = slice(b * LANES, (b + 1) * LANES)
        acc = matrix_ref[rows, 0:LANES] * pieces[0]
        for t in range(1, width // LANES):
            acc = acc + matrix_ref[rows, t * LANES : (t + 1) * LANES] * pieces[t]
        column = jnp.sum(acc, axis=1, keepdims=True)
        for s in range(LANES // TILE):
            index = iota((TILE, TILE * LANES), 0) + (b * LANES + s * TILE)
            out = out + jnp.where(map_row == index, column[s * TILE : (s + 1) * TILE, :], 0.0)
    return jnp.sum(out, axis=0, keepdims=True)


def coarse_load(weighted, modes_ref, near_ref, rt_ref, l_ref, chunks):
    own = jnp.sum(modes_ref[...] * weighted, axis=1, keepdims=True)
    near = near_ref[...] * weighted
    loads = [own]
    for q in range(4):
        loads.append(-jnp.sum(near[:, SLOT * q : SLOT * (q + 1)], axis=1, keepdims=True))
    loads.append(jnp.zeros((LANES - 5 * CORNERS, 1), jnp.float32))
    column = jnp.concatenate(loads, axis=0)
    return jnp.dot(rt_ref[0:chunks, :], column * l_ref[...], precision=HIGHEST)


def plane_edges(tile, target, ncols):
    pair, col = target // ncols, target % ncols
    same = lax.axis_index("xl") == pair
    here = lax.axis_index("sy")
    first = jnp.where(
        same,
        jnp.where(here + 1 == col, tile[0:2], jnp.where(here - 1 == col, tile[4:6], 0.0)),
        jnp.where(here == col, tile[2:4], 0.0),
    )
    second = jnp.where(same, 0.0, jnp.where(here == col, tile[6:8], 0.0))
    return first, second


def plane_arrivals(arrived, row, ncols):
    pair, here = lax.axis_index("xl"), lax.axis_index("sy")
    base = pair * ncols
    east = arrived[base + jnp.minimum(here + 1, ncols - 1), row : row + 2, :]
    west = arrived[base + jnp.maximum(here - 1, 0), row : row + 2, :]
    other = (1 - pair) * ncols + here
    their_south = arrived[other, row : row + 2, :]
    their_north = arrived[other, row + 2 : row + 4, :]
    south = jnp.where(pair == 0, their_north, 0.0)
    north = jnp.where(pair == 0, 0.0, their_south)
    forward = jnp.where(pair == 0, their_south, their_north)
    return jnp.concatenate([east, south, west, north], axis=0), forward


def z_edge(forward, target):
    goal = jnp.where(lax.axis_index("xl") == 0, lax.axis_index("z") + 1, lax.axis_index("z") - 1)
    return jnp.where(goal == target, forward, 0.0)


def z_arrival(arrived, row, partner):
    levels = arrived.shape[0]
    pair, level = lax.axis_index("xl"), lax.axis_index("z")
    source = jnp.where(pair == 0, jnp.maximum(level - 1, 0), jnp.minimum(level + 1, levels - 1))
    edge = arrived[source, row : row + 2, :]
    south = jnp.where(pair == 0, partner[2:4], edge)
    north = jnp.where(pair == 0, edge, partner[6:8])
    return jnp.concatenate([partner[0:2], south, partner[4:6], north], axis=0)


def apply_schur(tile, map_tile, map_row, mask_row, schur_ref, modes_ref, near_ref, rt_ref, l_ref, out_ref):
    chunks = out_ref.shape[0]
    y_row = apply_matrix(tile, map_tile, map_row, schur_ref)
    load = coarse_load(0.25 * mask_row * y_row, modes_ref, near_ref, rt_ref, l_ref, chunks)
    y = as_tile(y_row)
    gamma = jnp.broadcast_to(0.25 * total(tile * y), (1, LANES))
    rest = jnp.zeros((2, LANES), jnp.float32)
    for p in range(chunks):
        first, second = plane_edges(y, p, chunks // 2)
        out_ref[p, 0:TILE, :] = jnp.concatenate([load[p : p + 1], gamma, first, second, rest], axis=0)
    return y


def pack_kernel(
    links_hbm, modes_hbm, map_hbm, gap_hbm, cmap_hbm, out_modes, to_east, to_south, to_west, to_north, out_row, out_tile,
    out_cmap, links_ref, modes_ref, map_ref, gap_ref, cmap_ref, sems,
):
    copies = [
        pltpu.make_async_copy(source, target, sems.at[k])
        for k, (source, target) in enumerate(
            (
                (modes_hbm, modes_ref), (map_hbm, map_ref), (gap_hbm, gap_ref), (cmap_hbm, cmap_ref),
                (links_hbm, links_ref),
            )
        )
    ]
    for copy in copies:
        copy.start()
    for copy in copies:
        copy.wait()
    nrows, ncols = lax.axis_size("z") * lax.axis_size("xl"), lax.axis_size("sy")
    row_here = lax.axis_index("z") * lax.axis_size("xl") + lax.axis_index("xl")
    map_row = jnp.concatenate(slots(map_ref[0], 4, -1), axis=1)
    out_row[...] = map_row
    out_tile[...] = as_tile(map_row)
    width = modes_ref.shape[3]
    modes = jnp.concatenate([modes_ref[0, 0], jnp.zeros((8, width), jnp.float32)], axis=0)
    first = modes.astype(jnp.bfloat16)
    left = modes - first.astype(jnp.float32)
    second = left.astype(jnp.bfloat16)
    third = (left - second.astype(jnp.float32)).astype(jnp.bfloat16)
    acc = jnp.zeros((CORNERS + 8, TILE * LANES), jnp.float32)
    for b in range(width // LANES):
        cols = slice(b * LANES, (b + 1) * LANES)
        index = iota((LANES, TILE * LANES), 0) + b * LANES
        hit = jnp.where(map_row == index, 1.0, 0.0).astype(jnp.bfloat16)
        for part in (first, second, third):
            acc = acc + jnp.dot(part[:, cols], hit, preferred_element_type=jnp.float32)
    acc = acc[0:CORNERS]
    out_modes[...] = acc
    links = jnp.where(links_ref[0] == 1, 1.0, 0.0)
    east = jnp.where(lax.axis_index("sy") < ncols - 1, links[:, 0:1], 0.0)
    south = jnp.where(row_here < nrows - 1, links[:, 1:2], 0.0)
    gaps = slots(gap_ref[0], 2, 0.0)
    out_cmap[...] = jnp.zeros(out_cmap.shape, jnp.float32)
    out_cmap[0:1, 0:CORNERS] = cmap_ref[0].astype(jnp.float32)
    cmap = out_cmap[...]
    rest = jnp.zeros((5, SLOT), jnp.float32)
    none = jnp.zeros((1, SLOT), jnp.float32)
    for q, ref in enumerate((to_east, to_south, to_west, to_north)):
        ref[0:CORNERS, :] = acc[:, SLOT * q : SLOT * (q + 1)]
        values, mask = none, none
        if q < 2:
            mask = none + (east, south)[q]
            values = gaps[q] * mask
        ref[CORNERS : CORNERS + 8, :] = jnp.concatenate([values, mask, cmap, rest], axis=0)


def load_kernel(schur_hbm, coarse_hbm, schur_out, blocks_out, coarse_ref, sems):
    matrix = pltpu.make_async_copy(schur_hbm.at[0, 0], schur_out, sems.at[0])
    coarse = pltpu.make_async_copy(coarse_hbm, coarse_ref, sems.at[1])
    coarse.start()
    matrix.start()
    coarse.wait()
    chunks = blocks_out.shape[0]
    ncoarse = coarse_ref.shape[1]
    block = ncoarse // chunks
    padded = -(-ncoarse // LANES) * LANES
    values = coarse_ref[...]
    if padded > ncoarse:
        values = jnp.pad(values, ((0, 0), (0, padded - ncoarse)))
    values = jnp.concatenate([values, jnp.zeros((TILE - NDOF, padded), jnp.float32)], axis=0)
    values = jnp.concatenate([values, jnp.zeros((TILE, LANES), jnp.float32)], axis=1)
    lanes = iota((TILE, LANES), 1)
    for p in range(chunks):
        start = block * p // LANES * LANES
        window = values[:, start : start + SLOT]
        shift = block * p - start
        if shift:
            window = pltpu.roll(window, SLOT - shift, 1)
        blocks_out[p] = jnp.where(lanes < block, window[:, 0:LANES], 0.0)
    matrix.wait()


def start_kernel(
    own_east, own_south, from_east, from_south, from_west, from_north, cmap_ref, map_ref, map_tile_ref, schur_ref, modes_ref,
    blocks_ref, out_ref, state, near, r_ref, rt_ref, l_ref, mask_row_ref,
):
    chunks = out_ref.shape[0]
    block = NDOF * chunks // 2
    row, cm = CORNERS, CORNERS + 2
    sources = (from_east, from_south, from_west, from_north)
    for q, ref in enumerate(sources):
        near[:, SLOT * q : SLOT * (q + 1)] = ref[0:CORNERS, :]
    values = [own_east[row : row + 1], own_south[row : row + 1], -from_west[row : row + 1], -from_north[row : row + 1]]
    masks = [ref[row + 1 : row + 2] for ref in (own_east, own_south, from_west, from_north)]
    residual = as_tile(jnp.concatenate(values, axis=1))
    mask_row = jnp.concatenate(masks, axis=1)
    mask_row_ref[...] = mask_row
    maps = [cmap_ref[:, 0:LANES]] + [ref[cm : cm + 1, 0:LANES] for ref in sources]
    columns = jnp.transpose(jnp.concatenate(maps + [jnp.zeros((3, LANES), jnp.float32)], axis=0))
    column = [columns[0:CORNERS, g : g + 1] for g in range(5)]
    column.append(jnp.full((LANES - 5 * CORNERS, 1), float(block * chunks), jnp.float32))
    column = jnp.concatenate(column, axis=0)
    group = jnp.floor((column + 0.5) * (1.0 / block))
    inside = column - group * block
    lanes = iota((LANES, LANES), 1).astype(jnp.float32)
    hit_row = jnp.where((group == lanes) & (lanes < chunks), 1.0, 0.0)
    r_ref[...] = hit_row
    rt_ref[...] = jnp.transpose(hit_row)
    l_ref[...] = jnp.where(inside == lanes, 1.0, 0.0)
    y = apply_schur(residual, map_tile_ref[...], map_ref[...], mask_row, schur_ref, modes_ref, near, rt_ref, l_ref, out_ref)
    for p in range(chunks):
        out_ref[p, TILE : 2 * TILE, :] = blocks_ref[p]
    state[...] = jnp.zeros(state.shape, jnp.float32)
    state[RES : RES + TILE, :] = residual
    state[IFACE : IFACE + TILE, :] = y
    state[MASK : MASK + TILE, :] = as_tile(mask_row)


def rows_kernel(arrived, state_in, out_ref, state):
    chunks, levels = arrived.shape[0], out_ref.shape[0]
    summed = arrived[0, 0:TILE, :]
    for p in range(1, chunks):
        summed = summed + arrived[p, 0:TILE, :]
    partner, forward = plane_arrivals(arrived, 2, chunks // 2)
    state[...] = state_in[...]
    state[PARTNER : PARTNER + TILE, :] = partner
    for level in range(levels):
        out_ref[level] = jnp.concatenate([summed[0:2], z_edge(forward, level)], axis=0)


def direction_kernel(step, arrived, state_in, map_ref, map_tile_ref, kinv_ref, blocks_ref, out_ref, state):
    chunks, levels = out_ref.shape[0], arrived.shape[0]
    half = chunks // 2
    summed = arrived[0]
    for level in range(1, levels):
        summed = summed + arrived[level]
    partner = z_arrival(arrived, 2, state_in[PARTNER : PARTNER + TILE, :])
    direction = 0.25 * state_in[MASK : MASK + TILE, :] * (state_in[IFACE : IFACE + TILE, :] - partner)
    load = summed[0:1]
    gamma = summed[1:2]
    if step:
        beta = gamma / state_in[GAMMA : GAMMA + 1, :]
        direction = direction + beta * state_in[DIR : DIR + TILE, :]
        load = load + beta * state_in[LOAD : LOAD + 1, :]
    inner = as_tile(apply_matrix(direction, map_tile_ref[...], map_ref[...], kinv_ref))
    energy = jnp.broadcast_to(total(direction * inner), (1, LANES))
    lanes = iota((TILE, LANES), 1)
    dof = iota((TILE, LANES), 0)
    solved = []
    for a in range(2):
        acc = jnp.zeros((TILE, LANES), jnp.float32)
        for p in range(half):
            column = jnp.sum(blocks_ref[a * half + p, TILE : 2 * TILE, :] * load, axis=1, keepdims=True)
            acc = acc + jnp.where((lanes == dof + p * NDOF) & (dof < NDOF), column, 0.0)
        solved.append(jnp.sum(acc, axis=0, keepdims=True))
    for p in range(chunks):
        first, second = plane_edges(inner, p, half)
        out_ref[p] = jnp.concatenate(solved + [load, energy, first, second], axis=0)
    state[...] = state_in[...]
    state[DIR : DIR + TILE, :] = direction
    state[IFACE : IFACE + TILE, :] = inner
    state[SCAL : SCAL + TILE, :] = jnp.concatenate([gamma, load, jnp.zeros((6, LANES), jnp.float32)], axis=0)


def solve_kernel(arrived, state_in, out_ref, state, whole_load):
    chunks, levels = arrived.shape[0], out_ref.shape[0]
    block = NDOF * chunks // 2
    summed = arrived[0]
    for p in range(1, chunks):
        summed = summed + arrived[p]
    whole_load[...] = jnp.concatenate([arrived[p, 2:3, :] for p in range(chunks)], axis=0)
    partner, forward = plane_arrivals(arrived, 4, chunks // 2)
    state[...] = state_in[...]
    state[PARTNER : PARTNER + TILE, :] = partner
    first = jnp.where(iota((1, LANES), 1) < block, summed[0:1], summed[3:4])
    for level in range(levels):
        out_ref[level] = jnp.concatenate([first, summed[1:2], z_edge(forward, level)], axis=0)


def advance(arrived, state_in, whole_load, modes_ref, near_ref, r_ref, l_ref):
    levels = arrived.shape[0]
    energy = arrived[0, 0:1, :]
    for level in range(1, levels):
        energy = energy + arrived[level, 0:1, :]
    partner = z_arrival(arrived, 2, state_in[PARTNER : PARTNER + TILE, :])
    solved = jnp.concatenate([arrived[level, 0:2, :] for level in range(levels)], axis=0)
    energy = energy[:, LANES - 1 : LANES] + total(whole_load[...] * solved)
    alpha = state_in[GAMMA : GAMMA + 1, :] / energy
    found = jnp.dot(r_ref[:, 0 : 2 * levels], solved, precision=HIGHEST)
    corners = jnp.sum(found * l_ref[...], axis=1, keepdims=True)
    coarse = jnp.sum(corners[0:CORNERS] * modes_ref[...], axis=0, keepdims=True)
    near = []
    for q in range(4):
        values = corners[CORNERS * (q + 1) : CORNERS * (q + 2)]
        near.append(jnp.sum(values * near_ref[:, SLOT * q : SLOT * (q + 1)], axis=0, keepdims=True))
    coarse = as_tile(coarse - jnp.concatenate(near, axis=1))
    image = state_in[MASK : MASK + TILE, :] * (state_in[IFACE : IFACE + TILE, :] - partner + coarse)
    multipliers = state_in[MUL : MUL + TILE, :] + alpha * state_in[DIR : DIR + TILE, :]
    residual = state_in[RES : RES + TILE, :] - alpha * image
    return multipliers, residual


def next_kernel(
    arrived, state_in, whole_load, modes_ref, near_ref, r_ref, l_ref, rt_ref, mask_row_ref, map_ref, map_tile_ref, schur_ref,
    out_ref, state,
):
    multipliers, residual = advance(arrived, state_in, whole_load, modes_ref, near_ref, r_ref, l_ref)
    y = apply_schur(
        residual, map_tile_ref[...], map_ref[...], mask_row_ref[...], schur_ref, modes_ref, near_ref, rt_ref, l_ref, out_ref
    )
    state[...] = state_in[...]
    state[RES : RES + TILE, :] = residual
    state[MUL : MUL + TILE, :] = multipliers
    state[IFACE : IFACE + TILE, :] = y


def last_kernel(
    arrived, state_in, whole_load, modes_ref, near_ref, r_ref, l_ref, out_multipliers, out_residual, scratch, sems
):
    results = advance(arrived, state_in, whole_load, modes_ref, near_ref, r_ref, l_ref)
    width = scratch.shape[3]
    none = jnp.zeros((1, width - SLOT), jnp.float32)
    lanes = iota((1, width), 1)
    copies = []
    for k, (tile, target) in enumerate(zip(results, (out_multipliers, out_residual))):
        east = jnp.concatenate([tile[0:1], tile[1:2], none], axis=1)
        south = jnp.concatenate([tile[2:3], tile[3:4], none], axis=1)
        south = pltpu.roll(jnp.broadcast_to(south, (TILE, width)), width // 2, 1)[0:1]
        scratch[k, 0] = jnp.where(lanes < width // 2, east, south)
        copies.append(pltpu.make_async_copy(scratch.at[k], target, sems.at[k]))
        copies[k].start()
    for copy in copies:
        copy.wait()


def shifted(block, axis, distance):
    devices = range(lax.axis_size(axis))
    route = [(i - distance, i) for i in devices if i - distance in devices]
    return lax.ppermute(block, axis, route)


def on_device(gap, kinv, schur, corner_modes, coarse_inverse, edge_map, corner_map, links):
    levels, chunks = lax.axis_size("z"), lax.axis_size("xl") * lax.axis_size("sy")
    width = kinv.shape[-1]
    kinv = kinv.reshape(width, width)
    ints = jnp.int32
    own_modes, east, south, west, north, map_row, map_tile, cmap = call(
        pack_kernel,
        (links, corner_modes, edge_map, gap, corner_map),
        [(CORNERS, TILE * LANES)]
        + [(CORNERS + 8, SLOT)] * 4
        + [jax.ShapeDtypeStruct((1, TILE * LANES), ints), jax.ShapeDtypeStruct((TILE, LANES), ints), (1, SLOT)],
        in_specs=[ANY] * 5,
        scratch=[
            pltpu.VMEM(links.shape, ints),
            pltpu.VMEM(corner_modes.shape, jnp.float32),
            pltpu.VMEM(edge_map.shape, ints),
            pltpu.VMEM(gap.shape, jnp.float32),
            pltpu.VMEM(corner_map.shape, ints),
            pltpu.SemaphoreType.DMA((5,)),
        ],
        name="pack",
    )
    from_west = shifted(east, "sy", 1)
    from_east = shifted(west, "sy", -1)
    from_north = shifted(south, ROWS_AXES, 1)
    from_south = shifted(north, ROWS_AXES, -1)
    schur, blocks = call(
        load_kernel,
        (schur, coarse_inverse),
        [(width, width), (chunks, TILE, LANES)],
        in_specs=[ANY] * 2,
        scratch=[pltpu.VMEM(coarse_inverse.shape, jnp.float32), pltpu.SemaphoreType.DMA((2,))],
        name="load",
    )
    square = (LANES, LANES)
    state_shape = (NSTATE, LANES)
    out, state, near, r, rt, l, mask_row = call(
        start_kernel,
        (
            east, south, from_east, from_south, from_west, from_north, cmap, map_row, map_tile, schur, own_modes, blocks,
        ),
        [(chunks, 2 * TILE, LANES), state_shape, (CORNERS, TILE * LANES), square, square, square, (1, TILE * LANES)],
        name="start",
    )
    to_plane, to_z = (chunks, TILE, LANES), (levels, 4, LANES)
    for step in range(ITERS):
        arrived = lax.all_to_all(out, PLANE, 0, 0, tiled=True)
        if step == 0:
            solver = arrived
        out, state = call(rows_kernel, (arrived, state), [to_z, state_shape], name="rows")
        arrived = lax.all_to_all(out, "z", 0, 0, tiled=True)

        def kernel(*refs, step=step):
            direction_kernel(step, *refs)

        out, state = call(
            kernel, (arrived, state, map_row, map_tile, kinv, solver), [to_plane, state_shape], name="direction"
        )
        arrived = lax.all_to_all(out, PLANE, 0, 0, tiled=True)
        out, state, load = call(solve_kernel, (arrived, state), [to_z, state_shape, (chunks, LANES)], name="solve")
        arrived = lax.all_to_all(out, "z", 0, 0, tiled=True)
        common = (arrived, state, load, own_modes, near, r, l)
        if step + 1 < ITERS:
            out, state = call(
                next_kernel, common + (rt, mask_row, map_row, map_tile, schur), [to_plane, state_shape], name="next"
            )
    return tuple(
        call(
            last_kernel,
            common,
            [gap.shape] * 2,
            out_specs=[ANY] * 2,
            scratch=[pltpu.VMEM((2,) + gap.shape[:2] + gap.shape[2:], jnp.float32), pltpu.SemaphoreType.DMA((2,))],
            name="last",
        )
    )


def solution(mesh):
    rows, cols = mesh.devices.shape
    split = Mesh(mesh.devices.reshape(rows // 2, 2, cols), ("z", "xl", "sy"))
    placed = (
        P(ROWS_AXES, "sy", None),
        P(ROWS_AXES, "sy", None, None),
        P(ROWS_AXES, "sy", None, None),
        P(ROWS_AXES, "sy", None, None),
        P(("z", "xl", "sy"), None),
        P(ROWS_AXES, "sy", None),
        P(ROWS_AXES, "sy", None),
        P(ROWS_AXES, "sy", None),
    )
    return jax.shard_map(
        on_device,
        mesh=split,
        in_specs=placed,
        out_specs=(P(ROWS_AXES, "sy", None), P(ROWS_AXES, "sy", None)),
        check_vma=False,
    )
```

time: 235 us -> 210 us (0.89)
  blocking collectives: 197 us -> 173 us
    all_to_all x12, blocking collectives: 197 us -> 173 us  [the longest x6 96.6 us: on_device(): arrived = lax.all_to_all(out, 'z', 0, 0, tiled=True)]
    unnamed x11 -> x16, local copies, waits for them, and re-layouts: 3.21 us -> 6.11 us
    reshape x10 -> x0, local copies, waits for them, and re-layouts: 2.58 us -> none  [the longest x4 1.31 us: on_device(): value.reshape(4, SLOT)[:2, :edge].reshape(gap.shape)]
    pallas_call x14 -> x15, Pallas kernels: 12 us -> 13 us  [call(): pl.pallas_call(kernel, out_shape=shapes, in_specs=in_specs or [VMEM] * le...]
where the time goes in v2:
time: 210 us; the launch traced here: 209 us
  blocking collectives  173 us (82%)
  starting transfers between devices  16 us (8%)
  Pallas kernels  13 us (6%)
  local copies, waits for them, and re-layouts  6.11 us (3%)
    all_to_all x6, blocking collectives, on_device(): arrived = lax.all_to_all(out, 'z', 0, 0, tiled=True)  96.6 us
    all_to_all x6, blocking collectives, on_device(): arrived = lax.all_to_all(out, PLANE, 0, 0, tiled=True)  76.5 us
    ppermute x4, starting transfers between devices, shifted(): return lax.ppermute(block, axis, route)  16 us
    pallas_call x15, Pallas kernels, call(): pl.pallas_call(kernel, out_shape=shapes, in_specs=in_specs or [VMEM] * le...  13 us
    unnamed x16, local copies, waits for them, and re-layouts  6.11 us
  transfers between devices with their start and end apart: 4, of which 0 were waited for; matrix products, arithmetic and copies ran while one was open for 0% of the time, Pallas kernels for 0%

profile of v2, /device:TPU:1, one launch (start us, length us, event | category | flops | bytes accessed | tf_op | source)
XLA Modules:
  0.0 209.2 jit_solution(10930126051393850733)
XLA Ops:
  0.6 0.0 copy-start.3
  0.6 0.9 copy-done.3
  1.5 0.0 copy-start.4
  1.5 0.7 copy-done.4
  2.2 0.0 copy-start.5
  2.2 0.7 copy-done.5
  2.9 0.0 copy-start.6
  2.9 0.7 copy-done.6
  3.5 0.0 copy-start.7
  3.5 0.7 copy-done.7
  4.2 0.9 pack.1
  5.1 8.8 %collective-permute-start = (f32[32,256]{1,0:T(8,128)S(1)}, f32[32,256]{1,0:T(8,128)S(1)}, u32[]{:S(2)}, u32[]{:S(2)}) collective-permute-start(f32[32,256]{1,0:T(8,128)S(1)} %get-tuple-element.46), channel_id=1, source_target_pairs={{1,0},{2,1},{3,2},{4,3},{5,4},{6,5},{7,6},{8,7},{9,8},{10,9},{11,1... | collective-permute-start | bytes 98312 | tf_op jit(solution)/shard_map/ppermute | solution.py:392
  13.9 1.3 collective-permute-start.1
  15.2 1.9 collective-permute-start.2
  17.1 4.0 %collective-permute-start.3 = (f32[32,256]{1,0:T(8,128)S(1)}, f32[32,256]{1,0:T(8,128)S(1)}, u32[]{:S(2)}, u32[]{:S(2)}) collective-permute-start(f32[32,256]{1,0:T(8,128)S(1)} %get-tuple-element.45.own_south), channel_id=1, source_target_pairs={{0,16},{16,32},{32,48},{48,64},{64,80},{80,96},{96,112},{112,128},... | collective-permute-start | bytes 98312 | tf_op jit(solution)/shard_map/ppermute | solution.py:392
  21.1 0.0 copy-start.1
  21.2 1.7 copy-done.1
  22.8 0.0 copy-start.2
  22.8 0.9 copy-done.2
  23.7 0.4 load.1
  24.1 0.0 copy-start
  24.1 0.0 collective-permute-done.from_east
  24.1 0.0 collective-permute-done.1.from_south
  24.1 0.0 collective-permute-done.2.from_west
  24.1 0.0 collective-permute-done.3.from_north
  24.2 1.8 start.1
  26.0 15.4 %all_to_all.60.arrived.refs_5_ = f32[32,16,128]{2,1,0:T(8,128)S(1)} all-to-all(f32[32,16,128]{2,1,0:T(8,128)S(1)} %get-tuple-element.54), channel_id=1, replica_groups=mesh['z'=16,'xl'=2,'sy'=16] {'xl','sy'}, dimensions={0} | all-to-all | bytes 524288 | tf_op jit(solution)/shard_map/all_to_all | solution.py:441
  41.5 26.2 %all_to_all.61.refs_0_ = f32[16,4,128]{2,1,0:T(4,128)S(1)} all-to-all(f32[16,4,128]{2,1,0:T(4,128)S(1)} %get-tuple-element.56), channel_id=1, replica_groups=mesh['z'=16,'xl'=2,'sy'=16] {'z'}, dimensions={0} | all-to-all | bytes 65536 | tf_op jit(solution)/shard_map/all_to_all | solution.py:445
  67.7 0.0 copy-done
  67.7 1.5 direction.3
  69.2 12.3 %all_to_all.62.arrived = f32[32,8,128]{2,1,0:T(8,128)S(1)} all-to-all(f32[32,8,128]{2,1,0:T(8,128)S(1)} %get-tuple-element.58), channel_id=1, replica_groups=mesh['z'=16,'xl'=2,'sy'=16] {'xl','sy'}, dimensions={0} | all-to-all | bytes 262144 | tf_op jit(solution)/shard_map/all_to_all | solution.py:453
  81.6 14.1 %all_to_all.63.arrived = f32[16,4,128]{2,1,0:T(4,128)S(1)} all-to-all(f32[16,4,128]{2,1,0:T(4,128)S(1)} %get-tuple-element.60), channel_id=1, replica_groups=mesh['z'=16,'xl'=2,'sy'=16] {'z'}, dimensions={0} | all-to-all | bytes 65536 | tf_op jit(solution)/shard_map/all_to_all | solution.py:455
  95.7 2.0 next.2
  97.7 12.2 %all_to_all.64.arrived = f32[32,8,128]{2,1,0:T(8,128)S(1)} all-to-all(f32[32,8,128]{2,1,0:T(8,128)S(1)} %get-tuple-element.68), channel_id=1, replica_groups=mesh['z'=16,'xl'=2,'sy'=16] {'xl','sy'}, dimensions={0} | all-to-all | bytes 262144 | tf_op jit(solution)/shard_map/all_to_all | solution.py:441
  109.9 14.1 %all_to_all.65.refs_0_ = f32[16,4,128]{2,1,0:T(4,128)S(1)} all-to-all(f32[16,4,128]{2,1,0:T(4,128)S(1)} %get-tuple-element.70), channel_id=1, replica_groups=mesh['z'=16,'xl'=2,'sy'=16] {'z'}, dimensions={0} | all-to-all | bytes 65536 | tf_op jit(solution)/shard_map/all_to_all | solution.py:445
  124.0 1.5 direction.4
  125.5 12.2 %all_to_all.66.arrived = f32[32,8,128]{2,1,0:T(8,128)S(1)} all-to-all(f32[32,8,128]{2,1,0:T(8,128)S(1)} %get-tuple-element.72), channel_id=1, replica_groups=mesh['z'=16,'xl'=2,'sy'=16] {'xl','sy'}, dimensions={0} | all-to-all | bytes 262144 | tf_op jit(solution)/shard_map/all_to_all | solution.py:453
  137.7 14.1 %all_to_all.67.arrived = f32[16,4,128]{2,1,0:T(4,128)S(1)} all-to-all(f32[16,4,128]{2,1,0:T(4,128)S(1)} %get-tuple-element.74), channel_id=1, replica_groups=mesh['z'=16,'xl'=2,'sy'=16] {'z'}, dimensions={0} | all-to-all | bytes 65536 | tf_op jit(solution)/shard_map/all_to_all | solution.py:455
  151.8 2.0 next.3
  153.8 12.3 %all_to_all.68.arrived = f32[32,8,128]{2,1,0:T(8,128)S(1)} all-to-all(f32[32,8,128]{2,1,0:T(8,128)S(1)} %get-tuple-element.77), channel_id=1, replica_groups=mesh['z'=16,'xl'=2,'sy'=16] {'xl','sy'}, dimensions={0} | all-to-all | bytes 262144 | tf_op jit(solution)/shard_map/all_to_all | solution.py:441
  166.2 14.1 %all_to_all.69.refs_0_ = f32[16,4,128]{2,1,0:T(4,128)S(1)} all-to-all(f32[16,4,128]{2,1,0:T(4,128)S(1)} %get-tuple-element.79), channel_id=1, replica_groups=mesh['z'=16,'xl'=2,'sy'=16] {'z'}, dimensions={0} | all-to-all | bytes 65536 | tf_op jit(solution)/shard_map/all_to_all | solution.py:445
  180.3 1.5 direction.5
  181.8 12.2 %all_to_all.70.arrived = f32[32,8,128]{2,1,0:T(8,128)S(1)} all-to-all(f32[32,8,128]{2,1,0:T(8,128)S(1)} %get-tuple-element.81), channel_id=1, replica_groups=mesh['z'=16,'xl'=2,'sy'=16] {'xl','sy'}, dimensions={0} | all-to-all | bytes 262144 | tf_op jit(solution)/shard_map/all_to_all | solution.py:453
  194.0 14.1 %all_to_all.71.arrived = f32[16,4,128]{2,1,0:T(4,128)S(1)} all-to-all(f32[16,4,128]{2,1,0:T(4,128)S(1)} %get-tuple-element.83), channel_id=1, replica_groups=mesh['z'=16,'xl'=2,'sy'=16] {'z'}, dimensions={0} | all-to-all | bytes 65536 | tf_op jit(solution)/shard_map/all_to_all | solution.py:455
  208.1 0.9 last.1
  (6 shorter events, 0.3 us)
Async XLA Ops:
  0.6 0.9 copy-start.3
  1.5 0.7 copy-start.4
  2.2 0.7 copy-start.5
  2.9 0.7 copy-start.6
  3.5 0.7 copy-start.7
  5.1 19.0 %collective-permute-start = (f32[32,256]{1,0:T(8,128)S(1)}, f32[32,256]{1,0:T(8,128)S(1)}, u32[]{:S(2)}, u32[]{:S(2)}) collective-permute-start(f32[32,256]{1,0:T(8,128)S(1)} %get-tuple-element.46), channel_id=1, source_target_pairs={{1,0},{2,1},{3,2},{4,3},{5,4},{6,5},{7,6},{8,7},{9,8},{10,9},{11,1... | collective-permute-start | bytes 98312 | tf_op jit(solution)/shard_map/ppermute | solution.py:392
  13.9 10.2 %collective-permute-start.1 = (f32[32,256]{1,0:T(8,128)S(1)}, f32[32,256]{1,0:T(8,128)S(1)}, u32[]{:S(2)}, u32[]{:S(2)}) collective-permute-start(f32[32,256]{1,0:T(8,128)S(1)} %get-tuple-element.47), channel_id=1, source_target_pairs={{16,0},{32,16},{48,32},{64,48},{80,64},{96,80},{112,96},{128,112},... | collective-permute-start | bytes 98312 | tf_op jit(solution)/shard_map/ppermute | solution.py:392
  15.2 8.9 %collective-permute-start.2 = (f32[32,256]{1,0:T(8,128)S(1)}, f32[32,256]{1,0:T(8,128)S(1)}, u32[]{:S(2)}, u32[]{:S(2)}) collective-permute-start(f32[32,256]{1,0:T(8,128)S(1)} %get-tuple-element.44.own_east), channel_id=1, source_target_pairs={{0,1},{1,2},{2,3},{3,4},{4,5},{5,6},{6,7},{7,8},{8,9},{9,10},{10,1... | collective-permute-start | bytes 98312 | tf_op jit(solution)/shard_map/ppermute | solution.py:392
  17.1 7.0 %collective-permute-start.3 = (f32[32,256]{1,0:T(8,128)S(1)}, f32[32,256]{1,0:T(8,128)S(1)}, u32[]{:S(2)}, u32[]{:S(2)}) collective-permute-start(f32[32,256]{1,0:T(8,128)S(1)} %get-tuple-element.45.own_south), channel_id=1, source_target_pairs={{0,16},{16,32},{32,48},{48,64},{64,80},{80,96},{96,112},{112,128},... | collective-permute-start | bytes 98312 | tf_op jit(solution)/shard_map/ppermute | solution.py:392
  21.1 1.7 copy-start.1
  22.8 0.9 copy-start.2
  24.1 43.6 %copy-start = (f32[1,1,768,768]{3,2,1,0:T(8,128)S(1)}, f32[1,1,768,768]{3,2,1,0:T(8,128)}, u32[]{:S(2)}) copy-start(f32[1,1,768,768]{3,2,1,0:T(8,128)} %param.9) | copy-start | bytes 7077892

commit v3 on v2

--- a/solution.py
+++ b/solution.py
@@ -14,7 +14,7 @@
 NDOF = 6
 HIGHEST = lax.Precision.HIGHEST
 VMEM = pl.BlockSpec(memory_space=pltpu.VMEM)
-ANY = pl.BlockSpec(memory_space=pl.ANY)
+HBM = pl.BlockSpec(memory_space=pl.ANY)
 LIMIT = 40 * 1024 * 1024
 
 ROWS_AXES = ("z", "xl")
@@ -35,6 +35,10 @@
         compiler_params=pltpu.CompilerParams(vmem_limit_bytes=LIMIT),
         name=name,
     )(*inputs)
+
+
+def in_hbm(*arrays):
+    return tuple(pltpu.with_memory_space_constraint(array, pltpu.HBM) for array in arrays)
 
 
 def iota(shape, dim):
@@ -399,11 +403,11 @@
     ints = jnp.int32
     own_modes, east, south, west, north, map_row, map_tile, cmap = call(
         pack_kernel,
-        (links, corner_modes, edge_map, gap, corner_map),
+        in_hbm(links, corner_modes, edge_map, gap, corner_map),
         [(CORNERS, TILE * LANES)]
         + [(CORNERS + 8, SLOT)] * 4
         + [jax.ShapeDtypeStruct((1, TILE * LANES), ints), jax.ShapeDtypeStruct((TILE, LANES), ints), (1, SLOT)],
-        in_specs=[ANY] * 5,
+        in_specs=[HBM] * 5,
         scratch=[
             pltpu.VMEM(links.shape, ints),
             pltpu.VMEM(corner_modes.shape, jnp.float32),
@@ -420,9 +424,9 @@
     from_south = shifted(north, ROWS_AXES, -1)
     schur, blocks = call(
         load_kernel,
-        (schur, coarse_inverse),
+        in_hbm(schur, coarse_inverse),
         [(width, width), (chunks, TILE, LANES)],
-        in_specs=[ANY] * 2,
+        in_specs=[HBM] * 2,
         scratch=[pltpu.VMEM(coarse_inverse.shape, jnp.float32), pltpu.SemaphoreType.DMA((2,))],
         name="load",
     )
@@ -463,7 +467,7 @@
             last_kernel,
             common,
             [gap.shape] * 2,
-            out_specs=[ANY] * 2,
+            out_specs=[HBM] * 2,
             scratch=[pltpu.VMEM((2,) + gap.shape[:2] + gap.shape[2:], jnp.float32), pltpu.SemaphoreType.DMA((2,))],
             name="last",
         )

time: 210 us -> 206 us (0.981)
  local copies, waits for them, and re-layouts: 6.11 us -> 0.01 us
    unnamed x16 -> x2, local copies, waits for them, and re-layouts: 6.11 us -> 0.01 us
    pallas_call x15, Pallas kernels: 13 us -> 15.1 us  [call(): pl.pallas_call(kernel, out_shape=shapes, in_specs=in_specs or [VMEM] * le...]
  transfers between devices with their start and end apart: 4 -> 4, of which waited for: 0 -> 0; matrix products, arithmetic and copies ran while one was open for 0% -> 0% of each run, Pallas kernels for 0% -> 1%
where the time goes in v3:
time: 206 us
  blocking collectives  174 us (84%)
  starting transfers between devices  16 us (8%)
  Pallas kernels  15.1 us (7%)
    all_to_all x6, blocking collectives, on_device(): arrived = lax.all_to_all(out, 'z', 0, 0, tiled=True)  97.1 us
    all_to_all x6, blocking collectives, on_device(): arrived = lax.all_to_all(out, PLANE, 0, 0, tiled=True)  76.5 us
    ppermute x4, starting transfers between devices, shifted(): return lax.ppermute(block, axis, route)  16 us
    pallas_call x15, Pallas kernels, call(): pl.pallas_call(kernel, out_shape=shapes, in_specs=in_specs or [VMEM] * le...  15.1 us
  transfers between devices with their start and end apart: 4, of which 0 were waited for; matrix products, arithmetic and copies ran while one was open for 0% of the time, Pallas kernels for 1%

profile of v3, /device:TPU:1, one launch (start us, length us, event | category | flops | bytes accessed | tf_op | source)
XLA Modules:
  0.0 205.8 jit_solution(5241015537338088138)
XLA Ops:
  0.6 1.7 pack.1
  2.4 8.8 %collective-permute-start = (f32[32,256]{1,0:T(8,128)S(1)}, f32[32,256]{1,0:T(8,128)S(1)}, u32[]{:S(2)}, u32[]{:S(2)}) collective-permute-start(f32[32,256]{1,0:T(8,128)S(1)} %get-tuple-element.46), channel_id=1, source_target_pairs={{1,0},{2,1},{3,2},{4,3},{5,4},{6,5},{7,6},{8,7},{9,8},{10,9},{11,1... | collective-permute-start | bytes 98312 | tf_op jit(solution)/shard_map/ppermute | solution.py:396
  11.2 1.3 collective-permute-start.1
  12.5 1.9 collective-permute-start.2
  14.4 4.0 %collective-permute-start.3 = (f32[32,256]{1,0:T(8,128)S(1)}, f32[32,256]{1,0:T(8,128)S(1)}, u32[]{:S(2)}, u32[]{:S(2)}) collective-permute-start(f32[32,256]{1,0:T(8,128)S(1)} %get-tuple-element.45.own_south), channel_id=1, source_target_pairs={{0,16},{16,32},{32,48},{48,64},{64,80},{80,96},{96,112},{112,128},... | collective-permute-start | bytes 98312 | tf_op jit(solution)/shard_map/ppermute | solution.py:396
  18.4 1.7 load.1
  20.2 0.0 copy-start
  20.2 0.0 collective-permute-done.from_east
  20.2 0.0 collective-permute-done.1.from_south
  20.2 0.0 collective-permute-done.2.from_west
  20.2 0.0 collective-permute-done.3.from_north
  20.2 1.8 start.1
  22.1 15.4 %all_to_all.60.arrived.refs_5_ = f32[32,16,128]{2,1,0:T(8,128)S(1)} all-to-all(f32[32,16,128]{2,1,0:T(8,128)S(1)} %get-tuple-element.54), channel_id=1, replica_groups=mesh['z'=16,'xl'=2,'sy'=16] {'xl','sy'}, dimensions={0} | all-to-all | bytes 524288 | tf_op jit(solution)/shard_map/all_to_all | solution.py:445
  37.5 26.7 %all_to_all.61.refs_0_ = f32[16,4,128]{2,1,0:T(4,128)S(1)} all-to-all(f32[16,4,128]{2,1,0:T(4,128)S(1)} %get-tuple-element.56), channel_id=1, replica_groups=mesh['z'=16,'xl'=2,'sy'=16] {'z'}, dimensions={0} | all-to-all | bytes 65536 | tf_op jit(solution)/shard_map/all_to_all | solution.py:449
  64.2 0.0 copy-done
  64.3 1.5 direction.3
  65.8 12.3 %all_to_all.62.arrived = f32[32,8,128]{2,1,0:T(8,128)S(1)} all-to-all(f32[32,8,128]{2,1,0:T(8,128)S(1)} %get-tuple-element.58), channel_id=1, replica_groups=mesh['z'=16,'xl'=2,'sy'=16] {'xl','sy'}, dimensions={0} | all-to-all | bytes 262144 | tf_op jit(solution)/shard_map/all_to_all | solution.py:457
  78.1 14.1 %all_to_all.63.arrived = f32[16,4,128]{2,1,0:T(4,128)S(1)} all-to-all(f32[16,4,128]{2,1,0:T(4,128)S(1)} %get-tuple-element.60), channel_id=1, replica_groups=mesh['z'=16,'xl'=2,'sy'=16] {'z'}, dimensions={0} | all-to-all | bytes 65536 | tf_op jit(solution)/shard_map/all_to_all | solution.py:459
  92.2 2.0 next.2
  94.3 12.2 %all_to_all.64.arrived = f32[32,8,128]{2,1,0:T(8,128)S(1)} all-to-all(f32[32,8,128]{2,1,0:T(8,128)S(1)} %get-tuple-element.68), channel_id=1, replica_groups=mesh['z'=16,'xl'=2,'sy'=16] {'xl','sy'}, dimensions={0} | all-to-all | bytes 262144 | tf_op jit(solution)/shard_map/all_to_all | solution.py:445
  106.5 14.1 %all_to_all.65.refs_0_ = f32[16,4,128]{2,1,0:T(4,128)S(1)} all-to-all(f32[16,4,128]{2,1,0:T(4,128)S(1)} %get-tuple-element.70), channel_id=1, replica_groups=mesh['z'=16,'xl'=2,'sy'=16] {'z'}, dimensions={0} | all-to-all | bytes 65536 | tf_op jit(solution)/shard_map/all_to_all | solution.py:449
  120.5 1.5 direction.4
  122.1 12.2 %all_to_all.66.arrived = f32[32,8,128]{2,1,0:T(8,128)S(1)} all-to-all(f32[32,8,128]{2,1,0:T(8,128)S(1)} %get-tuple-element.72), channel_id=1, replica_groups=mesh['z'=16,'xl'=2,'sy'=16] {'xl','sy'}, dimensions={0} | all-to-all | bytes 262144 | tf_op jit(solution)/shard_map/all_to_all | solution.py:457
  134.3 14.1 %all_to_all.67.arrived = f32[16,4,128]{2,1,0:T(4,128)S(1)} all-to-all(f32[16,4,128]{2,1,0:T(4,128)S(1)} %get-tuple-element.74), channel_id=1, replica_groups=mesh['z'=16,'xl'=2,'sy'=16] {'z'}, dimensions={0} | all-to-all | bytes 65536 | tf_op jit(solution)/shard_map/all_to_all | solution.py:459
  148.3 2.0 next.3
  150.4 12.3 %all_to_all.68.arrived = f32[32,8,128]{2,1,0:T(8,128)S(1)} all-to-all(f32[32,8,128]{2,1,0:T(8,128)S(1)} %get-tuple-element.77), channel_id=1, replica_groups=mesh['z'=16,'xl'=2,'sy'=16] {'xl','sy'}, dimensions={0} | all-to-all | bytes 262144 | tf_op jit(solution)/shard_map/all_to_all | solution.py:445
  162.8 14.1 %all_to_all.69.refs_0_ = f32[16,4,128]{2,1,0:T(4,128)S(1)} all-to-all(f32[16,4,128]{2,1,0:T(4,128)S(1)} %get-tuple-element.79), channel_id=1, replica_groups=mesh['z'=16,'xl'=2,'sy'=16] {'z'}, dimensions={0} | all-to-all | bytes 65536 | tf_op jit(solution)/shard_map/all_to_all | solution.py:449
  176.9 1.5 direction.5
  178.4 12.2 %all_to_all.70.arrived = f32[32,8,128]{2,1,0:T(8,128)S(1)} all-to-all(f32[32,8,128]{2,1,0:T(8,128)S(1)} %get-tuple-element.81), channel_id=1, replica_groups=mesh['z'=16,'xl'=2,'sy'=16] {'xl','sy'}, dimensions={0} | all-to-all | bytes 262144 | tf_op jit(solution)/shard_map/all_to_all | solution.py:457
  190.6 14.1 %all_to_all.71.arrived = f32[16,4,128]{2,1,0:T(4,128)S(1)} all-to-all(f32[16,4,128]{2,1,0:T(4,128)S(1)} %get-tuple-element.83), channel_id=1, replica_groups=mesh['z'=16,'xl'=2,'sy'=16] {'z'}, dimensions={0} | all-to-all | bytes 65536 | tf_op jit(solution)/shard_map/all_to_all | solution.py:459
  204.6 0.9 last.1
  (6 shorter events, 0.3 us)
Async XLA Ops:
  2.4 17.8 %collective-permute-start = (f32[32,256]{1,0:T(8,128)S(1)}, f32[32,256]{1,0:T(8,128)S(1)}, u32[]{:S(2)}, u32[]{:S(2)}) collective-permute-start(f32[32,256]{1,0:T(8,128)S(1)} %get-tuple-element.46), channel_id=1, source_target_pairs={{1,0},{2,1},{3,2},{4,3},{5,4},{6,5},{7,6},{8,7},{9,8},{10,9},{11,1... | collective-permute-start | bytes 98312 | tf_op jit(solution)/shard_map/ppermute | solution.py:396
  11.2 9.0 %collective-permute-start.1 = (f32[32,256]{1,0:T(8,128)S(1)}, f32[32,256]{1,0:T(8,128)S(1)}, u32[]{:S(2)}, u32[]{:S(2)}) collective-permute-start(f32[32,256]{1,0:T(8,128)S(1)} %get-tuple-element.47), channel_id=1, source_target_pairs={{16,0},{32,16},{48,32},{64,48},{80,64},{96,80},{112,96},{128,112},... | collective-permute-start | bytes 98312 | tf_op jit(solution)/shard_map/ppermute | solution.py:396
  12.5 7.7 %collective-permute-start.2 = (f32[32,256]{1,0:T(8,128)S(1)}, f32[32,256]{1,0:T(8,128)S(1)}, u32[]{:S(2)}, u32[]{:S(2)}) collective-permute-start(f32[32,256]{1,0:T(8,128)S(1)} %get-tuple-element.44.own_east), channel_id=1, source_target_pairs={{0,1},{1,2},{2,3},{3,4},{4,5},{5,6},{6,7},{7,8},{8,9},{9,10},{10,1... | collective-permute-start | bytes 98312 | tf_op jit(solution)/shard_map/ppermute | solution.py:396
  14.4 5.8 %collective-permute-start.3 = (f32[32,256]{1,0:T(8,128)S(1)}, f32[32,256]{1,0:T(8,128)S(1)}, u32[]{:S(2)}, u32[]{:S(2)}) collective-permute-start(f32[32,256]{1,0:T(8,128)S(1)} %get-tuple-element.45.own_south), channel_id=1, source_target_pairs={{0,16},{16,32},{32,48},{48,64},{64,80},{80,96},{96,112},{112,128},... | collective-permute-start | bytes 98312 | tf_op jit(solution)/shard_map/ppermute | solution.py:396
  20.2 44.1 %copy-start = (f32[1,1,768,768]{3,2,1,0:T(8,128)S(1)}, f32[1,1,768,768]{3,2,1,0:T(8,128)}, u32[]{:S(2)}) copy-start(f32[1,1,768,768]{3,2,1,0:T(8,128)} %param.9) | copy-start | bytes 7077892

commit v4 on v3

--- a/solution.py
+++ b/solution.py
@@ -157,8 +157,8 @@
 
 
 def pack_kernel(
-    links_hbm, modes_hbm, map_hbm, gap_hbm, cmap_hbm, out_modes, to_east, to_south, to_west, to_north, out_row, out_tile,
-    out_cmap, links_ref, modes_ref, map_ref, gap_ref, cmap_ref, sems,
+    links_hbm, modes_hbm, map_hbm, gap_hbm, cmap_hbm, schur_hbm, out_modes, col_even, col_odd, row_pair, row_cross, out_own,
+    out_row, out_tile, out_cmap, out_schur, links_ref, modes_ref, map_ref, gap_ref, cmap_ref, sems,
 ):
     copies = [
         pltpu.make_async_copy(source, target, sems.at[k])
@@ -169,8 +169,10 @@
             )
         )
     ]
+    matrix = pltpu.make_async_copy(schur_hbm.at[0, 0], out_schur, sems.at[len(copies)])
     for copy in copies:
         copy.start()
+    matrix.start()
     for copy in copies:
         copy.wait()
     nrows, ncols = lax.axis_size("z") * lax.axis_size("xl"), lax.axis_size("sy")
@@ -202,20 +204,28 @@
     cmap = out_cmap[...]
     rest = jnp.zeros((5, SLOT), jnp.float32)
     none = jnp.zeros((1, SLOT), jnp.float32)
-    for q, ref in enumerate((to_east, to_south, to_west, to_north)):
-        ref[0:CORNERS, :] = acc[:, SLOT * q : SLOT * (q + 1)]
+    parts = []
+    own = []
+    for q in range(4):
         values, mask = none, none
         if q < 2:
             mask = none + (east, south)[q]
             values = gaps[q] * mask
-        ref[CORNERS : CORNERS + 8, :] = jnp.concatenate([values, mask, cmap, rest], axis=0)
-
-
-def load_kernel(schur_hbm, coarse_hbm, schur_out, blocks_out, coarse_ref, sems):
-    matrix = pltpu.make_async_copy(schur_hbm.at[0, 0], schur_out, sems.at[0])
-    coarse = pltpu.make_async_copy(coarse_hbm, coarse_ref, sems.at[1])
+            own += [values, mask]
+        parts.append(jnp.concatenate([acc[:, SLOT * q : SLOT * (q + 1)], values, mask, cmap, rest], axis=0))
+    out_own[...] = jnp.concatenate(own + [jnp.zeros((4, SLOT), jnp.float32)], axis=0)
+    even = lax.axis_index("sy") % 2 == 0
+    first_row = lax.axis_index("xl") == 0
+    col_even[...] = jnp.where(even, parts[0], parts[2])
+    col_odd[...] = jnp.where(even, parts[2], parts[0])
+    row_pair[...] = jnp.where(first_row, parts[1], parts[3])
+    row_cross[...] = jnp.where(first_row, parts[3], parts[1])
+    matrix.wait()
+
+
+def load_kernel(coarse_hbm, blocks_out, coarse_ref, sem):
+    coarse = pltpu.make_async_copy(coarse_hbm, coarse_ref, sem)
     coarse.start()
-    matrix.start()
     coarse.wait()
     chunks = blocks_out.shape[0]
     ncoarse = coarse_ref.shape[1]
@@ -234,25 +244,30 @@
         if shift:
             window = pltpu.roll(window, SLOT - shift, 1)
         blocks_out[p] = jnp.where(lanes < block, window[:, 0:LANES], 0.0)
-    matrix.wait()
 
 
 def start_kernel(
-    own_east, own_south, from_east, from_south, from_west, from_north, cmap_ref, map_ref, map_tile_ref, schur_ref, modes_ref,
-    blocks_ref, out_ref, state, near, r_ref, rt_ref, l_ref, mask_row_ref,
+    own_ref, col_even, col_odd, row_pair, row_cross, cmap_ref, map_ref, map_tile_ref, schur_ref, modes_ref, blocks_ref, out_ref,
+    state, near, r_ref, rt_ref, l_ref, mask_row_ref,
 ):
     chunks = out_ref.shape[0]
     block = NDOF * chunks // 2
     row, cm = CORNERS, CORNERS + 2
+    even = lax.axis_index("sy") % 2 == 0
+    first_row = lax.axis_index("xl") == 0
+    from_east = jnp.where(even, col_even[...], col_odd[...])
+    from_west = jnp.where(even, col_odd[...], col_even[...])
+    from_south = jnp.where(first_row, row_pair[...], row_cross[...])
+    from_north = jnp.where(first_row, row_cross[...], row_pair[...])
     sources = (from_east, from_south, from_west, from_north)
-    for q, ref in enumerate(sources):
-        near[:, SLOT * q : SLOT * (q + 1)] = ref[0:CORNERS, :]
-    values = [own_east[row : row + 1], own_south[row : row + 1], -from_west[row : row + 1], -from_north[row : row + 1]]
-    masks = [ref[row + 1 : row + 2] for ref in (own_east, own_south, from_west, from_north)]
+    for q, part in enumerate(sources):
+        near[:, SLOT * q : SLOT * (q + 1)] = part[0:CORNERS]
+    values = [own_ref[0:1], own_ref[2:3], -from_west[row : row + 1], -from_north[row : row + 1]]
+    masks = [own_ref[1:2], own_ref[3:4], from_west[row + 1 : row + 2], from_north[row + 1 : row + 2]]
     residual = as_tile(jnp.concatenate(values, axis=1))
     mask_row = jnp.concatenate(masks, axis=1)
     mask_row_ref[...] = mask_row
-    maps = [cmap_ref[:, 0:LANES]] + [ref[cm : cm + 1, 0:LANES] for ref in sources]
+    maps = [cmap_ref[:, 0:LANES]] + [part[cm : cm + 1, 0:LANES] for part in sources]
     columns = jnp.transpose(jnp.concatenate(maps + [jnp.zeros((3, LANES), jnp.float32)], axis=0))
     column = [columns[0:CORNERS, g : g + 1] for g in range(5)]
     column.append(jnp.full((LANES - 5 * CORNERS, 1), float(block * chunks), jnp.float32))
@@ -390,9 +405,11 @@
         copy.wait()
 
 
-def shifted(block, axis, distance):
-    devices = range(lax.axis_size(axis))
-    route = [(i - distance, i) for i in devices if i - distance in devices]
+def swapped(block, axis, first):
+    count = lax.axis_size(axis)
+    route = []
+    for i in range(first, count - 1, 2):
+        route += [(i, i + 1), (i + 1, i)]
     return lax.ppermute(block, axis, route)
 
 
@@ -401,33 +418,34 @@
     width = kinv.shape[-1]
     kinv = kinv.reshape(width, width)
     ints = jnp.int32
-    own_modes, east, south, west, north, map_row, map_tile, cmap = call(
+    own_modes, col_even, col_odd, row_pair, row_cross, own, map_row, map_tile, cmap, schur = call(
         pack_kernel,
-        in_hbm(links, corner_modes, edge_map, gap, corner_map),
+        in_hbm(links, corner_modes, edge_map, gap, corner_map, schur),
         [(CORNERS, TILE * LANES)]
         + [(CORNERS + 8, SLOT)] * 4
-        + [jax.ShapeDtypeStruct((1, TILE * LANES), ints), jax.ShapeDtypeStruct((TILE, LANES), ints), (1, SLOT)],
-        in_specs=[HBM] * 5,
+        + [(TILE, SLOT), jax.ShapeDtypeStruct((1, TILE * LANES), ints), jax.ShapeDtypeStruct((TILE, LANES), ints)]
+        + [(1, SLOT), (width, width)],
+        in_specs=[HBM] * 6,
         scratch=[
             pltpu.VMEM(links.shape, ints),
             pltpu.VMEM(corner_modes.shape, jnp.float32),
             pltpu.VMEM(edge_map.shape, ints),
             pltpu.VMEM(gap.shape, jnp.float32),
             pltpu.VMEM(corner_map.shape, ints),
-            pltpu.SemaphoreType.DMA((5,)),
+            pltpu.SemaphoreType.DMA((6,)),
         ],
         name="pack",
     )
-    from_west = shifted(east, "sy", 1)
-    from_east = shifted(west, "sy", -1)
-    from_north = shifted(south, ROWS_AXES, 1)
-    from_south = shifted(north, ROWS_AXES, -1)
-    schur, blocks = call(
+    col_even = swapped(col_even, "sy", 0)
+    col_odd = swapped(col_odd, "sy", 1)
+    row_pair = swapped(row_pair, ROWS_AXES, 0)
+    row_cross = swapped(row_cross, ROWS_AXES, 1)
+    (blocks,) = call(
         load_kernel,
-        in_hbm(schur, coarse_inverse),
-        [(width, width), (chunks, TILE, LANES)],
-        in_specs=[HBM] * 2,
-        scratch=[pltpu.VMEM(coarse_inverse.shape, jnp.float32), pltpu.SemaphoreType.DMA((2,))],
+        in_hbm(coarse_inverse),
+        [(chunks, TILE, LANES)],
+        in_specs=[HBM],
+        scratch=[pltpu.VMEM(coarse_inverse.shape, jnp.float32), pltpu.SemaphoreType.DMA(())],
         name="load",
     )
     square = (LANES, LANES)
@@ -435,7 +453,7 @@
     out, state, near, r, rt, l, mask_row = call(
         start_kernel,
         (
-            east, south, from_east, from_south, from_west, from_north, cmap, map_row, map_tile, schur, own_modes, blocks,
+            own, col_even, col_odd, row_pair, row_cross, cmap, map_row, map_tile, schur, own_modes, blocks,
         ),
         [(chunks, 2 * TILE, LANES), state_shape, (CORNERS, TILE * LANES), square, square, square, (1, TILE * LANES)],
         name="start",

time: 206 us -> 207 us (level)
  starting transfers between devices: 16 us -> 13.4 us
    ppermute x4, starting transfers between devices: 16 us -> 13.4 us  [swapped(): return lax.ppermute(block, axis, route)]
    all_to_all x6, blocking collectives: 76.5 us -> 79 us  [on_device(): arrived = lax.all_to_all(out, PLANE, 0, 0, tiled=True)]
  transfers between devices with their start and end apart: 4 -> 4, of which waited for: 0 -> 1; matrix products, arithmetic and copies ran while one was open for 0% -> 0% of each run, Pallas kernels for 1% -> 0%
where the time goes in v4:
time: 207 us; the launch traced here: 206 us
  blocking collectives  176 us (85%)
  Pallas kernels  14.5 us (7%)
  starting transfers between devices  13.4 us (6%)
    all_to_all x6, blocking collectives, on_device(): arrived = lax.all_to_all(out, 'z', 0, 0, tiled=True)  97 us
    all_to_all x6, blocking collectives, on_device(): arrived = lax.all_to_all(out, PLANE, 0, 0, tiled=True)  79 us
    pallas_call x15, Pallas kernels, call(): pl.pallas_call(kernel, out_shape=shapes, in_specs=in_specs or [VMEM] * le...  14.5 us
    ppermute x4, starting transfers between devices, swapped(): return lax.ppermute(block, axis, route)  13.4 us
  transfers between devices with their start and end apart: 4, of which 1 were waited for; matrix products, arithmetic and copies ran while one was open for 0% of the time, Pallas kernels for 0%

profile of v4, /device:TPU:1, one launch (start us, length us, event | category | flops | bytes accessed | tf_op | source)
XLA Modules:
  0.0 205.9 jit_solution(3115054541975035242)
XLA Ops:
  0.6 1.8 pack.1
  2.5 0.0 copy-start
  2.5 8.9 %collective-permute-start = (f32[32,256]{1,0:T(8,128)S(1)}, f32[32,256]{1,0:T(8,128)S(1)}, u32[]{:S(2)}, u32[]{:S(2)}) collective-permute-start(f32[32,256]{1,0:T(8,128)S(1)} %get-tuple-element.45), channel_id=1, source_target_pairs={{0,1},{1,0},{2,3},{3,2},{4,5},{5,4},{6,7},{7,6},{8,9},{9,8},{10,11... | collective-permute-start | bytes 98312 | tf_op jit(solution)/shard_map/ppermute | solution.py:413
  11.4 1.9 collective-permute-start.1
  13.3 1.9 collective-permute-start.2
  15.3 0.7 collective-permute-start.3
  15.9 1.0 load.1.blocks_ref
  17.0 0.0 collective-permute-done.col_even
  17.0 0.0 collective-permute-done.1.col_odd
  17.0 1.0 collective-permute-done.2.row_pair
  18.0 0.0 collective-permute-done.3.row_cross
  18.0 1.8 start.1
  19.8 17.8 %all_to_all.60.arrived.refs_5_ = f32[32,16,128]{2,1,0:T(8,128)S(1)} all-to-all(f32[32,16,128]{2,1,0:T(8,128)S(1)} %get-tuple-element.54), channel_id=1, replica_groups=mesh['z'=16,'xl'=2,'sy'=16] {'xl','sy'}, dimensions={0} | all-to-all | bytes 524288 | tf_op jit(solution)/shard_map/all_to_all | solution.py:463
  37.7 26.6 %all_to_all.61.refs_0_ = f32[16,4,128]{2,1,0:T(4,128)S(1)} all-to-all(f32[16,4,128]{2,1,0:T(4,128)S(1)} %get-tuple-element.56), channel_id=1, replica_groups=mesh['z'=16,'xl'=2,'sy'=16] {'z'}, dimensions={0} | all-to-all | bytes 65536 | tf_op jit(solution)/shard_map/all_to_all | solution.py:467
  64.4 0.0 copy-done
  64.4 1.5 direction.3
  65.9 12.3 %all_to_all.62.arrived = f32[32,8,128]{2,1,0:T(8,128)S(1)} all-to-all(f32[32,8,128]{2,1,0:T(8,128)S(1)} %get-tuple-element.58), channel_id=1, replica_groups=mesh['z'=16,'xl'=2,'sy'=16] {'xl','sy'}, dimensions={0} | all-to-all | bytes 262144 | tf_op jit(solution)/shard_map/all_to_all | solution.py:475
  78.2 14.1 %all_to_all.63.arrived = f32[16,4,128]{2,1,0:T(4,128)S(1)} all-to-all(f32[16,4,128]{2,1,0:T(4,128)S(1)} %get-tuple-element.60), channel_id=1, replica_groups=mesh['z'=16,'xl'=2,'sy'=16] {'z'}, dimensions={0} | all-to-all | bytes 65536 | tf_op jit(solution)/shard_map/all_to_all | solution.py:477
  92.3 2.0 next.2
  94.4 12.2 %all_to_all.64.arrived = f32[32,8,128]{2,1,0:T(8,128)S(1)} all-to-all(f32[32,8,128]{2,1,0:T(8,128)S(1)} %get-tuple-element.68), channel_id=1, replica_groups=mesh['z'=16,'xl'=2,'sy'=16] {'xl','sy'}, dimensions={0} | all-to-all | bytes 262144 | tf_op jit(solution)/shard_map/all_to_all | solution.py:463
  106.6 14.1 %all_to_all.65.refs_0_ = f32[16,4,128]{2,1,0:T(4,128)S(1)} all-to-all(f32[16,4,128]{2,1,0:T(4,128)S(1)} %get-tuple-element.70), channel_id=1, replica_groups=mesh['z'=16,'xl'=2,'sy'=16] {'z'}, dimensions={0} | all-to-all | bytes 65536 | tf_op jit(solution)/shard_map/all_to_all | solution.py:467
  120.7 1.5 direction.4
  122.2 12.2 %all_to_all.66.arrived = f32[32,8,128]{2,1,0:T(8,128)S(1)} all-to-all(f32[32,8,128]{2,1,0:T(8,128)S(1)} %get-tuple-element.72), channel_id=1, replica_groups=mesh['z'=16,'xl'=2,'sy'=16] {'xl','sy'}, dimensions={0} | all-to-all | bytes 262144 | tf_op jit(solution)/shard_map/all_to_all | solution.py:475
  134.4 14.1 %all_to_all.67.arrived = f32[16,4,128]{2,1,0:T(4,128)S(1)} all-to-all(f32[16,4,128]{2,1,0:T(4,128)S(1)} %get-tuple-element.74), channel_id=1, replica_groups=mesh['z'=16,'xl'=2,'sy'=16] {'z'}, dimensions={0} | all-to-all | bytes 65536 | tf_op jit(solution)/shard_map/all_to_all | solution.py:477
  148.5 2.0 next.3
  150.5 12.3 %all_to_all.68.arrived = f32[32,8,128]{2,1,0:T(8,128)S(1)} all-to-all(f32[32,8,128]{2,1,0:T(8,128)S(1)} %get-tuple-element.77), channel_id=1, replica_groups=mesh['z'=16,'xl'=2,'sy'=16] {'xl','sy'}, dimensions={0} | all-to-all | bytes 262144 | tf_op jit(solution)/shard_map/all_to_all | solution.py:463
  162.9 14.1 %all_to_all.69.refs_0_ = f32[16,4,128]{2,1,0:T(4,128)S(1)} all-to-all(f32[16,4,128]{2,1,0:T(4,128)S(1)} %get-tuple-element.79), channel_id=1, replica_groups=mesh['z'=16,'xl'=2,'sy'=16] {'z'}, dimensions={0} | all-to-all | bytes 65536 | tf_op jit(solution)/shard_map/all_to_all | solution.py:467
  177.0 1.5 direction.5
  178.5 12.2 %all_to_all.70.arrived = f32[32,8,128]{2,1,0:T(8,128)S(1)} all-to-all(f32[32,8,128]{2,1,0:T(8,128)S(1)} %get-tuple-element.81), channel_id=1, replica_groups=mesh['z'=16,'xl'=2,'sy'=16] {'xl','sy'}, dimensions={0} | all-to-all | bytes 262144 | tf_op jit(solution)/shard_map/all_to_all | solution.py:475
  190.7 14.1 %all_to_all.71.arrived = f32[16,4,128]{2,1,0:T(4,128)S(1)} all-to-all(f32[16,4,128]{2,1,0:T(4,128)S(1)} %get-tuple-element.83), channel_id=1, replica_groups=mesh['z'=16,'xl'=2,'sy'=16] {'z'}, dimensions={0} | all-to-all | bytes 65536 | tf_op jit(solution)/shard_map/all_to_all | solution.py:477
  204.8 0.9 last.1
  (6 shorter events, 0.3 us)
Async XLA Ops:
  2.5 61.9 %copy-start = (f32[1,1,768,768]{3,2,1,0:T(8,128)S(1)}, f32[1,1,768,768]{3,2,1,0:T(8,128)}, u32[]{:S(2)}) copy-start(f32[1,1,768,768]{3,2,1,0:T(8,128)} %param.9) | copy-start | bytes 7077892
  2.5 14.5 %collective-permute-start = (f32[32,256]{1,0:T(8,128)S(1)}, f32[32,256]{1,0:T(8,128)S(1)}, u32[]{:S(2)}, u32[]{:S(2)}) collective-permute-start(f32[32,256]{1,0:T(8,128)S(1)} %get-tuple-element.45), channel_id=1, source_target_pairs={{0,1},{1,0},{2,3},{3,2},{4,5},{5,4},{6,7},{7,6},{8,9},{9,8},{10,11... | collective-permute-start | bytes 98312 | tf_op jit(solution)/shard_map/ppermute | solution.py:413
  11.4 5.6 %collective-permute-start.1 = (f32[32,256]{1,0:T(8,128)S(1)}, f32[32,256]{1,0:T(8,128)S(1)}, u32[]{:S(2)}, u32[]{:S(2)}) collective-permute-start(f32[32,256]{1,0:T(8,128)S(1)} %get-tuple-element.46), channel_id=1, source_target_pairs={{1,2},{2,1},{3,4},{4,3},{5,6},{6,5},{7,8},{8,7},{9,10},{10,9},{11,... | collective-permute-start | bytes 98312 | tf_op jit(solution)/shard_map/ppermute | solution.py:413
  13.3 4.7 %collective-permute-start.2 = (f32[32,256]{1,0:T(8,128)S(1)}, f32[32,256]{1,0:T(8,128)S(1)}, u32[]{:S(2)}, u32[]{:S(2)}) collective-permute-start(f32[32,256]{1,0:T(8,128)S(1)} %get-tuple-element.47), channel_id=1, source_target_pairs={{0,16},{16,0},{32,48},{48,32},{64,80},{80,64},{96,112},{112,96},{1... | collective-permute-start | bytes 98312 | tf_op jit(solution)/shard_map/ppermute | solution.py:413
  15.3 2.7 %collective-permute-start.3 = (f32[32,256]{1,0:T(8,128)S(1)}, f32[32,256]{1,0:T(8,128)S(1)}, u32[]{:S(2)}, u32[]{:S(2)}) collective-permute-start(f32[32,256]{1,0:T(8,128)S(1)} %get-tuple-element.48), channel_id=1, source_target_pairs={{16,32},{32,16},{48,64},{64,48},{80,96},{96,80},{112,128},{128,112... | collective-permute-start | bytes 98312 | tf_op jit(solution)/shard_map/ppermute | solution.py:413

commit v5 on v4

--- a/solution.py
+++ b/solution.py
@@ -1,3 +1,5 @@
+import functools
+
 import jax
 import jax.numpy as jnp
 from jax import lax
@@ -20,8 +22,8 @@
 ROWS_AXES = ("z", "xl")
 PLANE = ("xl", "sy")
 
-RES, MUL, DIR, IFACE, PARTNER, MASK, SCAL, NSTATE = 0, 8, 16, 24, 32, 40, 48, 56
-GAMMA, LOAD = 48, 49
+RES, MUL, DIR, IFACE, PARTNER, MASK, SCAL, INNER, NSTATE = 0, 8, 16, 24, 32, 40, 48, 56, 64
+GAMMA, LOAD, CARRY, ENERGY = 48, 49, 50, 51
 
 
 def call(kernel, inputs, outputs, in_specs=None, out_specs=None, scratch=(), name=None):
@@ -143,16 +145,17 @@
     return jnp.concatenate([partner[0:2], south, partner[4:6], north], axis=0)
 
 
-def apply_schur(tile, map_tile, map_row, mask_row, schur_ref, modes_ref, near_ref, rt_ref, l_ref, out_ref):
+def apply_schur(tile, map_tile, map_row, mask_row, schur_ref, modes_ref, near_ref, rt_ref, l_ref, out_ref, nrows):
     chunks = out_ref.shape[0]
     y_row = apply_matrix(tile, map_tile, map_row, schur_ref)
-    load = coarse_load(0.25 * mask_row * y_row, modes_ref, near_ref, rt_ref, l_ref, chunks)
+    load = coarse_load(0.25 * mask_row * y_row, modes_ref, near_ref, rt_ref, l_ref, nrows)
     y = as_tile(y_row)
     gamma = jnp.broadcast_to(0.25 * total(tile * y), (1, LANES))
     rest = jnp.zeros((2, LANES), jnp.float32)
     for p in range(chunks):
         first, second = plane_edges(y, p, chunks // 2)
-        out_ref[p, 0:TILE, :] = jnp.concatenate([load[p : p + 1], gamma, first, second, rest], axis=0)
+        chunk = load[p : p + 1] if p < nrows else jnp.zeros((1, LANES), jnp.float32)
+        out_ref[p, 0:TILE, :] = jnp.concatenate([chunk, gamma, first, second, rest], axis=0)
     return y
 
 
@@ -227,31 +230,18 @@
     coarse = pltpu.make_async_copy(coarse_hbm, coarse_ref, sem)
     coarse.start()
     coarse.wait()
-    chunks = blocks_out.shape[0]
     ncoarse = coarse_ref.shape[1]
-    block = ncoarse // chunks
-    padded = -(-ncoarse // LANES) * LANES
-    values = coarse_ref[...]
-    if padded > ncoarse:
-        values = jnp.pad(values, ((0, 0), (0, padded - ncoarse)))
-    values = jnp.concatenate([values, jnp.zeros((TILE - NDOF, padded), jnp.float32)], axis=0)
-    values = jnp.concatenate([values, jnp.zeros((TILE, LANES), jnp.float32)], axis=1)
-    lanes = iota((TILE, LANES), 1)
-    for p in range(chunks):
-        start = block * p // LANES * LANES
-        window = values[:, start : start + SLOT]
-        shift = block * p - start
-        if shift:
-            window = pltpu.roll(window, SLOT - shift, 1)
-        blocks_out[p] = jnp.where(lanes < block, window[:, 0:LANES], 0.0)
+    blocks_out[...] = jnp.zeros(blocks_out.shape, jnp.float32)
+    for p in range(-(-ncoarse // LANES)):
+        width = min(LANES, ncoarse - p * LANES)
+        blocks_out[p, 0:NDOF, 0:width] = coarse_ref[:, p * LANES : p * LANES + width]
 
 
 def start_kernel(
-    own_ref, col_even, col_odd, row_pair, row_cross, cmap_ref, map_ref, map_tile_ref, schur_ref, modes_ref, blocks_ref, out_ref,
+    nrows, own_ref, col_even, col_odd, row_pair, row_cross, cmap_ref, map_ref, map_tile_ref, schur_ref, modes_ref, blocks_ref, out_ref,
     state, near, r_ref, rt_ref, l_ref, mask_row_ref,
 ):
     chunks = out_ref.shape[0]
-    block = NDOF * chunks // 2
     row, cm = CORNERS, CORNERS + 2
     even = lax.axis_index("sy") % 2 == 0
     first_row = lax.axis_index("xl") == 0
@@ -270,16 +260,18 @@
     maps = [cmap_ref[:, 0:LANES]] + [part[cm : cm + 1, 0:LANES] for part in sources]
     columns = jnp.transpose(jnp.concatenate(maps + [jnp.zeros((3, LANES), jnp.float32)], axis=0))
     column = [columns[0:CORNERS, g : g + 1] for g in range(5)]
-    column.append(jnp.full((LANES - 5 * CORNERS, 1), float(block * chunks), jnp.float32))
+    column.append(jnp.full((LANES - 5 * CORNERS, 1), float(nrows * LANES), jnp.float32))
     column = jnp.concatenate(column, axis=0)
-    group = jnp.floor((column + 0.5) * (1.0 / block))
-    inside = column - group * block
+    group = jnp.floor((column + 0.5) * (1.0 / LANES))
+    inside = column - group * LANES
     lanes = iota((LANES, LANES), 1).astype(jnp.float32)
-    hit_row = jnp.where((group == lanes) & (lanes < chunks), 1.0, 0.0)
+    hit_row = jnp.where((group == lanes) & (lanes < nrows), 1.0, 0.0)
     r_ref[...] = hit_row
     rt_ref[...] = jnp.transpose(hit_row)
     l_ref[...] = jnp.where(inside == lanes, 1.0, 0.0)
-    y = apply_schur(residual, map_tile_ref[...], map_ref[...], mask_row, schur_ref, modes_ref, near, rt_ref, l_ref, out_ref)
+    y = apply_schur(
+        residual, map_tile_ref[...], map_ref[...], mask_row, schur_ref, modes_ref, near, rt_ref, l_ref, out_ref, nrows
+    )
     for p in range(chunks):
         out_ref[p, TILE : 2 * TILE, :] = blocks_ref[p]
     state[...] = jnp.zeros(state.shape, jnp.float32)
@@ -288,7 +280,7 @@
     state[MASK : MASK + TILE, :] = as_tile(mask_row)
 
 
-def rows_kernel(arrived, state_in, out_ref, state):
+def rows_kernel(arrived, state_in, out_ref, state, own_block):
     chunks, levels = arrived.shape[0], out_ref.shape[0]
     summed = arrived[0, 0:TILE, :]
     for p in range(1, chunks):
@@ -298,11 +290,13 @@
     state[PARTNER : PARTNER + TILE, :] = partner
     for level in range(levels):
         out_ref[level] = jnp.concatenate([summed[0:2], z_edge(forward, level)], axis=0)
-
-
-def direction_kernel(step, arrived, state_in, map_ref, map_tile_ref, kinv_ref, blocks_ref, out_ref, state):
+    block = jnp.concatenate([arrived[p, TILE : TILE + NDOF, :] for p in range(chunks)], axis=0)
+    for k in range(own_block.shape[0]):
+        own_block[k] = block[k * TILE : (k + 1) * TILE]
+
+
+def first_direction_kernel(arrived, state_in, map_ref, map_tile_ref, kinv_ref, block_ref, out_ref, state):
     chunks, levels = out_ref.shape[0], arrived.shape[0]
-    half = chunks // 2
     summed = arrived[0]
     for level in range(1, levels):
         summed = summed + arrived[level]
@@ -310,55 +304,140 @@
     direction = 0.25 * state_in[MASK : MASK + TILE, :] * (state_in[IFACE : IFACE + TILE, :] - partner)
     load = summed[0:1]
     gamma = summed[1:2]
-    if step:
-        beta = gamma / state_in[GAMMA : GAMMA + 1, :]
-        direction = direction + beta * state_in[DIR : DIR + TILE, :]
-        load = load + beta * state_in[LOAD : LOAD + 1, :]
     inner = as_tile(apply_matrix(direction, map_tile_ref[...], map_ref[...], kinv_ref))
     energy = jnp.broadcast_to(total(direction * inner), (1, LANES))
-    lanes = iota((TILE, LANES), 1)
-    dof = iota((TILE, LANES), 0)
-    solved = []
-    for a in range(2):
-        acc = jnp.zeros((TILE, LANES), jnp.float32)
-        for p in range(half):
-            column = jnp.sum(blocks_ref[a * half + p, TILE : 2 * TILE, :] * load, axis=1, keepdims=True)
-            acc = acc + jnp.where((lanes == dof + p * NDOF) & (dof < NDOF), column, 0.0)
-        solved.append(jnp.sum(acc, axis=0, keepdims=True))
+    place = iota((TILE, LANES), 1) - iota((TILE, LANES), 0) - lax.rem(lax.axis_index("z") * (NDOF * chunks), LANES)
+    window = [jnp.zeros((TILE, LANES), jnp.float32)] * 2
+    for k in range(block_ref.shape[0]):
+        column = jnp.sum(block_ref[k] * load, axis=1, keepdims=True)
+        window = [window[a] + jnp.where(place + a * LANES == k * TILE, column, 0.0) for a in range(2)]
+    window = [jnp.sum(half, axis=0, keepdims=True) for half in window]
     for p in range(chunks):
-        first, second = plane_edges(inner, p, half)
-        out_ref[p] = jnp.concatenate(solved + [load, energy, first, second], axis=0)
+        first, second = plane_edges(inner, p, chunks // 2)
+        out_ref[p] = jnp.concatenate(window + [load, energy, first, second], axis=0)
     state[...] = state_in[...]
     state[DIR : DIR + TILE, :] = direction
-    state[IFACE : IFACE + TILE, :] = inner
+    state[INNER : INNER + TILE, :] = inner
     state[SCAL : SCAL + TILE, :] = jnp.concatenate([gamma, load, jnp.zeros((6, LANES), jnp.float32)], axis=0)
 
 
-def solve_kernel(arrived, state_in, out_ref, state, whole_load):
+def first_solve_kernel(arrived, state_in, out_ref, state, whole_load):
     chunks, levels = arrived.shape[0], out_ref.shape[0]
-    block = NDOF * chunks // 2
+    size = NDOF * chunks
     summed = arrived[0]
     for p in range(1, chunks):
         summed = summed + arrived[p]
-    whole_load[...] = jnp.concatenate([arrived[p, 2:3, :] for p in range(chunks)], axis=0)
+    for p in range(whole_load.shape[0]):
+        whole_load[p : p + 1, :] = arrived[p, 2:3, :]
     partner, forward = plane_arrivals(arrived, 4, chunks // 2)
     state[...] = state_in[...]
     state[PARTNER : PARTNER + TILE, :] = partner
-    first = jnp.where(iota((1, LANES), 1) < block, summed[0:1], summed[3:4])
+    begin = lax.rem(lax.axis_index("z") * size, LANES)
+    places = iota((2, LANES), 1) + LANES * iota((2, LANES), 0) - begin
+    window = jnp.where((places >= 0) & (places < size), summed[0:2], summed[3:4])
     for level in range(levels):
-        out_ref[level] = jnp.concatenate([first, summed[1:2], z_edge(forward, level)], axis=0)
-
-
-def advance(arrived, state_in, whole_load, modes_ref, near_ref, r_ref, l_ref):
-    levels = arrived.shape[0]
-    energy = arrived[0, 0:1, :]
+        out_ref[level] = jnp.concatenate([window, z_edge(forward, level)], axis=0)
+
+
+def first_image_parts(arrived, state_in, whole_load):
+    levels, nrows = arrived.shape[0], whole_load.shape[0]
+    size = NDOF * 2 * lax.axis_size("sy")
+    energy = jnp.zeros((1, 1), jnp.float32)
+    rows = [jnp.zeros((1, LANES), jnp.float32)] * (nrows + 2)
+    lanes = iota((1, LANES), 1)
+    for level in range(levels):
+        base, begin = divmod(level * size, LANES)
+        for a in range(2):
+            places = lanes + (a * LANES - begin)
+            values = arrived[level, a : a + 1, :]
+            rows[base + a] = rows[base + a] + jnp.where((places >= 0) & (places < size), values, 0.0)
+        if begin + size < 2 * LANES:
+            energy = energy + arrived[level, 1:2, LANES - 1 : LANES]
+        else:
+            energy = energy + arrived[level, 0:1, 0:1]
+    partner = z_arrival(arrived, 2, state_in[PARTNER : PARTNER + TILE, :])
+    return energy, partner, whole_load[...], jnp.concatenate(rows[0:nrows], axis=0)
+
+
+def with_crossing(partner, crossed):
+    pair = lax.axis_index("xl")
+    south = jnp.where(pair == 0, partner[2:4], crossed[6:8])
+    north = jnp.where(pair == 0, crossed[2:4], partner[6:8])
+    return jnp.concatenate([partner[0:2], south, partner[4:6], north], axis=0)
+
+
+def inner_kernel(arrived, crossed, state_in, map_ref, map_tile_ref, kinv_ref, out_ref, state):
+    chunks, levels = arrived.shape[0], out_ref.shape[0]
+    summed = arrived[0]
+    for p in range(1, chunks):
+        summed = summed + arrived[p]
+    partner, _ = plane_arrivals(arrived, 2, chunks // 2)
+    partner = with_crossing(partner, crossed[...])
+    z = 0.25 * state_in[MASK : MASK + TILE, :] * (state_in[IFACE : IFACE + TILE, :] - partner)
+    inner = as_tile(apply_matrix(z, map_tile_ref[...], map_ref[...], kinv_ref))
+    own = jnp.broadcast_to(total(z * inner), (1, LANES))
+    mixed = z * state_in[INNER : INNER + TILE, :] + state_in[DIR : DIR + TILE, :] * inner
+    mixed = jnp.broadcast_to(total(mixed), (1, LANES))
+    message = jnp.concatenate([summed[0:2], own, mixed], axis=0)
+    for level in range(levels):
+        out_ref[level] = message
+    state[...] = state_in[...]
+    state[IFACE : IFACE + TILE, :] = inner
+    state[PARTNER : PARTNER + TILE, :] = z
+
+
+def direction_kernel(arrived, state_in, columns_ref, out_ref, state, crossing):
+    chunks, levels = out_ref.shape[0], arrived.shape[0]
+    summed = arrived[0]
     for level in range(1, levels):
-        energy = energy + arrived[level, 0:1, :]
-    partner = z_arrival(arrived, 2, state_in[PARTNER : PARTNER + TILE, :])
-    solved = jnp.concatenate([arrived[level, 0:2, :] for level in range(levels)], axis=0)
-    energy = energy[:, LANES - 1 : LANES] + total(whole_load[...] * solved)
+        summed = summed + arrived[level]
+    gamma = summed[1:2]
+    beta = gamma / state_in[GAMMA : GAMMA + 1, :]
+    direction = state_in[PARTNER : PARTNER + TILE, :] + beta * state_in[DIR : DIR + TILE, :]
+    inner = state_in[IFACE : IFACE + TILE, :] + beta * state_in[INNER : INNER + TILE, :]
+    load = summed[0:1] + beta * state_in[LOAD : LOAD + 1, :]
+    energy = summed[2:3] + beta * summed[3:4]
+    carry = beta * beta * state_in[ENERGY : ENERGY + 1, :]
+    place = iota((TILE, LANES), 1) - iota((TILE, LANES), 0)
+    groups = columns_ref.shape[0]
+    per_row = LANES // TILE
+    message = []
+    for r in range(-(-groups // per_row)):
+        acc = jnp.zeros((TILE, LANES), jnp.float32)
+        for k in range(min(per_row, groups - r * per_row)):
+            column = jnp.sum(columns_ref[r * per_row + k] * load, axis=1, keepdims=True)
+            acc = acc + jnp.where(place == k * TILE, column, 0.0)
+        message.append(jnp.sum(acc, axis=0, keepdims=True))
+    message += [load, energy]
+    rest = out_ref.shape[1] - len(message) - 4
+    for p in range(chunks):
+        first, second = plane_edges(inner, p, chunks // 2)
+        tail = [jnp.zeros((rest, LANES), jnp.float32)] if rest else []
+        out_ref[p] = jnp.concatenate(message + [first, second] + tail, axis=0)
+    crossing[...] = inner
+    state[...] = state_in[...]
+    state[DIR : DIR + TILE, :] = direction
+    state[INNER : INNER + TILE, :] = inner
+    state[SCAL : SCAL + TILE, :] = jnp.concatenate([gamma, load, carry, jnp.zeros((5, LANES), jnp.float32)], axis=0)
+
+
+def image_parts(arrived, state_in, crossed, nrows):
+    chunks = arrived.shape[0]
+    summed = arrived[0]
+    for p in range(1, chunks):
+        summed = summed + arrived[p]
+    energy = summed[nrows + 1 : nrows + 2, 0:1] + state_in[CARRY : CARRY + 1, 0:1]
+    partner, _ = plane_arrivals(arrived, nrows + 2, chunks // 2)
+    partner = with_crossing(partner, crossed[...])
+    load = jnp.concatenate([arrived[p, nrows : nrows + 1, :] for p in range(nrows)], axis=0)
+    return energy, partner, load, summed[0:nrows]
+
+
+def advance(parts, state_in, modes_ref, near_ref, r_ref, l_ref):
+    inner_energy, partner, load, solved = parts
+    energy = inner_energy + total(load * solved)
     alpha = state_in[GAMMA : GAMMA + 1, :] / energy
-    found = jnp.dot(r_ref[:, 0 : 2 * levels], solved, precision=HIGHEST)
+    found = jnp.dot(r_ref[:, 0 : solved.shape[0]], solved, precision=HIGHEST)
     corners = jnp.sum(found * l_ref[...], axis=1, keepdims=True)
     coarse = jnp.sum(corners[0:CORNERS] * modes_ref[...], axis=0, keepdims=True)
     near = []
@@ -366,30 +445,35 @@
         values = corners[CORNERS * (q + 1) : CORNERS * (q + 2)]
         near.append(jnp.sum(values * near_ref[:, SLOT * q : SLOT * (q + 1)], axis=0, keepdims=True))
     coarse = as_tile(coarse - jnp.concatenate(near, axis=1))
-    image = state_in[MASK : MASK + TILE, :] * (state_in[IFACE : IFACE + TILE, :] - partner + coarse)
+    image = state_in[MASK : MASK + TILE, :] * (state_in[INNER : INNER + TILE, :] - partner + coarse)
     multipliers = state_in[MUL : MUL + TILE, :] + alpha * state_in[DIR : DIR + TILE, :]
     residual = state_in[RES : RES + TILE, :] - alpha * image
     return multipliers, residual
 
 
 def next_kernel(
-    arrived, state_in, whole_load, modes_ref, near_ref, r_ref, l_ref, rt_ref, mask_row_ref, map_ref, map_tile_ref, schur_ref,
-    out_ref, state,
+    step, nrows, arrived, extra, state_in, modes_ref, near_ref, r_ref, l_ref, rt_ref, mask_row_ref, map_ref, map_tile_ref,
+    schur_ref, out_ref, state, crossing,
 ):
-    multipliers, residual = advance(arrived, state_in, whole_load, modes_ref, near_ref, r_ref, l_ref)
+    parts = image_parts(arrived, state_in, extra, nrows) if step else first_image_parts(arrived, state_in, extra)
+    multipliers, residual = advance(parts, state_in, modes_ref, near_ref, r_ref, l_ref)
     y = apply_schur(
-        residual, map_tile_ref[...], map_ref[...], mask_row_ref[...], schur_ref, modes_ref, near_ref, rt_ref, l_ref, out_ref
-    )
+        residual, map_tile_ref[...], map_ref[...], mask_row_ref[...], schur_ref, modes_ref, near_ref, rt_ref, l_ref, out_ref,
+        nrows,
+    )
+    crossing[...] = y
     state[...] = state_in[...]
     state[RES : RES + TILE, :] = residual
     state[MUL : MUL + TILE, :] = multipliers
     state[IFACE : IFACE + TILE, :] = y
+    state[ENERGY : ENERGY + 1, :] = jnp.broadcast_to(parts[0], (1, LANES))
 
 
 def last_kernel(
-    arrived, state_in, whole_load, modes_ref, near_ref, r_ref, l_ref, out_multipliers, out_residual, scratch, sems
+    nrows, arrived, crossed, state_in, modes_ref, near_ref, r_ref, l_ref, out_multipliers, out_residual, scratch, sems
 ):
-    results = advance(arrived, state_in, whole_load, modes_ref, near_ref, r_ref, l_ref)
+    parts = image_parts(arrived, state_in, crossed, nrows)
+    results = advance(parts, state_in, modes_ref, near_ref, r_ref, l_ref)
     width = scratch.shape[3]
     none = jnp.zeros((1, width - SLOT), jnp.float32)
     lanes = iota((1, width), 1)
@@ -450,43 +534,67 @@
     )
     square = (LANES, LANES)
     state_shape = (NSTATE, LANES)
+    ncoarse = coarse_inverse.shape[1]
+    nrows = -(-ncoarse // LANES)
+    to_plane, to_z = (chunks, TILE, LANES), (levels, 4, LANES)
+    to_plane_whole = (chunks, -(-(nrows + 6) // TILE) * TILE, LANES)
+    tile_shape = (TILE, LANES)
     out, state, near, r, rt, l, mask_row = call(
-        start_kernel,
+        functools.partial(start_kernel, nrows),
         (
             own, col_even, col_odd, row_pair, row_cross, cmap, map_row, map_tile, schur, own_modes, blocks,
         ),
         [(chunks, 2 * TILE, LANES), state_shape, (CORNERS, TILE * LANES), square, square, square, (1, TILE * LANES)],
         name="start",
     )
-    to_plane, to_z = (chunks, TILE, LANES), (levels, 4, LANES)
     for step in range(ITERS):
         arrived = lax.all_to_all(out, PLANE, 0, 0, tiled=True)
         if step == 0:
-            solver = arrived
-        out, state = call(rows_kernel, (arrived, state), [to_z, state_shape], name="rows")
-        arrived = lax.all_to_all(out, "z", 0, 0, tiled=True)
-
-        def kernel(*refs, step=step):
-            direction_kernel(step, *refs)
-
-        out, state = call(
-            kernel, (arrived, state, map_row, map_tile, kinv, solver), [to_plane, state_shape], name="direction"
-        )
-        arrived = lax.all_to_all(out, PLANE, 0, 0, tiled=True)
-        out, state, load = call(solve_kernel, (arrived, state), [to_z, state_shape, (chunks, LANES)], name="solve")
-        arrived = lax.all_to_all(out, "z", 0, 0, tiled=True)
-        common = (arrived, state, load, own_modes, near, r, l)
+            out, state, block = call(
+                rows_kernel,
+                (arrived, state),
+                [to_z, state_shape, (ncoarse // levels // TILE, TILE, LANES)],
+                name="rows",
+            )
+            columns = lax.all_gather(block, "z", axis=0, tiled=True)
+            arrived = lax.all_to_all(out, "z", 0, 0, tiled=True)
+            out, state = call(
+                first_direction_kernel,
+                (arrived, state, map_row, map_tile, kinv, block),
+                [to_plane, state_shape],
+                name="first_direction",
+            )
+            arrived = lax.all_to_all(out, PLANE, 0, 0, tiled=True)
+            out, state, extra = call(
+                first_solve_kernel, (arrived, state), [to_z, state_shape, (nrows, LANES)], name="first_solve"
+            )
+            arrived = lax.all_to_all(out, "z", 0, 0, tiled=True)
+        else:
+            crossed = swapped(crossing, ROWS_AXES, 1)
+            out, state = call(
+                inner_kernel, (arrived, crossed, state, map_row, map_tile, kinv), [to_z, state_shape], name="inner"
+            )
+            arrived = lax.all_to_all(out, "z", 0, 0, tiled=True)
+            out, state, crossing = call(
+                direction_kernel, (arrived, state, columns), [to_plane_whole, state_shape, tile_shape], name="direction"
+            )
+            extra = swapped(crossing, ROWS_AXES, 1)
+            arrived = lax.all_to_all(out, PLANE, 0, 0, tiled=True)
+        common = (arrived, extra, state, own_modes, near, r, l)
         if step + 1 < ITERS:
-            out, state = call(
-                next_kernel, common + (rt, mask_row, map_row, map_tile, schur), [to_plane, state_shape], name="next"
+            out, state, crossing = call(
+                functools.partial(next_kernel, step, nrows),
+                common + (rt, mask_row, map_row, map_tile, schur),
+                [to_plane, state_shape, tile_shape],
+                name="next",
             )
     return tuple(
         call(
-            last_kernel,
+            functools.partial(last_kernel, nrows),
             common,
             [gap.shape] * 2,
             out_specs=[HBM] * 2,
-            scratch=[pltpu.VMEM((2,) + gap.shape[:2] + gap.shape[2:], jnp.float32), pltpu.SemaphoreType.DMA((2,))],
+            scratch=[pltpu.VMEM((2,) + gap.shape, jnp.float32), pltpu.SemaphoreType.DMA((2,))],
             name="last",
         )
     )

time: 207 us -> 217 us (1.048)
  blocking collectives: 176 us -> 99.3 us
  waiting for transfers between devices: 1.02 us -> 37.5 us
  starting transfers between devices: 13.4 us -> 41.1 us
  between operations: 0.94 us -> 14.3 us
  local copies, waits for them, and re-layouts: 0.01 us -> 5.29 us
  Pallas kernels: 14.5 us -> 18.8 us
    all_to_all x6 -> x2, blocking collectives: 79 us -> 30.2 us  [on_device(): arrived = lax.all_to_all(out, PLANE, 0, 0, tiled=True)]
    all_to_all x0 -> x4, waiting for transfers between devices: none -> 36.4 us  [on_device(): arrived = lax.all_to_all(out, PLANE, 0, 0, tiled=True)]
    all_to_all x6 -> x4, blocking collectives: 97 us -> 69.1 us  [on_device(): arrived = lax.all_to_all(out, 'z', 0, 0, tiled=True)]
    all_to_all x0 -> x4, starting transfers between devices: none -> 24.8 us  [on_device(): arrived = lax.all_to_all(out, PLANE, 0, 0, tiled=True)]
    unnamed x2 -> x14, local copies, waits for them, and re-layouts: 0.01 us -> 5.29 us
    pallas_call x15 -> x13, Pallas kernels: 14.5 us -> 18.8 us  [call(): pl.pallas_call(kernel, out_shape=shapes, in_specs=in_specs or [VMEM] * le...]
    ppermute x4 -> x8, starting transfers between devices: 13.4 us -> 16.2 us  [swapped(): return lax.ppermute(block, axis, route)]
  transfers between devices with their start and end apart: 4 -> 13, of which waited for: 1 -> 5; matrix products, arithmetic and copies ran while one was open for 0% -> 0% of each run, Pallas kernels for 0% -> 3%
where the time goes in v5:
time: 217 us; the launch traced here: 216 us
  blocking collectives  99.3 us (46%)
  starting transfers between devices  41.1 us (19%)
  waiting for transfers between devices  37.5 us (17%)
  Pallas kernels  18.8 us (9%)
  between operations  14.3 us (7%)
  local copies, waits for them, and re-layouts  5.29 us (2%)
    all_to_all x4, blocking collectives, on_device(): arrived = lax.all_to_all(out, 'z', 0, 0, tiled=True)  69.1 us
    all_to_all x4, waiting for transfers between devices, on_device(): arrived = lax.all_to_all(out, PLANE, 0, 0, tiled=True)  36.4 us
    all_to_all x2, blocking collectives, on_device(): arrived = lax.all_to_all(out, PLANE, 0, 0, tiled=True)  30.2 us
    all_to_all x4, starting transfers between devices, on_device(): arrived = lax.all_to_all(out, PLANE, 0, 0, tiled=True)  24.8 us
    pallas_call x13, Pallas kernels, call(): pl.pallas_call(kernel, out_shape=shapes, in_specs=in_specs or [VMEM] * le...  18.8 us
    ppermute x8, starting transfers between devices, swapped(): return lax.ppermute(block, axis, route)  16.2 us
    unnamed x14, local copies, waits for them, and re-layouts  5.29 us
  transfers between devices with their start and end apart: 13, of which 5 were waited for; matrix products, arithmetic and copies ran while one was open for 0% of the time, Pallas kernels for 3%

profile of v5, /device:TPU:1, one launch (start us, length us, event | category | flops | bytes accessed | tf_op | source)
XLA Modules:
  0.0 216.3 jit_solution(4355810302727525557)
XLA Ops:
  7.2 0.0 all-gather.2.cloned.1.call-start
  7.2 1.8 pack.1
  9.0 0.0 copy-start
  9.1 8.9 %collective-permute-start = (f32[32,256]{1,0:T(8,128)S(1)}, f32[32,256]{1,0:T(8,128)S(1)}, u32[]{:S(2)}, u32[]{:S(2)}) collective-permute-start(f32[32,256]{1,0:T(8,128)S(1)} %get-tuple-element.44), channel_id=1, source_target_pairs={{0,1},{1,0},{2,3},{3,2},{4,5},{5,4},{6,7},{7,6},{8,9},{9,8},{10,11... | collective-permute-start | bytes 98312 | tf_op jit(solution)/shard_map/ppermute | solution.py:497
  18.0 1.9 collective-permute-start.1
  19.9 1.9 collective-permute-start.2
  21.8 0.7 collective-permute-start.3
  22.5 0.9 load.1.blocks_ref
  23.4 0.0 collective-permute-done.col_even
  23.5 0.0 collective-permute-done.1.col_odd
  23.5 1.1 collective-permute-done.2.row_pair
  24.6 0.0 collective-permute-done.3.row_cross
  24.6 1.8 start.1
  26.4 1.4 copy-done.1
  27.8 17.8 %all_to_all.50.arrived = f32[32,16,128]{2,1,0:T(8,128)S(1)} all-to-all(f32[32,16,128]{2,1,0:T(8,128)S(1)} %get-tuple-element.53), channel_id=1, replica_groups=mesh['z'=16,'xl'=2,'sy'=16] {'xl','sy'}, dimensions={0} | all-to-all | bytes 524288 | tf_op jit(solution)/shard_map/all_to_all | solution.py:551
  45.7 0.7 rows.1
  46.3 0.0 all-gather.2.cloned.1.call-update
  46.4 26.8 %all_to_all.51.arrived = f32[16,4,128]{2,1,0:T(4,128)S(1)} all-to-all(f32[16,4,128]{2,1,0:T(4,128)S(1)} %get-tuple-element.55), channel_id=1, replica_groups=mesh['z'=16,'xl'=2,'sy'=16] {'z'}, dimensions={0} | all-to-all | bytes 65536 | tf_op jit(solution)/shard_map/all_to_all | solution.py:560
  73.2 2.4 %first_direction.1 = (f32[32,8,128]{2,1,0:T(8,128)S(1)}, f32[64,128]{1,0:T(8,128)S(1)}) custom-call(f32[16,4,128]{2,1,0:T(4,128)S(1)} %all_to_all.51.arrived, f32[64,128]{1,0:T(8,128)S(1)} %get-tuple-element.56.state_in, s32[1,1024]{1,0:T(1,128)S(1)} %get-tuple-element.49.map_ref, s32[8,128]{1,0:T(8,128)S(1)} %get-tuple-element.50.map_tile_ref, ...), custom_call_target="tpu_custom_call" | custom-call | tf_op jit(solution)/shard_map/first_direction/pallas_call | solution.py:31
  75.6 12.4 %all_to_all.52.arrived = f32[32,8,128]{2,1,0:T(8,128)S(1)} all-to-all(f32[32,8,128]{2,1,0:T(8,128)S(1)} %get-tuple-element.58), channel_id=1, replica_groups=mesh['z'=16,'xl'=2,'sy'=16] {'xl','sy'}, dimensions={0} | all-to-all | bytes 262144 | tf_op jit(solution)/shard_map/all_to_all | solution.py:567
  88.0 0.1 first_solve.1
  88.0 14.1 %all_to_all.53.arrived = f32[16,4,128]{2,1,0:T(4,128)S(1)} all-to-all(f32[16,4,128]{2,1,0:T(4,128)S(1)} %get-tuple-element.60), channel_id=1, replica_groups=mesh['z'=16,'xl'=2,'sy'=16] {'z'}, dimensions={0} | all-to-all | bytes 65536 | tf_op jit(solution)/shard_map/all_to_all | solution.py:571
  102.2 2.7 %next.2 = (f32[32,8,128]{2,1,0:T(8,128)}, f32[64,128]{1,0:T(8,128)S(1)}, f32[8,128]{1,0:T(8,128)S(1)}) custom-call(f32[16,4,128]{2,1,0:T(4,128)S(1)} %all_to_all.53.arrived, f32[24,128]{1,0:T(8,128)S(1)} %get-tuple-element.61.extra, f32[64,128]{1,0:T(8,128)S(1)} %get-tuple-element.62.state_in, f32[24,1024]{1,0:T(8,128)S(1)} %get-tuple-element.52.modes_ref, ...), custom_call_target="tpu_custom_call" | custom-call | tf_op jit(solution)/shard_map/next/pallas_call | solution.py:31
  104.9 5.0 %all-to-all-start.4 = ((f32[32,8,128]{2,1,0:T(8,128)}), f32[32,8,128]{2,1,0:T(8,128)S(1)}, u32[]{:S(2)}, u32[]{:S(2)}) async-start(f32[32,8,128]{2,1,0:T(8,128)} %get-tuple-element.68), calls=%async_computation.4 | async-start | bytes 262144 | tf_op jit(solution)/shard_map/all_to_all | solution.py:551
  109.8 0.7 collective-permute-start.4
  110.5 7.1 %all-to-all-done.4.arrived = f32[32,8,128]{2,1,0:T(8,128)S(1)} async-done(((f32[32,8,128]{2,1,0:T(8,128)}), f32[32,8,128]{2,1,0:T(8,128)S(1)}, u32[]{:S(2)}, u32[]{:S(2)}) %all-to-all-start.4) | async-done | bytes 131104 | tf_op jit(solution)/shard_map/all_to_all | solution.py:551
  117.6 1.5 inner.2
  119.1 14.1 %all_to_all.54.arrived = f32[16,4,128]{2,1,0:T(4,128)S(1)} all-to-all(f32[16,4,128]{2,1,0:T(4,128)S(1)} %get-tuple-element.71), channel_id=1, replica_groups=mesh['z'=16,'xl'=2,'sy'=16] {'z'}, dimensions={0} | all-to-all | bytes 65536 | tf_op jit(solution)/shard_map/all_to_all | solution.py:577
  133.2 1.4 copy-done.4
  134.6 0.5 direction.2
  135.1 0.8 copy-done.6
  135.9 8.0 %all-to-all-start.6 = ((f32[32,32,128]{2,1,0:T(8,128)}), f32[32,32,128]{2,1,0:T(8,128)S(1)}, u32[]{:S(2)}, u32[]{:S(2)}) async-start(f32[32,32,128]{2,1,0:T(8,128)} %copy-done.6), calls=%async_computation.6 | async-start | bytes 1048576 | tf_op jit(solution)/shard_map/all_to_all | solution.py:582
  143.9 0.8 collective-permute-start.5
  144.8 0.0 collective-permute-done.5.extra
  144.8 11.0 %all-to-all-done.6.arrived = f32[32,32,128]{2,1,0:T(8,128)S(1)} async-done(((f32[32,32,128]{2,1,0:T(8,128)}), f32[32,32,128]{2,1,0:T(8,128)S(1)}, u32[]{:S(2)}, u32[]{:S(2)}) %all-to-all-start.6) | async-done | bytes 524320 | tf_op jit(solution)/shard_map/all_to_all | solution.py:582
  155.8 1.7 copy-done.3
  157.5 2.7 %next.3 = (f32[32,8,128]{2,1,0:T(8,128)}, f32[64,128]{1,0:T(8,128)S(1)}, f32[8,128]{1,0:T(8,128)S(1)}) custom-call(f32[32,32,128]{2,1,0:T(8,128)S(1)} %all-to-all-done.6.arrived, f32[8,128]{1,0:T(8,128)S(1)} %collective-permute-done.5.extra, f32[64,128]{1,0:T(8,128)S(1)} %get-tuple-element.75.state_in, f32[24,1024]{1,0:T(8,128)S(1)} %get-tuple-element.52.modes_ref, ...), custom_call_target="tpu_custom_call" | custom-call | tf_op jit(solution)/shard_map/next/pallas_call | solution.py:31
  160.1 3.6 %all-to-all-start.7 = ((f32[32,8,128]{2,1,0:T(8,128)}), f32[32,8,128]{2,1,0:T(8,128)S(1)}, u32[]{:S(2)}, u32[]{:S(2)}) async-start(f32[32,8,128]{2,1,0:T(8,128)} %get-tuple-element.76), calls=%async_computation.7 | async-start | bytes 262144 | tf_op jit(solution)/shard_map/all_to_all | solution.py:551
  163.8 0.7 collective-permute-start.6
  164.5 0.0 collective-permute-done.6.crossed
  164.5 7.1 %all-to-all-done.7.arrived = f32[32,8,128]{2,1,0:T(8,128)S(1)} async-done(((f32[32,8,128]{2,1,0:T(8,128)}), f32[32,8,128]{2,1,0:T(8,128)S(1)}, u32[]{:S(2)}, u32[]{:S(2)}) %all-to-all-start.7) | async-done | bytes 131104 | tf_op jit(solution)/shard_map/all_to_all | solution.py:551
  171.5 1.5 inner.3
  173.0 14.1 %all_to_all.55.arrived = f32[16,4,128]{2,1,0:T(4,128)S(1)} all-to-all(f32[16,4,128]{2,1,0:T(4,128)S(1)} %get-tuple-element.79), channel_id=1, replica_groups=mesh['z'=16,'xl'=2,'sy'=16] {'z'}, dimensions={0} | all-to-all | bytes 65536 | tf_op jit(solution)/shard_map/all_to_all | solution.py:577
  187.1 1.3 direction.3
  188.4 8.2 %all-to-all-start.9 = ((f32[32,32,128]{2,1,0:T(8,128)}), f32[32,32,128]{2,1,0:T(8,128)S(1)}, u32[]{:S(2)}, u32[]{:S(2)}) async-start(f32[32,32,128]{2,1,0:T(8,128)} %get-tuple-element.81), calls=%async_computation.9 | async-start | bytes 1048576 | tf_op jit(solution)/shard_map/all_to_all | solution.py:582
  196.6 0.7 collective-permute-start.7
  197.3 11.2 %all-to-all-done.9.arrived = f32[32,32,128]{2,1,0:T(8,128)S(1)} async-done(((f32[32,32,128]{2,1,0:T(8,128)}), f32[32,32,128]{2,1,0:T(8,128)S(1)}, u32[]{:S(2)}, u32[]{:S(2)}) %all-to-all-start.9) | async-done | bytes 524320 | tf_op jit(solution)/shard_map/all_to_all | solution.py:582
  208.5 1.0 last.1
  (12 shorter events, 0.0 us)
Async XLA Ops:
  7.2 126.0 %all-gather.2.cloned.1.call-start = ((), (), s32[]{:S(2)}) async-start(), calls=%async_computation.10 | async-start | bytes 1671168 | tf_op jit(solution)/shard_map/all_gather | solution.py:559
  9.0 64.1 %copy-start = (f32[1,1,768,768]{3,2,1,0:T(8,128)S(1)}, f32[1,1,768,768]{3,2,1,0:T(8,128)}, u32[]{:S(2)}) copy-start(f32[1,1,768,768]{3,2,1,0:T(8,128)} %param.9) | copy-start | bytes 7077892
  9.1 14.4 %collective-permute-start = (f32[32,256]{1,0:T(8,128)S(1)}, f32[32,256]{1,0:T(8,128)S(1)}, u32[]{:S(2)}, u32[]{:S(2)}) collective-permute-start(f32[32,256]{1,0:T(8,128)S(1)} %get-tuple-element.44), channel_id=1, source_target_pairs={{0,1},{1,0},{2,3},{3,2},{4,5},{5,4},{6,7},{7,6},{8,9},{9,8},{10,11... | collective-permute-start | bytes 98312 | tf_op jit(solution)/shard_map/ppermute | solution.py:497
  18.0 5.5 %collective-permute-start.1 = (f32[32,256]{1,0:T(8,128)S(1)}, f32[32,256]{1,0:T(8,128)S(1)}, u32[]{:S(2)}, u32[]{:S(2)}) collective-permute-start(f32[32,256]{1,0:T(8,128)S(1)} %get-tuple-element.45), channel_id=1, source_target_pairs={{1,2},{2,1},{3,4},{4,3},{5,6},{6,5},{7,8},{8,7},{9,10},{10,9},{11,... | collective-permute-start | bytes 98312 | tf_op jit(solution)/shard_map/ppermute | solution.py:497
  19.9 4.7 %collective-permute-start.2 = (f32[32,256]{1,0:T(8,128)S(1)}, f32[32,256]{1,0:T(8,128)S(1)}, u32[]{:S(2)}, u32[]{:S(2)}) collective-permute-start(f32[32,256]{1,0:T(8,128)S(1)} %get-tuple-element.46), channel_id=1, source_target_pairs={{0,16},{16,0},{32,48},{48,32},{64,80},{80,64},{96,112},{112,96},{1... | collective-permute-start | bytes 98312 | tf_op jit(solution)/shard_map/ppermute | solution.py:497
  21.8 2.7 %collective-permute-start.3 = (f32[32,256]{1,0:T(8,128)S(1)}, f32[32,256]{1,0:T(8,128)S(1)}, u32[]{:S(2)}, u32[]{:S(2)}) collective-permute-start(f32[32,256]{1,0:T(8,128)S(1)} %get-tuple-element.47), channel_id=1, source_target_pairs={{16,32},{32,16},{48,64},{64,48},{80,96},{96,80},{112,128},{128,112... | collective-permute-start | bytes 98312 | tf_op jit(solution)/shard_map/ppermute | solution.py:497
  26.4 1.4 copy-start.1
  46.4 55.8 %copy-start.2 = (f32[768,768]{1,0:T(8,128)S(1)}, f32[768,768]{1,0:T(8,128)}, u32[]{:S(2)}) copy-start(f32[768,768]{1,0:T(8,128)} %copy-done.1) | copy-start | bytes 7077892
  104.9 12.8 %all-to-all-start.4 = ((f32[32,8,128]{2,1,0:T(8,128)}), f32[32,8,128]{2,1,0:T(8,128)S(1)}, u32[]{:S(2)}, u32[]{:S(2)}) async-start(f32[32,8,128]{2,1,0:T(8,128)} %get-tuple-element.68), calls=%async_computation.4 | async-start | bytes 262144 | tf_op jit(solution)/shard_map/all_to_all | solution.py:551
  109.8 0.7 collective-permute-start.4
  133.2 1.4 copy-start.4
  135.1 0.8 copy-start.6
  135.9 19.9 %all-to-all-start.6 = ((f32[32,32,128]{2,1,0:T(8,128)}), f32[32,32,128]{2,1,0:T(8,128)S(1)}, u32[]{:S(2)}, u32[]{:S(2)}) async-start(f32[32,32,128]{2,1,0:T(8,128)} %copy-done.6), calls=%async_computation.6 | async-start | bytes 1048576 | tf_op jit(solution)/shard_map/all_to_all | solution.py:582
  143.9 0.9 collective-permute-start.5
  155.8 1.7 copy-start.3
  160.1 11.4 %all-to-all-start.7 = ((f32[32,8,128]{2,1,0:T(8,128)}), f32[32,8,128]{2,1,0:T(8,128)S(1)}, u32[]{:S(2)}, u32[]{:S(2)}) async-start(f32[32,8,128]{2,1,0:T(8,128)} %get-tuple-element.76), calls=%async_computation.7 | async-start | bytes 262144 | tf_op jit(solution)/shard_map/all_to_all | solution.py:551
  163.8 0.7 collective-permute-start.6
  171.5 15.5 %copy-start.5 = (f32[384,8,128]{2,1,0:T(8,128)S(1)}, f32[384,8,128]{2,1,0:T(8,128)}, u32[]{:S(2)}) copy-start(f32[384,8,128]{2,1,0:T(8,128)} %all-gather.2.cloned.1.call-done.columns_ref) | copy-start | bytes 4718596
  188.4 20.0 %all-to-all-start.9 = ((f32[32,32,128]{2,1,0:T(8,128)}), f32[32,32,128]{2,1,0:T(8,128)S(1)}, u32[]{:S(2)}, u32[]{:S(2)}) async-start(f32[32,32,128]{2,1,0:T(8,128)} %get-tuple-element.81), calls=%async_computation.9 | async-start | bytes 1048576 | tf_op jit(solution)/shard_map/all_to_all | solution.py:582
  196.6 0.7 collective-permute-start.7
Sparse Core Ops, SparseCore 0:
  46.5 64.9 all-gather.1

commit v6 on v4

--- a/solution.py
+++ b/solution.py
@@ -45,6 +45,10 @@
     return lax.broadcasted_iota(jnp.int32, shape, dim)
 
 
+def as_row(tile):
+    return jnp.concatenate([tile[c : c + 1, :] for c in range(TILE)], axis=1)
+
+
 def as_tile(row):
     return jnp.concatenate([row[:, LANES * c : LANES * (c + 1)] for c in range(TILE)], axis=0)
 
@@ -65,29 +69,39 @@
     return pieces
 
 
-def apply_matrix(tile, map_tile, map_row, matrix_ref):
+def bf16_parts(value):
+    first = value.astype(jnp.bfloat16).astype(jnp.float32)
+    left = value - first
+    second = left.astype(jnp.bfloat16).astype(jnp.float32)
+    return jnp.concatenate([first, second, left - second], axis=0)
+
+
+def apply_matrix(tile, group_row, hits, matrix_ref):
     width = matrix_ref.shape[0]
-    values = jnp.transpose(tile)
-    places = jnp.transpose(map_tile)
-    lanes = iota((LANES, LANES), 1)
-    pieces = []
-    for t in range(width // LANES):
-        acc = jnp.zeros((LANES, LANES), jnp.float32)
-        for c in range(TILE):
-            hit = places[:, c : c + 1] == lanes + t * LANES
-            acc = acc + jnp.where(hit, values[:, c : c + 1], 0.0)
-        pieces.append(jnp.sum(acc, axis=0, keepdims=True))
-    out = jnp.zeros((TILE, TILE * LANES), jnp.float32)
+    ours = group_row == iota((TILE, TILE * LANES), 0)
+    none = jnp.zeros((TILE, TILE * LANES), jnp.float32)
+    parts = bf16_parts(jnp.where(ours, as_row(tile), 0.0))
+    parts = jnp.concatenate([parts, none], axis=0).astype(jnp.bfloat16)
+    local = lax.dot_general(parts, hits, (((1,), (1,)), ((), ())), preferred_element_type=jnp.float32)
+    local = local[0:TILE] + local[TILE : 2 * TILE] + local[2 * TILE : 3 * TILE]
+    place = iota((TILE, LANES), 1) - iota((TILE, LANES), 0)
+    rows = []
     for b in range(width // LANES):
-        rows = slice(b * LANES, (b + 1) * LANES)
-        acc = matrix_ref[rows, 0:LANES] * pieces[0]
+        block = slice(b * LANES, (b + 1) * LANES)
+        acc = matrix_ref[block, 0:LANES] * local[0:1]
         for t in range(1, width // LANES):
-            acc = acc + matrix_ref[rows, t * LANES : (t + 1) * LANES] * pieces[t]
+            acc = acc + matrix_ref[block, t * LANES : (t + 1) * LANES] * local[t : t + 1]
         column = jnp.sum(acc, axis=1, keepdims=True)
-        for s in range(LANES // TILE):
-            index = iota((TILE, TILE * LANES), 0) + (b * LANES + s * TILE)
-            out = out + jnp.where(map_row == index, column[s * TILE : (s + 1) * TILE, :], 0.0)
-    return jnp.sum(out, axis=0, keepdims=True)
+        row = jnp.zeros((TILE, LANES), jnp.float32)
+        for k in range(LANES // TILE):
+            row = row + jnp.where(place == k * TILE, column[k * TILE : (k + 1) * TILE], 0.0)
+        rows.append(jnp.sum(row, axis=0, keepdims=True))
+    rows.append(jnp.zeros((TILE - len(rows), LANES), jnp.float32))
+    parts = bf16_parts(jnp.concatenate(rows, axis=0))
+    parts = jnp.concatenate([parts, jnp.zeros((TILE, LANES), jnp.float32)], axis=0).astype(jnp.bfloat16)
+    found = jnp.dot(parts, hits, preferred_element_type=jnp.float32)
+    found = found[0:TILE] + found[TILE : 2 * TILE] + found[2 * TILE : 3 * TILE]
+    return jnp.sum(jnp.where(ours, found, 0.0), axis=0, keepdims=True)
 
 
 def coarse_load(weighted, modes_ref, near_ref, rt_ref, l_ref, chunks):
@@ -143,9 +157,9 @@
     return jnp.concatenate([partner[0:2], south, partner[4:6], north], axis=0)
 
 
-def apply_schur(tile, map_tile, map_row, mask_row, schur_ref, modes_ref, near_ref, rt_ref, l_ref, out_ref):
+def apply_schur(tile, group_row, hits, mask_row, schur_ref, modes_ref, near_ref, rt_ref, l_ref, out_ref):
     chunks = out_ref.shape[0]
-    y_row = apply_matrix(tile, map_tile, map_row, schur_ref)
+    y_row = apply_matrix(tile, group_row, hits, schur_ref)
     load = coarse_load(0.25 * mask_row * y_row, modes_ref, near_ref, rt_ref, l_ref, chunks)
     y = as_tile(y_row)
     gamma = jnp.broadcast_to(0.25 * total(tile * y), (1, LANES))
@@ -158,7 +172,7 @@
 
 def pack_kernel(
     links_hbm, modes_hbm, map_hbm, gap_hbm, cmap_hbm, schur_hbm, out_modes, col_even, col_odd, row_pair, row_cross, out_own,
-    out_row, out_tile, out_cmap, out_schur, links_ref, modes_ref, map_ref, gap_ref, cmap_ref, sems,
+    out_group, out_hits, out_cmap, out_schur, links_ref, modes_ref, map_ref, gap_ref, cmap_ref, sems,
 ):
     copies = [
         pltpu.make_async_copy(source, target, sems.at[k])
@@ -178,22 +192,19 @@
     nrows, ncols = lax.axis_size("z") * lax.axis_size("xl"), lax.axis_size("sy")
     row_here = lax.axis_index("z") * lax.axis_size("xl") + lax.axis_index("xl")
     map_row = jnp.concatenate(slots(map_ref[0], 4, -1), axis=1)
-    out_row[...] = map_row
-    out_tile[...] = as_tile(map_row)
-    width = modes_ref.shape[3]
-    modes = jnp.concatenate([modes_ref[0, 0], jnp.zeros((8, width), jnp.float32)], axis=0)
-    first = modes.astype(jnp.bfloat16)
-    left = modes - first.astype(jnp.float32)
-    second = left.astype(jnp.bfloat16)
-    third = (left - second.astype(jnp.float32)).astype(jnp.bfloat16)
-    acc = jnp.zeros((CORNERS + 8, TILE * LANES), jnp.float32)
-    for b in range(width // LANES):
-        cols = slice(b * LANES, (b + 1) * LANES)
-        index = iota((LANES, TILE * LANES), 0) + b * LANES
-        hit = jnp.where(map_row == index, 1.0, 0.0).astype(jnp.bfloat16)
-        for part in (first, second, third):
-            acc = acc + jnp.dot(part[:, cols], hit, preferred_element_type=jnp.float32)
-    acc = acc[0:CORNERS]
+    group = lax.shift_right_arithmetic(map_row, 7)
+    out_group[...] = group
+    hits = jnp.where(map_row - LANES * group == iota((LANES, TILE * LANES), 0), 1.0, 0.0)
+    hits = jnp.where(group >= 0, hits, 0.0).astype(jnp.bfloat16)
+    out_hits[...] = hits
+    count = modes_ref.shape[3] // LANES
+    parts = [modes_ref[0, 0, :, t * LANES : (t + 1) * LANES] for t in range(count)]
+    parts = bf16_parts(jnp.concatenate(parts, axis=0)).astype(jnp.bfloat16)
+    found = jnp.dot(parts, hits, preferred_element_type=jnp.float32)
+    acc = jnp.zeros((CORNERS, TILE * LANES), jnp.float32)
+    for t in range(count):
+        pieces = [found[(count * k + t) * CORNERS : (count * k + t + 1) * CORNERS] for k in range(3)]
+        acc = acc + jnp.where(group == t, pieces[0] + pieces[1] + pieces[2], 0.0)
     out_modes[...] = acc
     links = jnp.where(links_ref[0] == 1, 1.0, 0.0)
     east = jnp.where(lax.axis_index("sy") < ncols - 1, links[:, 0:1], 0.0)
@@ -223,33 +234,21 @@
     matrix.wait()
 
 
-def load_kernel(coarse_hbm, blocks_out, coarse_ref, sem):
-    coarse = pltpu.make_async_copy(coarse_hbm, coarse_ref, sem)
-    coarse.start()
-    coarse.wait()
-    chunks = blocks_out.shape[0]
-    ncoarse = coarse_ref.shape[1]
-    block = ncoarse // chunks
-    padded = -(-ncoarse // LANES) * LANES
-    values = coarse_ref[...]
-    if padded > ncoarse:
-        values = jnp.pad(values, ((0, 0), (0, padded - ncoarse)))
-    values = jnp.concatenate([values, jnp.zeros((TILE - NDOF, padded), jnp.float32)], axis=0)
-    values = jnp.concatenate([values, jnp.zeros((TILE, LANES), jnp.float32)], axis=1)
-    lanes = iota((TILE, LANES), 1)
-    for p in range(chunks):
-        start = block * p // LANES * LANES
-        window = values[:, start : start + SLOT]
-        shift = block * p - start
-        if shift:
-            window = pltpu.roll(window, SLOT - shift, 1)
-        blocks_out[p] = jnp.where(lanes < block, window[:, 0:LANES], 0.0)
+def column_chunk(coarse, p, block):
+    start = block * p // LANES * LANES
+    window = coarse[:, start : start + SLOT]
+    shift = block * p - start
+    if shift:
+        window = pltpu.roll(window, SLOT - shift, 1)
+    return jnp.where(iota((TILE, LANES), 1) < block, window[:, 0:LANES], 0.0)
 
 
 def start_kernel(
-    own_ref, col_even, col_odd, row_pair, row_cross, cmap_ref, map_ref, map_tile_ref, schur_ref, modes_ref, blocks_ref, out_ref,
-    state, near, r_ref, rt_ref, l_ref, mask_row_ref,
+    own_ref, row_cross, col_odd, row_pair, col_even, cmap_ref, group_ref, hits_ref, schur_ref, modes_ref, coarse_hbm, out_ref,
+    state, near, r_ref, rt_ref, l_ref, mask_row_ref, coarse_ref, sem,
 ):
+    copy = pltpu.make_async_copy(coarse_hbm, coarse_ref, sem)
+    copy.start()
     chunks = out_ref.shape[0]
     block = NDOF * chunks // 2
     row, cm = CORNERS, CORNERS + 2
@@ -279,9 +278,14 @@
     r_ref[...] = hit_row
     rt_ref[...] = jnp.transpose(hit_row)
     l_ref[...] = jnp.where(inside == lanes, 1.0, 0.0)
-    y = apply_schur(residual, map_tile_ref[...], map_ref[...], mask_row, schur_ref, modes_ref, near, rt_ref, l_ref, out_ref)
+    y = apply_schur(residual, group_ref[...], hits_ref[...], mask_row, schur_ref, modes_ref, near, rt_ref, l_ref, out_ref)
+    copy.wait()
+    ncoarse = coarse_ref.shape[1]
+    wide = (-(-ncoarse // LANES) + 1) * LANES
+    coarse = jnp.concatenate([coarse_ref[...], jnp.zeros((TILE - NDOF, ncoarse), jnp.float32)], axis=0)
+    coarse = jnp.pad(coarse, ((0, 0), (0, wide - ncoarse)))
     for p in range(chunks):
-        out_ref[p, TILE : 2 * TILE, :] = blocks_ref[p]
+        out_ref[p, TILE : 2 * TILE, :] = column_chunk(coarse, p, block)
     state[...] = jnp.zeros(state.shape, jnp.float32)
     state[RES : RES + TILE, :] = residual
     state[IFACE : IFACE + TILE, :] = y
@@ -300,7 +304,7 @@
         out_ref[level] = jnp.concatenate([summed[0:2], z_edge(forward, level)], axis=0)
 
 
-def direction_kernel(step, arrived, state_in, map_ref, map_tile_ref, kinv_ref, blocks_ref, out_ref, state):
+def direction_kernel(step, arrived, state_in, group_ref, hits_ref, kinv_ref, blocks_ref, out_ref, state):
     chunks, levels = out_ref.shape[0], arrived.shape[0]
     half = chunks // 2
     summed = arrived[0]
@@ -314,7 +318,7 @@
         beta = gamma / state_in[GAMMA : GAMMA + 1, :]
         direction = direction + beta * state_in[DIR : DIR + TILE, :]
         load = load + beta * state_in[LOAD : LOAD + 1, :]
-    inner = as_tile(apply_matrix(direction, map_tile_ref[...], map_ref[...], kinv_ref))
+    inner = as_tile(apply_matrix(direction, group_ref[...], hits_ref[...], kinv_ref))
     energy = jnp.broadcast_to(total(direction * inner), (1, LANES))
     lanes = iota((TILE, LANES), 1)
     dof = iota((TILE, LANES), 0)
@@ -373,12 +377,12 @@
 
 
 def next_kernel(
-    arrived, state_in, whole_load, modes_ref, near_ref, r_ref, l_ref, rt_ref, mask_row_ref, map_ref, map_tile_ref, schur_ref,
+    arrived, state_in, whole_load, modes_ref, near_ref, r_ref, l_ref, rt_ref, mask_row_ref, group_ref, hits_ref, schur_ref,
     out_ref, state,
 ):
     multipliers, residual = advance(arrived, state_in, whole_load, modes_ref, near_ref, r_ref, l_ref)
     y = apply_schur(
-        residual, map_tile_ref[...], map_ref[...], mask_row_ref[...], schur_ref, modes_ref, near_ref, rt_ref, l_ref, out_ref
+        residual, group_ref[...], hits_ref[...], mask_row_ref[...], schur_ref, modes_ref, near_ref, rt_ref, l_ref, out_ref
     )
     state[...] = state_in[...]
     state[RES : RES + TILE, :] = residual
@@ -418,12 +422,13 @@
     width = kinv.shape[-1]
     kinv = kinv.reshape(width, width)
     ints = jnp.int32
-    own_modes, col_even, col_odd, row_pair, row_cross, own, map_row, map_tile, cmap, schur = call(
+    own_modes, col_even, col_odd, row_pair, row_cross, own, group, hits, cmap, schur = call(
         pack_kernel,
         in_hbm(links, corner_modes, edge_map, gap, corner_map, schur),
         [(CORNERS, TILE * LANES)]
         + [(CORNERS + 8, SLOT)] * 4
-        + [(TILE, SLOT), jax.ShapeDtypeStruct((1, TILE * LANES), ints), jax.ShapeDtypeStruct((TILE, LANES), ints)]
+        + [(TILE, SLOT), jax.ShapeDtypeStruct((1, TILE * LANES), ints)]
+        + [jax.ShapeDtypeStruct((LANES, TILE * LANES), jnp.bfloat16)]
         + [(1, SLOT), (width, width)],
         in_specs=[HBM] * 6,
         scratch=[
@@ -436,26 +441,21 @@
         ],
         name="pack",
     )
-    col_even = swapped(col_even, "sy", 0)
+    row_cross = swapped(row_cross, ROWS_AXES, 1)
     col_odd = swapped(col_odd, "sy", 1)
     row_pair = swapped(row_pair, ROWS_AXES, 0)
-    row_cross = swapped(row_cross, ROWS_AXES, 1)
-    (blocks,) = call(
-        load_kernel,
-        in_hbm(coarse_inverse),
-        [(chunks, TILE, LANES)],
-        in_specs=[HBM],
-        scratch=[pltpu.VMEM(coarse_inverse.shape, jnp.float32), pltpu.SemaphoreType.DMA(())],
-        name="load",
-    )
+    col_even = swapped(col_even, "sy", 0)
     square = (LANES, LANES)
     state_shape = (NSTATE, LANES)
     out, state, near, r, rt, l, mask_row = call(
         start_kernel,
         (
-            own, col_even, col_odd, row_pair, row_cross, cmap, map_row, map_tile, schur, own_modes, blocks,
+            own, row_cross, col_odd, row_pair, col_even, cmap, group, hits, schur, own_modes,
+            *in_hbm(coarse_inverse),
         ),
         [(chunks, 2 * TILE, LANES), state_shape, (CORNERS, TILE * LANES), square, square, square, (1, TILE * LANES)],
+        in_specs=[VMEM] * 10 + [HBM],
+        scratch=[pltpu.VMEM(coarse_inverse.shape, jnp.float32), pltpu.SemaphoreType.DMA(())],
         name="start",
     )
     to_plane, to_z = (chunks, TILE, LANES), (levels, 4, LANES)
@@ -470,7 +470,7 @@
             direction_kernel(step, *refs)
 
         out, state = call(
-            kernel, (arrived, state, map_row, map_tile, kinv, solver), [to_plane, state_shape], name="direction"
+            kernel, (arrived, state, group, hits, kinv, solver), [to_plane, state_shape], name="direction"
         )
         arrived = lax.all_to_all(out, PLANE, 0, 0, tiled=True)
         out, state, load = call(solve_kernel, (arrived, state), [to_z, state_shape, (chunks, LANES)], name="solve")
@@ -478,7 +478,7 @@
         common = (arrived, state, load, own_modes, near, r, l)
         if step + 1 < ITERS:
             out, state = call(
-                next_kernel, common + (rt, mask_row, map_row, map_tile, schur), [to_plane, state_shape], name="next"
+                next_kernel, common + (rt, mask_row, group, hits, schur), [to_plane, state_shape], name="next"
             )
     return tuple(
         call(

time: 207 us -> 198 us (0.957)
  Pallas kernels: 14.5 us -> 9.29 us
  blocking collectives: 176 us -> 172 us
    pallas_call x15 -> x14, Pallas kernels: 14.5 us -> 9.29 us  [call(): pl.pallas_call(kernel, out_shape=shapes, in_specs=in_specs or [VMEM] * le...]
    all_to_all x6, blocking collectives: 79 us -> 76.8 us  [on_device(): arrived = lax.all_to_all(out, PLANE, 0, 0, tiled=True)]
where the time goes in v6:
time: 198 us; the launch traced here: 197 us
  blocking collectives  172 us (87%)
  starting transfers between devices  13.6 us (7%)
  Pallas kernels  9.29 us (5%)
    all_to_all x6, blocking collectives, on_device(): arrived = lax.all_to_all(out, 'z', 0, 0, tiled=True)  95.7 us
    all_to_all x6, blocking collectives, on_device(): arrived = lax.all_to_all(out, PLANE, 0, 0, tiled=True)  76.8 us
    ppermute x4, starting transfers between devices, swapped(): return lax.ppermute(block, axis, route)  13.6 us
    pallas_call x14, Pallas kernels, call(): pl.pallas_call(kernel, out_shape=shapes, in_specs=in_specs or [VMEM] * le...  9.29 us
  transfers between devices with their start and end apart: 4, of which 1 were waited for; matrix products, arithmetic and copies ran while one was open for 0% of the time, Pallas kernels for 0%

profile of v6, /device:TPU:1, one launch (start us, length us, event | category | flops | bytes accessed | tf_op | source)
XLA Modules:
  0.0 197.3 jit_solution(13511753433638663029)
XLA Ops:
  0.6 1.8 pack.1
  2.5 0.0 copy-start
  2.5 0.8 collective-permute-start
  3.3 4.6 %collective-permute-start.1 = (f32[32,256]{1,0:T(8,128)S(1)}, f32[32,256]{1,0:T(8,128)S(1)}, u32[]{:S(2)}, u32[]{:S(2)}) collective-permute-start(f32[32,256]{1,0:T(8,128)S(1)} %get-tuple-element.46), channel_id=1, source_target_pairs={{1,2},{2,1},{3,4},{4,3},{5,6},{6,5},{7,8},{8,7},{9,10},{10,9},{11,... | collective-permute-start | bytes 98312 | tf_op jit(solution)/shard_map/ppermute | solution.py:417
  7.9 6.3 %collective-permute-start.2 = (f32[32,256]{1,0:T(8,128)S(1)}, f32[32,256]{1,0:T(8,128)S(1)}, u32[]{:S(2)}, u32[]{:S(2)}) collective-permute-start(f32[32,256]{1,0:T(8,128)S(1)} %get-tuple-element.47), channel_id=1, source_target_pairs={{0,16},{16,0},{32,48},{48,32},{64,80},{80,64},{96,112},{112,96},{1... | collective-permute-start | bytes 98312 | tf_op jit(solution)/shard_map/ppermute | solution.py:417
  14.1 1.9 collective-permute-start.3
  16.1 0.0 collective-permute-done.row_cross
  16.1 0.0 collective-permute-done.1.col_odd
  16.1 0.0 collective-permute-done.2.row_pair
  16.1 1.1 collective-permute-done.3.col_even
  17.2 1.3 start.1
  18.5 15.8 %all_to_all.60.arrived.refs_5_ = f32[32,16,128]{2,1,0:T(8,128)S(1)} all-to-all(f32[32,16,128]{2,1,0:T(8,128)S(1)} %get-tuple-element.54), channel_id=1, replica_groups=mesh['z'=16,'xl'=2,'sy'=16] {'xl','sy'}, dimensions={0} | all-to-all | bytes 524288 | tf_op jit(solution)/shard_map/all_to_all | solution.py:463
  34.4 25.3 %all_to_all.61.refs_0_ = f32[16,4,128]{2,1,0:T(4,128)S(1)} all-to-all(f32[16,4,128]{2,1,0:T(4,128)S(1)} %get-tuple-element.56), channel_id=1, replica_groups=mesh['z'=16,'xl'=2,'sy'=16] {'z'}, dimensions={0} | all-to-all | bytes 65536 | tf_op jit(solution)/shard_map/all_to_all | solution.py:467
  59.7 0.0 copy-done
  59.7 0.8 direction.3
  60.5 12.3 %all_to_all.62.arrived = f32[32,8,128]{2,1,0:T(8,128)S(1)} all-to-all(f32[32,8,128]{2,1,0:T(8,128)S(1)} %get-tuple-element.58), channel_id=1, replica_groups=mesh['z'=16,'xl'=2,'sy'=16] {'xl','sy'}, dimensions={0} | all-to-all | bytes 262144 | tf_op jit(solution)/shard_map/all_to_all | solution.py:475
  72.9 14.1 %all_to_all.63.arrived = f32[16,4,128]{2,1,0:T(4,128)S(1)} all-to-all(f32[16,4,128]{2,1,0:T(4,128)S(1)} %get-tuple-element.60), channel_id=1, replica_groups=mesh['z'=16,'xl'=2,'sy'=16] {'z'}, dimensions={0} | all-to-all | bytes 65536 | tf_op jit(solution)/shard_map/all_to_all | solution.py:477
  86.9 1.3 next.2
  88.3 12.2 %all_to_all.64.arrived = f32[32,8,128]{2,1,0:T(8,128)S(1)} all-to-all(f32[32,8,128]{2,1,0:T(8,128)S(1)} %get-tuple-element.68), channel_id=1, replica_groups=mesh['z'=16,'xl'=2,'sy'=16] {'xl','sy'}, dimensions={0} | all-to-all | bytes 262144 | tf_op jit(solution)/shard_map/all_to_all | solution.py:463
  100.5 14.1 %all_to_all.65.refs_0_ = f32[16,4,128]{2,1,0:T(4,128)S(1)} all-to-all(f32[16,4,128]{2,1,0:T(4,128)S(1)} %get-tuple-element.70), channel_id=1, replica_groups=mesh['z'=16,'xl'=2,'sy'=16] {'z'}, dimensions={0} | all-to-all | bytes 65536 | tf_op jit(solution)/shard_map/all_to_all | solution.py:467
  114.6 0.8 direction.4
  115.3 12.2 %all_to_all.66.arrived = f32[32,8,128]{2,1,0:T(8,128)S(1)} all-to-all(f32[32,8,128]{2,1,0:T(8,128)S(1)} %get-tuple-element.72), channel_id=1, replica_groups=mesh['z'=16,'xl'=2,'sy'=16] {'xl','sy'}, dimensions={0} | all-to-all | bytes 262144 | tf_op jit(solution)/shard_map/all_to_all | solution.py:475
  127.5 14.1 %all_to_all.67.arrived = f32[16,4,128]{2,1,0:T(4,128)S(1)} all-to-all(f32[16,4,128]{2,1,0:T(4,128)S(1)} %get-tuple-element.74), channel_id=1, replica_groups=mesh['z'=16,'xl'=2,'sy'=16] {'z'}, dimensions={0} | all-to-all | bytes 65536 | tf_op jit(solution)/shard_map/all_to_all | solution.py:477
  141.6 1.4 next.3
  143.0 12.2 %all_to_all.68.arrived = f32[32,8,128]{2,1,0:T(8,128)S(1)} all-to-all(f32[32,8,128]{2,1,0:T(8,128)S(1)} %get-tuple-element.77), channel_id=1, replica_groups=mesh['z'=16,'xl'=2,'sy'=16] {'xl','sy'}, dimensions={0} | all-to-all | bytes 262144 | tf_op jit(solution)/shard_map/all_to_all | solution.py:463
  155.2 14.1 %all_to_all.69.refs_0_ = f32[16,4,128]{2,1,0:T(4,128)S(1)} all-to-all(f32[16,4,128]{2,1,0:T(4,128)S(1)} %get-tuple-element.79), channel_id=1, replica_groups=mesh['z'=16,'xl'=2,'sy'=16] {'z'}, dimensions={0} | all-to-all | bytes 65536 | tf_op jit(solution)/shard_map/all_to_all | solution.py:467
  169.3 0.8 direction.5
  170.0 12.2 %all_to_all.70.arrived = f32[32,8,128]{2,1,0:T(8,128)S(1)} all-to-all(f32[32,8,128]{2,1,0:T(8,128)S(1)} %get-tuple-element.81), channel_id=1, replica_groups=mesh['z'=16,'xl'=2,'sy'=16] {'xl','sy'}, dimensions={0} | all-to-all | bytes 262144 | tf_op jit(solution)/shard_map/all_to_all | solution.py:475
  182.2 14.1 %all_to_all.71.arrived = f32[16,4,128]{2,1,0:T(4,128)S(1)} all-to-all(f32[16,4,128]{2,1,0:T(4,128)S(1)} %get-tuple-element.83), channel_id=1, replica_groups=mesh['z'=16,'xl'=2,'sy'=16] {'z'}, dimensions={0} | all-to-all | bytes 65536 | tf_op jit(solution)/shard_map/all_to_all | solution.py:477
  196.3 0.9 last.1
  (6 shorter events, 0.3 us)
Async XLA Ops:
  2.5 57.2 %copy-start = (f32[1,1,768,768]{3,2,1,0:T(8,128)S(1)}, f32[1,1,768,768]{3,2,1,0:T(8,128)}, u32[]{:S(2)}) copy-start(f32[1,1,768,768]{3,2,1,0:T(8,128)} %param.9) | copy-start | bytes 7077892
  2.5 13.6 %collective-permute-start = (f32[32,256]{1,0:T(8,128)S(1)}, f32[32,256]{1,0:T(8,128)S(1)}, u32[]{:S(2)}, u32[]{:S(2)}) collective-permute-start(f32[32,256]{1,0:T(8,128)S(1)} %get-tuple-element.45), channel_id=1, source_target_pairs={{16,32},{32,16},{48,64},{64,48},{80,96},{96,80},{112,128},{128,112... | collective-permute-start | bytes 98312 | tf_op jit(solution)/shard_map/ppermute | solution.py:417
  3.3 12.8 %collective-permute-start.1 = (f32[32,256]{1,0:T(8,128)S(1)}, f32[32,256]{1,0:T(8,128)S(1)}, u32[]{:S(2)}, u32[]{:S(2)}) collective-permute-start(f32[32,256]{1,0:T(8,128)S(1)} %get-tuple-element.46), channel_id=1, source_target_pairs={{1,2},{2,1},{3,4},{4,3},{5,6},{6,5},{7,8},{8,7},{9,10},{10,9},{11,... | collective-permute-start | bytes 98312 | tf_op jit(solution)/shard_map/ppermute | solution.py:417
  7.9 8.2 %collective-permute-start.2 = (f32[32,256]{1,0:T(8,128)S(1)}, f32[32,256]{1,0:T(8,128)S(1)}, u32[]{:S(2)}, u32[]{:S(2)}) collective-permute-start(f32[32,256]{1,0:T(8,128)S(1)} %get-tuple-element.47), channel_id=1, source_target_pairs={{0,16},{16,0},{32,48},{48,32},{64,80},{80,64},{96,112},{112,96},{1... | collective-permute-start | bytes 98312 | tf_op jit(solution)/shard_map/ppermute | solution.py:417
  14.1 3.1 %collective-permute-start.3 = (f32[32,256]{1,0:T(8,128)S(1)}, f32[32,256]{1,0:T(8,128)S(1)}, u32[]{:S(2)}, u32[]{:S(2)}) collective-permute-start(f32[32,256]{1,0:T(8,128)S(1)} %get-tuple-element.48), channel_id=1, source_target_pairs={{0,1},{1,0},{2,3},{3,2},{4,5},{5,4},{6,7},{7,6},{8,9},{9,8},{10,11... | collective-permute-start | bytes 98312 | tf_op jit(solution)/shard_map/ppermute | solution.py:417

commit v7 on v6

--- a/solution.py
+++ b/solution.py
@@ -12,7 +12,6 @@
 TILE = 8
 CORNERS = 24
 NDOF = 6
-HIGHEST = lax.Precision.HIGHEST
 VMEM = pl.BlockSpec(memory_space=pltpu.VMEM)
 HBM = pl.BlockSpec(memory_space=pl.ANY)
 LIMIT = 40 * 1024 * 1024
@@ -69,11 +68,17 @@
     return pieces
 
 
-def bf16_parts(value):
+def bf16_parts(value, axis=0):
     first = value.astype(jnp.bfloat16).astype(jnp.float32)
     left = value - first
     second = left.astype(jnp.bfloat16).astype(jnp.float32)
-    return jnp.concatenate([first, second, left - second], axis=0)
+    return jnp.concatenate([first, second, left - second], axis=axis)
+
+
+def one_hot_product(hits, values):
+    parts = bf16_parts(values, axis=1).astype(jnp.bfloat16)
+    found = jnp.dot(hits, parts, preferred_element_type=jnp.float32)
+    return found[:, 0:LANES] + found[:, LANES : 2 * LANES] + found[:, 2 * LANES : 3 * LANES]
 
 
 def apply_matrix(tile, group_row, hits, matrix_ref):
@@ -112,7 +117,7 @@
         loads.append(-jnp.sum(near[:, SLOT * q : SLOT * (q + 1)], axis=1, keepdims=True))
     loads.append(jnp.zeros((LANES - 5 * CORNERS, 1), jnp.float32))
     column = jnp.concatenate(loads, axis=0)
-    return jnp.dot(rt_ref[0:chunks, :], column * l_ref[...], precision=HIGHEST)
+    return one_hot_product(rt_ref[0:chunks, :], column * l_ref[...])
 
 
 def plane_edges(tile, target, ncols):
@@ -128,14 +133,22 @@
     return first, second
 
 
-def plane_arrivals(arrived, row, ncols):
+def plane_arrivals(arrived, row, ncols, dense=False):
     pair, here = lax.axis_index("xl"), lax.axis_index("sy")
     base = pair * ncols
     east = arrived[base + jnp.minimum(here + 1, ncols - 1), row : row + 2, :]
     west = arrived[base + jnp.maximum(here - 1, 0), row : row + 2, :]
     other = (1 - pair) * ncols + here
-    their_south = arrived[other, row : row + 2, :]
-    their_north = arrived[other, row + 2 : row + 4, :]
+    if dense:
+        both = arrived[other, row : row + 3, :]
+        moved = pltpu.roll(jnp.concatenate([both, jnp.zeros((TILE - 3, LANES), jnp.float32)], axis=0), LANES // 2, 1)
+        low = iota((1, LANES), 1) < LANES // 2
+        their_south = jnp.concatenate([both[0:1], jnp.where(low, both[1:2], 0.0)], axis=0)
+        first = jnp.where(low, moved[1:2], moved[2:3])
+        their_north = jnp.concatenate([first, jnp.where(low, moved[2:3], 0.0)], axis=0)
+    else:
+        their_south = arrived[other, row : row + 2, :]
+        their_north = arrived[other, row + 2 : row + 4, :]
     south = jnp.where(pair == 0, their_north, 0.0)
     north = jnp.where(pair == 0, 0.0, their_south)
     forward = jnp.where(pair == 0, their_south, their_north)
@@ -163,10 +176,27 @@
     load = coarse_load(0.25 * mask_row * y_row, modes_ref, near_ref, rt_ref, l_ref, chunks)
     y = as_tile(y_row)
     gamma = jnp.broadcast_to(0.25 * total(tile * y), (1, LANES))
-    rest = jnp.zeros((2, LANES), jnp.float32)
+    if out_ref.shape[1] > TILE:
+        rest = jnp.zeros((2, LANES), jnp.float32)
+        for p in range(chunks):
+            first, second = plane_edges(y, p, chunks // 2)
+            out_ref[p, 0:TILE, :] = jnp.concatenate([load[p : p + 1], gamma, first, second, rest], axis=0)
+        return y
+    heads = jnp.where(iota((chunks, LANES), 1) < NDOF * chunks // 2, load, gamma)
+    pair, here, ncols = lax.axis_index("xl"), lax.axis_index("sy"), chunks // 2
+    none = jnp.zeros((1, LANES), jnp.float32)
+    east = jnp.concatenate([y[0:2], none], axis=0)
+    west = jnp.concatenate([y[4:6], none], axis=0)
+    moved = pltpu.roll(y, LANES // 2, 1)
+    low = iota((1, LANES), 1) < LANES // 2
+    middle = jnp.where(low, y[3:4], moved[6:7])
+    both = jnp.concatenate([y[2:3], middle, jnp.where(low, moved[6:7], moved[7:8])], axis=0)
+    to_east = jnp.where(here + 1 < ncols, pair * ncols + here + 1, -1)
+    to_west = jnp.where(here > 0, pair * ncols + here - 1, -1)
+    to_pair = (1 - pair) * ncols + here
     for p in range(chunks):
-        first, second = plane_edges(y, p, chunks // 2)
-        out_ref[p, 0:TILE, :] = jnp.concatenate([load[p : p + 1], gamma, first, second, rest], axis=0)
+        edges = jnp.where(to_east == p, east, jnp.where(to_west == p, west, jnp.where(to_pair == p, both, 0.0)))
+        out_ref[p] = jnp.concatenate([heads[p : p + 1], edges], axis=0)
     return y
 
 
@@ -275,8 +305,8 @@
     inside = column - group * block
     lanes = iota((LANES, LANES), 1).astype(jnp.float32)
     hit_row = jnp.where((group == lanes) & (lanes < chunks), 1.0, 0.0)
-    r_ref[...] = hit_row
-    rt_ref[...] = jnp.transpose(hit_row)
+    r_ref[...] = hit_row.astype(jnp.bfloat16)
+    rt_ref[...] = jnp.transpose(hit_row).astype(jnp.bfloat16)
     l_ref[...] = jnp.where(inside == lanes, 1.0, 0.0)
     y = apply_schur(residual, group_ref[...], hits_ref[...], mask_row, schur_ref, modes_ref, near, rt_ref, l_ref, out_ref)
     copy.wait()
@@ -294,14 +324,19 @@
 
 def rows_kernel(arrived, state_in, out_ref, state):
     chunks, levels = arrived.shape[0], out_ref.shape[0]
-    summed = arrived[0, 0:TILE, :]
+    dense = arrived.shape[1] < TILE
+    summed = arrived[0, 0:4, :]
     for p in range(1, chunks):
-        summed = summed + arrived[p, 0:TILE, :]
-    partner, forward = plane_arrivals(arrived, 2, chunks // 2)
+        summed = summed + arrived[p, 0:4, :]
+    load, gamma = summed[0:1], summed[1:2]
+    if dense:
+        gamma = jnp.broadcast_to(load[:, LANES - 1 : LANES], (1, LANES))
+        load = jnp.where(iota((1, LANES), 1) < NDOF * chunks // 2, load, 0.0)
+    partner, forward = plane_arrivals(arrived, 1 if dense else 2, chunks // 2, dense)
     state[...] = state_in[...]
     state[PARTNER : PARTNER + TILE, :] = partner
     for level in range(levels):
-        out_ref[level] = jnp.concatenate([summed[0:2], z_edge(forward, level)], axis=0)
+        out_ref[level] = jnp.concatenate([load, gamma, z_edge(forward, level)], axis=0)
 
 
 def direction_kernel(step, arrived, state_in, group_ref, hits_ref, kinv_ref, blocks_ref, out_ref, state):
@@ -362,7 +397,7 @@
     solved = jnp.concatenate([arrived[level, 0:2, :] for level in range(levels)], axis=0)
     energy = energy[:, LANES - 1 : LANES] + total(whole_load[...] * solved)
     alpha = state_in[GAMMA : GAMMA + 1, :] / energy
-    found = jnp.dot(r_ref[:, 0 : 2 * levels], solved, precision=HIGHEST)
+    found = one_hot_product(r_ref[:, 0 : 2 * levels], solved)
     corners = jnp.sum(found * l_ref[...], axis=1, keepdims=True)
     coarse = jnp.sum(corners[0:CORNERS] * modes_ref[...], axis=0, keepdims=True)
     near = []
@@ -445,7 +480,7 @@
     col_odd = swapped(col_odd, "sy", 1)
     row_pair = swapped(row_pair, ROWS_AXES, 0)
     col_even = swapped(col_even, "sy", 0)
-    square = (LANES, LANES)
+    hits_shape = jax.ShapeDtypeStruct((LANES, LANES), jnp.bfloat16)
     state_shape = (NSTATE, LANES)
     out, state, near, r, rt, l, mask_row = call(
         start_kernel,
@@ -453,12 +488,13 @@
             own, row_cross, col_odd, row_pair, col_even, cmap, group, hits, schur, own_modes,
             *in_hbm(coarse_inverse),
         ),
-        [(chunks, 2 * TILE, LANES), state_shape, (CORNERS, TILE * LANES), square, square, square, (1, TILE * LANES)],
+        [(chunks, 2 * TILE, LANES), state_shape, (CORNERS, TILE * LANES), hits_shape, hits_shape]
+        + [(LANES, LANES), (1, TILE * LANES)],
         in_specs=[VMEM] * 10 + [HBM],
         scratch=[pltpu.VMEM(coarse_inverse.shape, jnp.float32), pltpu.SemaphoreType.DMA(())],
         name="start",
     )
-    to_plane, to_z = (chunks, TILE, LANES), (levels, 4, LANES)
+    to_plane, to_plane_short, to_z = (chunks, TILE, LANES), (chunks, 4, LANES), (levels, 4, LANES)
     for step in range(ITERS):
         arrived = lax.all_to_all(out, PLANE, 0, 0, tiled=True)
         if step == 0:
@@ -478,7 +514,7 @@
         common = (arrived, state, load, own_modes, near, r, l)
         if step + 1 < ITERS:
             out, state = call(
-                next_kernel, common + (rt, mask_row, group, hits, schur), [to_plane, state_shape], name="next"
+                next_kernel, common + (rt, mask_row, group, hits, schur), [to_plane_short, state_shape], name="next"
             )
     return tuple(
         call(

time: 198 us -> 197 us (level)
  no operation moved by 1% of the time
where the time goes in v7:
time: 197 us; the launch traced here: 196 us
  blocking collectives  172 us (87%)
  starting transfers between devices  13.6 us (7%)
  Pallas kernels  9.2 us (5%)
    all_to_all x6, blocking collectives, on_device(): arrived = lax.all_to_all(out, 'z', 0, 0, tiled=True)  95.7 us
    all_to_all x6, blocking collectives, on_device(): arrived = lax.all_to_all(out, PLANE, 0, 0, tiled=True)  76 us
    ppermute x4, starting transfers between devices, swapped(): return lax.ppermute(block, axis, route)  13.6 us
    pallas_call x14, Pallas kernels, call(): pl.pallas_call(kernel, out_shape=shapes, in_specs=in_specs or [VMEM] * le...  9.2 us
  transfers between devices with their start and end apart: 4, of which 1 were waited for; matrix products, arithmetic and copies ran while one was open for 0% of the time, Pallas kernels for 0%

profile of v7, /device:TPU:1, one launch (start us, length us, event | category | flops | bytes accessed | tf_op | source)
XLA Modules:
  0.0 196.4 jit_solution(7509256647680369204)
XLA Ops:
  0.6 1.8 pack.1
  2.5 0.0 copy-start
  2.5 0.8 collective-permute-start
  3.3 4.6 %collective-permute-start.1 = (f32[32,256]{1,0:T(8,128)S(1)}, f32[32,256]{1,0:T(8,128)S(1)}, u32[]{:S(2)}, u32[]{:S(2)}) collective-permute-start(f32[32,256]{1,0:T(8,128)S(1)} %get-tuple-element.46), channel_id=1, source_target_pairs={{1,2},{2,1},{3,4},{4,3},{5,6},{6,5},{7,8},{8,7},{9,10},{10,9},{11,... | collective-permute-start | bytes 98312 | tf_op jit(solution)/shard_map/ppermute | solution.py:452
  7.9 6.3 %collective-permute-start.2 = (f32[32,256]{1,0:T(8,128)S(1)}, f32[32,256]{1,0:T(8,128)S(1)}, u32[]{:S(2)}, u32[]{:S(2)}) collective-permute-start(f32[32,256]{1,0:T(8,128)S(1)} %get-tuple-element.47), channel_id=1, source_target_pairs={{0,16},{16,0},{32,48},{48,32},{64,80},{80,64},{96,112},{112,96},{1... | collective-permute-start | bytes 98312 | tf_op jit(solution)/shard_map/ppermute | solution.py:452
  14.1 1.9 collective-permute-start.3
  16.1 0.0 collective-permute-done.row_cross
  16.1 0.0 collective-permute-done.1.col_odd
  16.1 0.0 collective-permute-done.2.row_pair
  16.1 1.1 collective-permute-done.3.col_even
  17.2 1.2 start.1
  18.4 15.8 %all_to_all.60.arrived.refs_5_ = f32[32,16,128]{2,1,0:T(8,128)S(1)} all-to-all(f32[32,16,128]{2,1,0:T(8,128)S(1)} %get-tuple-element.54), channel_id=1, replica_groups=mesh['z'=16,'xl'=2,'sy'=16] {'xl','sy'}, dimensions={0} | all-to-all | bytes 524288 | tf_op jit(solution)/shard_map/all_to_all | solution.py:499
  34.3 25.3 %all_to_all.61.refs_0_ = f32[16,4,128]{2,1,0:T(4,128)S(1)} all-to-all(f32[16,4,128]{2,1,0:T(4,128)S(1)} %get-tuple-element.56), channel_id=1, replica_groups=mesh['z'=16,'xl'=2,'sy'=16] {'z'}, dimensions={0} | all-to-all | bytes 65536 | tf_op jit(solution)/shard_map/all_to_all | solution.py:503
  59.6 0.0 copy-done
  59.6 0.8 direction.3
  60.4 12.3 %all_to_all.62.arrived = f32[32,8,128]{2,1,0:T(8,128)S(1)} all-to-all(f32[32,8,128]{2,1,0:T(8,128)S(1)} %get-tuple-element.58), channel_id=1, replica_groups=mesh['z'=16,'xl'=2,'sy'=16] {'xl','sy'}, dimensions={0} | all-to-all | bytes 262144 | tf_op jit(solution)/shard_map/all_to_all | solution.py:511
  72.8 14.1 %all_to_all.63.arrived = f32[16,4,128]{2,1,0:T(4,128)S(1)} all-to-all(f32[16,4,128]{2,1,0:T(4,128)S(1)} %get-tuple-element.60), channel_id=1, replica_groups=mesh['z'=16,'xl'=2,'sy'=16] {'z'}, dimensions={0} | all-to-all | bytes 65536 | tf_op jit(solution)/shard_map/all_to_all | solution.py:513
  86.8 1.3 next.2
  88.1 11.8 %all_to_all.64.arrived = f32[32,4,128]{2,1,0:T(4,128)S(1)} all-to-all(f32[32,4,128]{2,1,0:T(4,128)S(1)} %get-tuple-element.68), channel_id=1, replica_groups=mesh['z'=16,'xl'=2,'sy'=16] {'xl','sy'}, dimensions={0} | all-to-all | bytes 131072 | tf_op jit(solution)/shard_map/all_to_all | solution.py:499
  99.9 0.1 rows.4
  100.0 14.1 %all_to_all.65.refs_0_ = f32[16,4,128]{2,1,0:T(4,128)S(1)} all-to-all(f32[16,4,128]{2,1,0:T(4,128)S(1)} %get-tuple-element.70), channel_id=1, replica_groups=mesh['z'=16,'xl'=2,'sy'=16] {'z'}, dimensions={0} | all-to-all | bytes 65536 | tf_op jit(solution)/shard_map/all_to_all | solution.py:503
  114.1 0.8 direction.4
  114.9 12.2 %all_to_all.66.arrived = f32[32,8,128]{2,1,0:T(8,128)S(1)} all-to-all(f32[32,8,128]{2,1,0:T(8,128)S(1)} %get-tuple-element.72), channel_id=1, replica_groups=mesh['z'=16,'xl'=2,'sy'=16] {'xl','sy'}, dimensions={0} | all-to-all | bytes 262144 | tf_op jit(solution)/shard_map/all_to_all | solution.py:511
  127.1 14.1 %all_to_all.67.arrived = f32[16,4,128]{2,1,0:T(4,128)S(1)} all-to-all(f32[16,4,128]{2,1,0:T(4,128)S(1)} %get-tuple-element.74), channel_id=1, replica_groups=mesh['z'=16,'xl'=2,'sy'=16] {'z'}, dimensions={0} | all-to-all | bytes 65536 | tf_op jit(solution)/shard_map/all_to_all | solution.py:513
  141.2 1.3 next.3
  142.4 11.8 %all_to_all.68.arrived = f32[32,4,128]{2,1,0:T(4,128)S(1)} all-to-all(f32[32,4,128]{2,1,0:T(4,128)S(1)} %get-tuple-element.77), channel_id=1, replica_groups=mesh['z'=16,'xl'=2,'sy'=16] {'xl','sy'}, dimensions={0} | all-to-all | bytes 131072 | tf_op jit(solution)/shard_map/all_to_all | solution.py:499
  154.2 0.1 rows.5
  154.4 14.1 %all_to_all.69.refs_0_ = f32[16,4,128]{2,1,0:T(4,128)S(1)} all-to-all(f32[16,4,128]{2,1,0:T(4,128)S(1)} %get-tuple-element.79), channel_id=1, replica_groups=mesh['z'=16,'xl'=2,'sy'=16] {'z'}, dimensions={0} | all-to-all | bytes 65536 | tf_op jit(solution)/shard_map/all_to_all | solution.py:503
  168.4 0.8 direction.5
  169.2 12.2 %all_to_all.70.arrived = f32[32,8,128]{2,1,0:T(8,128)S(1)} all-to-all(f32[32,8,128]{2,1,0:T(8,128)S(1)} %get-tuple-element.81), channel_id=1, replica_groups=mesh['z'=16,'xl'=2,'sy'=16] {'xl','sy'}, dimensions={0} | all-to-all | bytes 262144 | tf_op jit(solution)/shard_map/all_to_all | solution.py:511
  181.4 14.1 %all_to_all.71.arrived = f32[16,4,128]{2,1,0:T(4,128)S(1)} all-to-all(f32[16,4,128]{2,1,0:T(4,128)S(1)} %get-tuple-element.83), channel_id=1, replica_groups=mesh['z'=16,'xl'=2,'sy'=16] {'z'}, dimensions={0} | all-to-all | bytes 65536 | tf_op jit(solution)/shard_map/all_to_all | solution.py:513
  195.5 0.9 last.1
  (4 shorter events, 0.2 us)
Async XLA Ops:
  2.5 57.1 %copy-start = (f32[1,1,768,768]{3,2,1,0:T(8,128)S(1)}, f32[1,1,768,768]{3,2,1,0:T(8,128)}, u32[]{:S(2)}) copy-start(f32[1,1,768,768]{3,2,1,0:T(8,128)} %param.9) | copy-start | bytes 7077892
  2.5 13.6 %collective-permute-start = (f32[32,256]{1,0:T(8,128)S(1)}, f32[32,256]{1,0:T(8,128)S(1)}, u32[]{:S(2)}, u32[]{:S(2)}) collective-permute-start(f32[32,256]{1,0:T(8,128)S(1)} %get-tuple-element.45), channel_id=1, source_target_pairs={{16,32},{32,16},{48,64},{64,48},{80,96},{96,80},{112,128},{128,112... | collective-permute-start | bytes 98312 | tf_op jit(solution)/shard_map/ppermute | solution.py:452
  3.3 12.8 %collective-permute-start.1 = (f32[32,256]{1,0:T(8,128)S(1)}, f32[32,256]{1,0:T(8,128)S(1)}, u32[]{:S(2)}, u32[]{:S(2)}) collective-permute-start(f32[32,256]{1,0:T(8,128)S(1)} %get-tuple-element.46), channel_id=1, source_target_pairs={{1,2},{2,1},{3,4},{4,3},{5,6},{6,5},{7,8},{8,7},{9,10},{10,9},{11,... | collective-permute-start | bytes 98312 | tf_op jit(solution)/shard_map/ppermute | solution.py:452
  7.9 8.2 %collective-permute-start.2 = (f32[32,256]{1,0:T(8,128)S(1)}, f32[32,256]{1,0:T(8,128)S(1)}, u32[]{:S(2)}, u32[]{:S(2)}) collective-permute-start(f32[32,256]{1,0:T(8,128)S(1)} %get-tuple-element.47), channel_id=1, source_target_pairs={{0,16},{16,0},{32,48},{48,32},{64,80},{80,64},{96,112},{112,96},{1... | collective-permute-start | bytes 98312 | tf_op jit(solution)/shard_map/ppermute | solution.py:452
  14.1 3.1 %collective-permute-start.3 = (f32[32,256]{1,0:T(8,128)S(1)}, f32[32,256]{1,0:T(8,128)S(1)}, u32[]{:S(2)}, u32[]{:S(2)}) collective-permute-start(f32[32,256]{1,0:T(8,128)S(1)} %get-tuple-element.48), channel_id=1, source_target_pairs={{0,1},{1,0},{2,3},{3,2},{4,5},{5,4},{6,7},{7,6},{8,9},{9,8},{10,11... | collective-permute-start | bytes 98312 | tf_op jit(solution)/shard_map/ppermute | solution.py:452

commit v8 on v7

--- a/solution.py
+++ b/solution.py
@@ -81,8 +81,9 @@
     return found[:, 0:LANES] + found[:, LANES : 2 * LANES] + found[:, 2 * LANES : 3 * LANES]
 
 
-def apply_matrix(tile, group_row, hits, matrix_ref):
-    width = matrix_ref.shape[0]
+def apply_matrix(tile, group_row, hits, *matrix_refs):
+    width = matrix_refs[0].shape[1]
+    held = matrix_refs[0].shape[0] // LANES
     ours = group_row == iota((TILE, TILE * LANES), 0)
     none = jnp.zeros((TILE, TILE * LANES), jnp.float32)
     parts = bf16_parts(jnp.where(ours, as_row(tile), 0.0))
@@ -92,7 +93,8 @@
     place = iota((TILE, LANES), 1) - iota((TILE, LANES), 0)
     rows = []
     for b in range(width // LANES):
-        block = slice(b * LANES, (b + 1) * LANES)
+        matrix_ref, first = matrix_refs[b // held], b % held * LANES
+        block = slice(first, first + LANES)
         acc = matrix_ref[block, 0:LANES] * local[0:1]
         for t in range(1, width // LANES):
             acc = acc + matrix_ref[block, t * LANES : (t + 1) * LANES] * local[t : t + 1]
@@ -170,9 +172,9 @@
     return jnp.concatenate([partner[0:2], south, partner[4:6], north], axis=0)
 
 
-def apply_schur(tile, group_row, hits, mask_row, schur_ref, modes_ref, near_ref, rt_ref, l_ref, out_ref):
+def apply_schur(tile, group_row, hits, mask_row, schur_refs, modes_ref, near_ref, rt_ref, l_ref, out_ref):
     chunks = out_ref.shape[0]
-    y_row = apply_matrix(tile, group_row, hits, schur_ref)
+    y_row = apply_matrix(tile, group_row, hits, *schur_refs)
     load = coarse_load(0.25 * mask_row * y_row, modes_ref, near_ref, rt_ref, l_ref, chunks)
     y = as_tile(y_row)
     gamma = jnp.broadcast_to(0.25 * total(tile * y), (1, LANES))
@@ -213,7 +215,7 @@
             )
         )
     ]
-    matrix = pltpu.make_async_copy(schur_hbm.at[0, 0], out_schur, sems.at[len(copies)])
+    matrix = pltpu.make_async_copy(schur_hbm.at[0, 0, pl.ds(0, out_schur.shape[0])], out_schur, sems.at[len(copies)])
     for copy in copies:
         copy.start()
     matrix.start()
@@ -273,12 +275,29 @@
     return jnp.where(iota((TILE, LANES), 1) < block, window[:, 0:LANES], 0.0)
 
 
+def load_kernel(schur_hbm, coarse_hbm, lower_out, blocks_out, coarse_ref, sems):
+    half = lower_out.shape[0]
+    matrix = pltpu.make_async_copy(schur_hbm.at[0, 0, pl.ds(half, half)], lower_out, sems.at[0])
+    copy = pltpu.make_async_copy(coarse_hbm, coarse_ref, sems.at[1])
+    copy.start()
+    matrix.start()
+    copy.wait()
+    chunks, ncoarse = blocks_out.shape[0], coarse_ref.shape[1]
+    block = ncoarse // chunks
+    wide = (-(-ncoarse // LANES) + 1) * LANES
+    coarse = jnp.concatenate([coarse_ref[...], jnp.zeros((TILE - NDOF, ncoarse), jnp.float32)], axis=0)
+    coarse = jnp.pad(coarse, ((0, 0), (0, wide - ncoarse)))
+    for p in range(chunks):
+        blocks_out[p] = column_chunk(coarse, p, block)
+    matrix.wait()
+
+
 def start_kernel(
-    own_ref, row_cross, col_odd, row_pair, col_even, cmap_ref, group_ref, hits_ref, schur_ref, modes_ref, coarse_hbm, out_ref,
-    state, near, r_ref, rt_ref, l_ref, mask_row_ref, coarse_ref, sem,
+    own_ref, row_cross, col_odd, row_pair, col_even, cmap_ref, group_ref, hits_ref, upper_ref, lower_ref, modes_ref, blocks_ref,
+    out_ref,
+    state, near, r_ref, rt_ref, l_ref, mask_row_ref,
 ):
-    copy = pltpu.make_async_copy(coarse_hbm, coarse_ref, sem)
-    copy.start()
+    schur_refs = (upper_ref, lower_ref)
     chunks = out_ref.shape[0]
     block = NDOF * chunks // 2
     row, cm = CORNERS, CORNERS + 2
@@ -308,14 +327,9 @@
     r_ref[...] = hit_row.astype(jnp.bfloat16)
     rt_ref[...] = jnp.transpose(hit_row).astype(jnp.bfloat16)
     l_ref[...] = jnp.where(inside == lanes, 1.0, 0.0)
-    y = apply_schur(residual, group_ref[...], hits_ref[...], mask_row, schur_ref, modes_ref, near, rt_ref, l_ref, out_ref)
-    copy.wait()
-    ncoarse = coarse_ref.shape[1]
-    wide = (-(-ncoarse // LANES) + 1) * LANES
-    coarse = jnp.concatenate([coarse_ref[...], jnp.zeros((TILE - NDOF, ncoarse), jnp.float32)], axis=0)
-    coarse = jnp.pad(coarse, ((0, 0), (0, wide - ncoarse)))
+    y = apply_schur(residual, group_ref[...], hits_ref[...], mask_row, schur_refs, modes_ref, near, rt_ref, l_ref, out_ref)
     for p in range(chunks):
-        out_ref[p, TILE : 2 * TILE, :] = column_chunk(coarse, p, block)
+        out_ref[p, TILE : 2 * TILE, :] = blocks_ref[p]
     state[...] = jnp.zeros(state.shape, jnp.float32)
     state[RES : RES + TILE, :] = residual
     state[IFACE : IFACE + TILE, :] = y
@@ -412,12 +426,12 @@
 
 
 def next_kernel(
-    arrived, state_in, whole_load, modes_ref, near_ref, r_ref, l_ref, rt_ref, mask_row_ref, group_ref, hits_ref, schur_ref,
+    arrived, state_in, whole_load, modes_ref, near_ref, r_ref, l_ref, rt_ref, mask_row_ref, group_ref, hits_ref, upper_ref, lower_ref,
     out_ref, state,
 ):
     multipliers, residual = advance(arrived, state_in, whole_load, modes_ref, near_ref, r_ref, l_ref)
     y = apply_schur(
-        residual, group_ref[...], hits_ref[...], mask_row_ref[...], schur_ref, modes_ref, near_ref, rt_ref, l_ref, out_ref
+        residual, group_ref[...], hits_ref[...], mask_row_ref[...], (upper_ref, lower_ref), modes_ref, near_ref, rt_ref, l_ref, out_ref
     )
     state[...] = state_in[...]
     state[RES : RES + TILE, :] = residual
@@ -457,14 +471,14 @@
     width = kinv.shape[-1]
     kinv = kinv.reshape(width, width)
     ints = jnp.int32
-    own_modes, col_even, col_odd, row_pair, row_cross, own, group, hits, cmap, schur = call(
+    own_modes, col_even, col_odd, row_pair, row_cross, own, group, hits, cmap, upper = call(
         pack_kernel,
         in_hbm(links, corner_modes, edge_map, gap, corner_map, schur),
         [(CORNERS, TILE * LANES)]
         + [(CORNERS + 8, SLOT)] * 4
         + [(TILE, SLOT), jax.ShapeDtypeStruct((1, TILE * LANES), ints)]
         + [jax.ShapeDtypeStruct((LANES, TILE * LANES), jnp.bfloat16)]
-        + [(1, SLOT), (width, width)],
+        + [(1, SLOT), (width // 2, width)],
         in_specs=[HBM] * 6,
         scratch=[
             pltpu.VMEM(links.shape, ints),
@@ -480,18 +494,23 @@
     col_odd = swapped(col_odd, "sy", 1)
     row_pair = swapped(row_pair, ROWS_AXES, 0)
     col_even = swapped(col_even, "sy", 0)
+    lower, blocks = call(
+        load_kernel,
+        in_hbm(schur, coarse_inverse),
+        [(width // 2, width), (chunks, TILE, LANES)],
+        in_specs=[HBM] * 2,
+        scratch=[pltpu.VMEM(coarse_inverse.shape, jnp.float32), pltpu.SemaphoreType.DMA((2,))],
+        name="load",
+    )
     hits_shape = jax.ShapeDtypeStruct((LANES, LANES), jnp.bfloat16)
     state_shape = (NSTATE, LANES)
     out, state, near, r, rt, l, mask_row = call(
         start_kernel,
         (
-            own, row_cross, col_odd, row_pair, col_even, cmap, group, hits, schur, own_modes,
-            *in_hbm(coarse_inverse),
+            own, row_cross, col_odd, row_pair, col_even, cmap, group, hits, upper, lower, own_modes, blocks,
         ),
         [(chunks, 2 * TILE, LANES), state_shape, (CORNERS, TILE * LANES), hits_shape, hits_shape]
         + [(LANES, LANES), (1, TILE * LANES)],
-        in_specs=[VMEM] * 10 + [HBM],
-        scratch=[pltpu.VMEM(coarse_inverse.shape, jnp.float32), pltpu.SemaphoreType.DMA(())],
         name="start",
     )
     to_plane, to_plane_short, to_z = (chunks, TILE, LANES), (chunks, 4, LANES), (levels, 4, LANES)
@@ -514,7 +533,7 @@
         common = (arrived, state, load, own_modes, near, r, l)
         if step + 1 < ITERS:
             out, state = call(
-                next_kernel, common + (rt, mask_row, group, hits, schur), [to_plane_short, state_shape], name="next"
+                next_kernel, common + (rt, mask_row, group, hits, upper, lower), [to_plane_short, state_shape], name="next"
             )
     return tuple(
         call(

time: 197 us -> 197 us (level)
    pallas_call x14 -> x15, Pallas kernels: 9.2 us -> 10 us  [call(): pl.pallas_call(kernel, out_shape=shapes, in_specs=in_specs or [VMEM] * le...]
  transfers between devices with their start and end apart: 4 -> 4, of which waited for: 1 -> 0; matrix products, arithmetic and copies ran while one was open for 0% -> 0% of each run, Pallas kernels for 0% -> 1%
where the time goes in v8:
time: 197 us; the launch traced here: 196 us
  blocking collectives  172 us (87%)
  starting transfers between devices  13.4 us (7%)
  Pallas kernels  10 us (5%)
    all_to_all x6, blocking collectives, on_device(): arrived = lax.all_to_all(out, 'z', 0, 0, tiled=True)  95.7 us
    all_to_all x6, blocking collectives, on_device(): arrived = lax.all_to_all(out, PLANE, 0, 0, tiled=True)  76.4 us
    ppermute x4, starting transfers between devices, swapped(): return lax.ppermute(block, axis, route)  13.4 us
    pallas_call x15, Pallas kernels, call(): pl.pallas_call(kernel, out_shape=shapes, in_specs=in_specs or [VMEM] * le...  10 us
  transfers between devices with their start and end apart: 4, of which 0 were waited for; matrix products, arithmetic and copies ran while one was open for 0% of the time, Pallas kernels for 1%

profile of v8, /device:TPU:1, one launch (start us, length us, event | category | flops | bytes accessed | tf_op | source)
XLA Modules:
  0.0 196.3 jit_solution(7655513108073752093)
XLA Ops:
  0.6 1.4 pack.1
  2.1 0.7 collective-permute-start
  2.7 4.6 %collective-permute-start.1 = (f32[32,256]{1,0:T(8,128)S(1)}, f32[32,256]{1,0:T(8,128)S(1)}, u32[]{:S(2)}, u32[]{:S(2)}) collective-permute-start(f32[32,256]{1,0:T(8,128)S(1)} %get-tuple-element.48), channel_id=1, source_target_pairs={{1,2},{2,1},{3,4},{4,3},{5,6},{6,5},{7,8},{8,7},{9,10},{10,9},{11,... | collective-permute-start | bytes 98312 | tf_op jit(solution)/shard_map/ppermute | solution.py:466
  7.3 6.3 %collective-permute-start.2 = (f32[32,256]{1,0:T(8,128)S(1)}, f32[32,256]{1,0:T(8,128)S(1)}, u32[]{:S(2)}, u32[]{:S(2)}) collective-permute-start(f32[32,256]{1,0:T(8,128)S(1)} %get-tuple-element.49), channel_id=1, source_target_pairs={{0,16},{16,0},{32,48},{48,32},{64,80},{80,64},{96,112},{112,96},{1... | collective-permute-start | bytes 98312 | tf_op jit(solution)/shard_map/ppermute | solution.py:466
  13.6 1.9 collective-permute-start.3
  15.5 1.4 load.1
  16.9 0.0 copy-start
  16.9 0.0 collective-permute-done.row_cross
  16.9 0.0 collective-permute-done.1.col_odd
  16.9 0.0 collective-permute-done.2.row_pair
  16.9 0.0 collective-permute-done.3.col_even
  17.0 1.1 start.1
  18.0 16.2 %all_to_all.60.arrived.refs_5_ = f32[32,16,128]{2,1,0:T(8,128)S(1)} all-to-all(f32[32,16,128]{2,1,0:T(8,128)S(1)} %get-tuple-element.58), channel_id=1, replica_groups=mesh['z'=16,'xl'=2,'sy'=16] {'xl','sy'}, dimensions={0} | all-to-all | bytes 524288 | tf_op jit(solution)/shard_map/all_to_all | solution.py:518
  34.2 25.3 %all_to_all.61.refs_0_ = f32[16,4,128]{2,1,0:T(4,128)S(1)} all-to-all(f32[16,4,128]{2,1,0:T(4,128)S(1)} %get-tuple-element.60), channel_id=1, replica_groups=mesh['z'=16,'xl'=2,'sy'=16] {'z'}, dimensions={0} | all-to-all | bytes 65536 | tf_op jit(solution)/shard_map/all_to_all | solution.py:522
  59.5 0.0 copy-done
  59.5 0.8 direction.3
  60.3 12.3 %all_to_all.62.arrived = f32[32,8,128]{2,1,0:T(8,128)S(1)} all-to-all(f32[32,8,128]{2,1,0:T(8,128)S(1)} %get-tuple-element.62), channel_id=1, replica_groups=mesh['z'=16,'xl'=2,'sy'=16] {'xl','sy'}, dimensions={0} | all-to-all | bytes 262144 | tf_op jit(solution)/shard_map/all_to_all | solution.py:530
  72.7 14.1 %all_to_all.63.arrived = f32[16,4,128]{2,1,0:T(4,128)S(1)} all-to-all(f32[16,4,128]{2,1,0:T(4,128)S(1)} %get-tuple-element.64), channel_id=1, replica_groups=mesh['z'=16,'xl'=2,'sy'=16] {'z'}, dimensions={0} | all-to-all | bytes 65536 | tf_op jit(solution)/shard_map/all_to_all | solution.py:532
  86.7 1.3 next.2
  88.0 11.8 %all_to_all.64.arrived = f32[32,4,128]{2,1,0:T(4,128)S(1)} all-to-all(f32[32,4,128]{2,1,0:T(4,128)S(1)} %get-tuple-element.72), channel_id=1, replica_groups=mesh['z'=16,'xl'=2,'sy'=16] {'xl','sy'}, dimensions={0} | all-to-all | bytes 131072 | tf_op jit(solution)/shard_map/all_to_all | solution.py:518
  99.8 0.1 rows.4
  99.9 14.1 %all_to_all.65.refs_0_ = f32[16,4,128]{2,1,0:T(4,128)S(1)} all-to-all(f32[16,4,128]{2,1,0:T(4,128)S(1)} %get-tuple-element.74), channel_id=1, replica_groups=mesh['z'=16,'xl'=2,'sy'=16] {'z'}, dimensions={0} | all-to-all | bytes 65536 | tf_op jit(solution)/shard_map/all_to_all | solution.py:522
  114.0 0.8 direction.4
  114.8 12.2 %all_to_all.66.arrived = f32[32,8,128]{2,1,0:T(8,128)S(1)} all-to-all(f32[32,8,128]{2,1,0:T(8,128)S(1)} %get-tuple-element.76), channel_id=1, replica_groups=mesh['z'=16,'xl'=2,'sy'=16] {'xl','sy'}, dimensions={0} | all-to-all | bytes 262144 | tf_op jit(solution)/shard_map/all_to_all | solution.py:530
  127.0 14.1 %all_to_all.67.arrived = f32[16,4,128]{2,1,0:T(4,128)S(1)} all-to-all(f32[16,4,128]{2,1,0:T(4,128)S(1)} %get-tuple-element.78), channel_id=1, replica_groups=mesh['z'=16,'xl'=2,'sy'=16] {'z'}, dimensions={0} | all-to-all | bytes 65536 | tf_op jit(solution)/shard_map/all_to_all | solution.py:532
  141.1 1.3 next.3
  142.4 11.8 %all_to_all.68.arrived = f32[32,4,128]{2,1,0:T(4,128)S(1)} all-to-all(f32[32,4,128]{2,1,0:T(4,128)S(1)} %get-tuple-element.81), channel_id=1, replica_groups=mesh['z'=16,'xl'=2,'sy'=16] {'xl','sy'}, dimensions={0} | all-to-all | bytes 131072 | tf_op jit(solution)/shard_map/all_to_all | solution.py:518
  154.2 0.1 rows.5
  154.3 14.1 %all_to_all.69.refs_0_ = f32[16,4,128]{2,1,0:T(4,128)S(1)} all-to-all(f32[16,4,128]{2,1,0:T(4,128)S(1)} %get-tuple-element.83), channel_id=1, replica_groups=mesh['z'=16,'xl'=2,'sy'=16] {'z'}, dimensions={0} | all-to-all | bytes 65536 | tf_op jit(solution)/shard_map/all_to_all | solution.py:522
  168.3 0.8 direction.5
  169.1 12.2 %all_to_all.70.arrived = f32[32,8,128]{2,1,0:T(8,128)S(1)} all-to-all(f32[32,8,128]{2,1,0:T(8,128)S(1)} %get-tuple-element.85), channel_id=1, replica_groups=mesh['z'=16,'xl'=2,'sy'=16] {'xl','sy'}, dimensions={0} | all-to-all | bytes 262144 | tf_op jit(solution)/shard_map/all_to_all | solution.py:530
  181.3 14.1 %all_to_all.71.arrived = f32[16,4,128]{2,1,0:T(4,128)S(1)} all-to-all(f32[16,4,128]{2,1,0:T(4,128)S(1)} %get-tuple-element.87), channel_id=1, replica_groups=mesh['z'=16,'xl'=2,'sy'=16] {'z'}, dimensions={0} | all-to-all | bytes 65536 | tf_op jit(solution)/shard_map/all_to_all | solution.py:532
  195.4 0.9 last.1
  (4 shorter events, 0.2 us)
Async XLA Ops:
  2.1 14.8 %collective-permute-start = (f32[32,256]{1,0:T(8,128)S(1)}, f32[32,256]{1,0:T(8,128)S(1)}, u32[]{:S(2)}, u32[]{:S(2)}) collective-permute-start(f32[32,256]{1,0:T(8,128)S(1)} %get-tuple-element.47), channel_id=1, source_target_pairs={{16,32},{32,16},{48,64},{64,48},{80,96},{96,80},{112,128},{128,112... | collective-permute-start | bytes 98312 | tf_op jit(solution)/shard_map/ppermute | solution.py:466
  2.7 14.2 %collective-permute-start.1 = (f32[32,256]{1,0:T(8,128)S(1)}, f32[32,256]{1,0:T(8,128)S(1)}, u32[]{:S(2)}, u32[]{:S(2)}) collective-permute-start(f32[32,256]{1,0:T(8,128)S(1)} %get-tuple-element.48), channel_id=1, source_target_pairs={{1,2},{2,1},{3,4},{4,3},{5,6},{6,5},{7,8},{8,7},{9,10},{10,9},{11,... | collective-permute-start | bytes 98312 | tf_op jit(solution)/shard_map/ppermute | solution.py:466
  7.3 9.6 %collective-permute-start.2 = (f32[32,256]{1,0:T(8,128)S(1)}, f32[32,256]{1,0:T(8,128)S(1)}, u32[]{:S(2)}, u32[]{:S(2)}) collective-permute-start(f32[32,256]{1,0:T(8,128)S(1)} %get-tuple-element.49), channel_id=1, source_target_pairs={{0,16},{16,0},{32,48},{48,32},{64,80},{80,64},{96,112},{112,96},{1... | collective-permute-start | bytes 98312 | tf_op jit(solution)/shard_map/ppermute | solution.py:466
  13.6 3.3 %collective-permute-start.3 = (f32[32,256]{1,0:T(8,128)S(1)}, f32[32,256]{1,0:T(8,128)S(1)}, u32[]{:S(2)}, u32[]{:S(2)}) collective-permute-start(f32[32,256]{1,0:T(8,128)S(1)} %get-tuple-element.50), channel_id=1, source_target_pairs={{0,1},{1,0},{2,3},{3,2},{4,5},{5,4},{6,7},{7,6},{8,9},{9,8},{10,11... | collective-permute-start | bytes 98312 | tf_op jit(solution)/shard_map/ppermute | solution.py:466
  16.9 42.6 %copy-start = (f32[1,1,768,768]{3,2,1,0:T(8,128)S(1)}, f32[1,1,768,768]{3,2,1,0:T(8,128)}, u32[]{:S(2)}) copy-start(f32[1,1,768,768]{3,2,1,0:T(8,128)} %param.9) | copy-start | bytes 7077892

commit v9 on v8

--- a/solution.py
+++ b/solution.py
@@ -210,7 +210,7 @@
         pltpu.make_async_copy(source, target, sems.at[k])
         for k, (source, target) in enumerate(
             (
-                (modes_hbm, modes_ref), (map_hbm, map_ref), (gap_hbm, gap_ref), (cmap_hbm, cmap_ref),
+                (map_hbm, map_ref), (modes_hbm, modes_ref), (gap_hbm, gap_ref), (cmap_hbm, cmap_ref),
                 (links_hbm, links_ref),
             )
         )
@@ -219,8 +219,7 @@
     for copy in copies:
         copy.start()
     matrix.start()
-    for copy in copies:
-        copy.wait()
+    copies[0].wait()
     nrows, ncols = lax.axis_size("z") * lax.axis_size("xl"), lax.axis_size("sy")
     row_here = lax.axis_index("z") * lax.axis_size("xl") + lax.axis_index("xl")
     map_row = jnp.concatenate(slots(map_ref[0], 4, -1), axis=1)
@@ -229,6 +228,7 @@
     hits = jnp.where(map_row - LANES * group == iota((LANES, TILE * LANES), 0), 1.0, 0.0)
     hits = jnp.where(group >= 0, hits, 0.0).astype(jnp.bfloat16)
     out_hits[...] = hits
+    copies[1].wait()
     count = modes_ref.shape[3] // LANES
     parts = [modes_ref[0, 0, :, t * LANES : (t + 1) * LANES] for t in range(count)]
     parts = bf16_parts(jnp.concatenate(parts, axis=0)).astype(jnp.bfloat16)
@@ -238,6 +238,8 @@
         pieces = [found[(count * k + t) * CORNERS : (count * k + t + 1) * CORNERS] for k in range(3)]
         acc = acc + jnp.where(group == t, pieces[0] + pieces[1] + pieces[2], 0.0)
     out_modes[...] = acc
+    for copy in copies[2:]:
+        copy.wait()
     links = jnp.where(links_ref[0] == 1, 1.0, 0.0)
     east = jnp.where(lax.axis_index("sy") < ncols - 1, links[:, 0:1], 0.0)
     south = jnp.where(row_here < nrows - 1, links[:, 1:2], 0.0)

time: 197 us -> 197 us (level)
  no operation moved by 1% of the time
where the time goes in v9:
time: 197 us; the launch traced here: 196 us
  blocking collectives  172 us (87%)
  starting transfers between devices  13.4 us (7%)
  Pallas kernels  10 us (5%)
    all_to_all x6, blocking collectives, on_device(): arrived = lax.all_to_all(out, 'z', 0, 0, tiled=True)  95.7 us
    all_to_all x6, blocking collectives, on_device(): arrived = lax.all_to_all(out, PLANE, 0, 0, tiled=True)  76.4 us
    ppermute x4, starting transfers between devices, swapped(): return lax.ppermute(block, axis, route)  13.4 us
    pallas_call x15, Pallas kernels, call(): pl.pallas_call(kernel, out_shape=shapes, in_specs=in_specs or [VMEM] * le...  10 us
  transfers between devices with their start and end apart: 4, of which 0 were waited for; matrix products, arithmetic and copies ran while one was open for 0% of the time, Pallas kernels for 1%

profile of v9, /device:TPU:1, one launch (start us, length us, event | category | flops | bytes accessed | tf_op | source)
XLA Modules:
  0.0 196.3 jit_solution(12449548958468609549)
XLA Ops:
  0.6 1.4 pack.1
  2.1 0.7 collective-permute-start
  2.7 4.6 %collective-permute-start.1 = (f32[32,256]{1,0:T(8,128)S(1)}, f32[32,256]{1,0:T(8,128)S(1)}, u32[]{:S(2)}, u32[]{:S(2)}) collective-permute-start(f32[32,256]{1,0:T(8,128)S(1)} %get-tuple-element.48), channel_id=1, source_target_pairs={{1,2},{2,1},{3,4},{4,3},{5,6},{6,5},{7,8},{8,7},{9,10},{10,9},{11,... | collective-permute-start | bytes 98312 | tf_op jit(solution)/shard_map/ppermute | solution.py:468
  7.3 6.3 %collective-permute-start.2 = (f32[32,256]{1,0:T(8,128)S(1)}, f32[32,256]{1,0:T(8,128)S(1)}, u32[]{:S(2)}, u32[]{:S(2)}) collective-permute-start(f32[32,256]{1,0:T(8,128)S(1)} %get-tuple-element.49), channel_id=1, source_target_pairs={{0,16},{16,0},{32,48},{48,32},{64,80},{80,64},{96,112},{112,96},{1... | collective-permute-start | bytes 98312 | tf_op jit(solution)/shard_map/ppermute | solution.py:468
  13.6 1.9 collective-permute-start.3
  15.5 1.4 load.1
  16.9 0.0 copy-start
  16.9 0.0 collective-permute-done.row_cross
  16.9 0.0 collective-permute-done.1.col_odd
  16.9 0.0 collective-permute-done.2.row_pair
  16.9 0.0 collective-permute-done.3.col_even
  17.0 1.1 start.1
  18.0 16.2 %all_to_all.60.arrived.refs_5_ = f32[32,16,128]{2,1,0:T(8,128)S(1)} all-to-all(f32[32,16,128]{2,1,0:T(8,128)S(1)} %get-tuple-element.58), channel_id=1, replica_groups=mesh['z'=16,'xl'=2,'sy'=16] {'xl','sy'}, dimensions={0} | all-to-all | bytes 524288 | tf_op jit(solution)/shard_map/all_to_all | solution.py:520
  34.2 25.3 %all_to_all.61.refs_0_ = f32[16,4,128]{2,1,0:T(4,128)S(1)} all-to-all(f32[16,4,128]{2,1,0:T(4,128)S(1)} %get-tuple-element.60), channel_id=1, replica_groups=mesh['z'=16,'xl'=2,'sy'=16] {'z'}, dimensions={0} | all-to-all | bytes 65536 | tf_op jit(solution)/shard_map/all_to_all | solution.py:524
  59.5 0.0 copy-done
  59.5 0.8 direction.3
  60.3 12.3 %all_to_all.62.arrived = f32[32,8,128]{2,1,0:T(8,128)S(1)} all-to-all(f32[32,8,128]{2,1,0:T(8,128)S(1)} %get-tuple-element.62), channel_id=1, replica_groups=mesh['z'=16,'xl'=2,'sy'=16] {'xl','sy'}, dimensions={0} | all-to-all | bytes 262144 | tf_op jit(solution)/shard_map/all_to_all | solution.py:532
  72.7 14.1 %all_to_all.63.arrived = f32[16,4,128]{2,1,0:T(4,128)S(1)} all-to-all(f32[16,4,128]{2,1,0:T(4,128)S(1)} %get-tuple-element.64), channel_id=1, replica_groups=mesh['z'=16,'xl'=2,'sy'=16] {'z'}, dimensions={0} | all-to-all | bytes 65536 | tf_op jit(solution)/shard_map/all_to_all | solution.py:534
  86.7 1.3 next.2
  88.0 11.8 %all_to_all.64.arrived = f32[32,4,128]{2,1,0:T(4,128)S(1)} all-to-all(f32[32,4,128]{2,1,0:T(4,128)S(1)} %get-tuple-element.72), channel_id=1, replica_groups=mesh['z'=16,'xl'=2,'sy'=16] {'xl','sy'}, dimensions={0} | all-to-all | bytes 131072 | tf_op jit(solution)/shard_map/all_to_all | solution.py:520
  99.8 0.1 rows.4
  99.9 14.1 %all_to_all.65.refs_0_ = f32[16,4,128]{2,1,0:T(4,128)S(1)} all-to-all(f32[16,4,128]{2,1,0:T(4,128)S(1)} %get-tuple-element.74), channel_id=1, replica_groups=mesh['z'=16,'xl'=2,'sy'=16] {'z'}, dimensions={0} | all-to-all | bytes 65536 | tf_op jit(solution)/shard_map/all_to_all | solution.py:524
  114.0 0.8 direction.4
  114.8 12.2 %all_to_all.66.arrived = f32[32,8,128]{2,1,0:T(8,128)S(1)} all-to-all(f32[32,8,128]{2,1,0:T(8,128)S(1)} %get-tuple-element.76), channel_id=1, replica_groups=mesh['z'=16,'xl'=2,'sy'=16] {'xl','sy'}, dimensions={0} | all-to-all | bytes 262144 | tf_op jit(solution)/shard_map/all_to_all | solution.py:532
  127.0 14.1 %all_to_all.67.arrived = f32[16,4,128]{2,1,0:T(4,128)S(1)} all-to-all(f32[16,4,128]{2,1,0:T(4,128)S(1)} %get-tuple-element.78), channel_id=1, replica_groups=mesh['z'=16,'xl'=2,'sy'=16] {'z'}, dimensions={0} | all-to-all | bytes 65536 | tf_op jit(solution)/shard_map/all_to_all | solution.py:534
  141.1 1.3 next.3
  142.4 11.8 %all_to_all.68.arrived = f32[32,4,128]{2,1,0:T(4,128)S(1)} all-to-all(f32[32,4,128]{2,1,0:T(4,128)S(1)} %get-tuple-element.81), channel_id=1, replica_groups=mesh['z'=16,'xl'=2,'sy'=16] {'xl','sy'}, dimensions={0} | all-to-all | bytes 131072 | tf_op jit(solution)/shard_map/all_to_all | solution.py:520
  154.2 0.1 rows.5
  154.3 14.1 %all_to_all.69.refs_0_ = f32[16,4,128]{2,1,0:T(4,128)S(1)} all-to-all(f32[16,4,128]{2,1,0:T(4,128)S(1)} %get-tuple-element.83), channel_id=1, replica_groups=mesh['z'=16,'xl'=2,'sy'=16] {'z'}, dimensions={0} | all-to-all | bytes 65536 | tf_op jit(solution)/shard_map/all_to_all | solution.py:524
  168.3 0.8 direction.5
  169.1 12.2 %all_to_all.70.arrived = f32[32,8,128]{2,1,0:T(8,128)S(1)} all-to-all(f32[32,8,128]{2,1,0:T(8,128)S(1)} %get-tuple-element.85), channel_id=1, replica_groups=mesh['z'=16,'xl'=2,'sy'=16] {'xl','sy'}, dimensions={0} | all-to-all | bytes 262144 | tf_op jit(solution)/shard_map/all_to_all | solution.py:532
  181.3 14.1 %all_to_all.71.arrived = f32[16,4,128]{2,1,0:T(4,128)S(1)} all-to-all(f32[16,4,128]{2,1,0:T(4,128)S(1)} %get-tuple-element.87), channel_id=1, replica_groups=mesh['z'=16,'xl'=2,'sy'=16] {'z'}, dimensions={0} | all-to-all | bytes 65536 | tf_op jit(solution)/shard_map/all_to_all | solution.py:534
  195.4 0.9 last.1
  (4 shorter events, 0.2 us)
Async XLA Ops:
  2.1 14.8 %collective-permute-start = (f32[32,256]{1,0:T(8,128)S(1)}, f32[32,256]{1,0:T(8,128)S(1)}, u32[]{:S(2)}, u32[]{:S(2)}) collective-permute-start(f32[32,256]{1,0:T(8,128)S(1)} %get-tuple-element.47), channel_id=1, source_target_pairs={{16,32},{32,16},{48,64},{64,48},{80,96},{96,80},{112,128},{128,112... | collective-permute-start | bytes 98312 | tf_op jit(solution)/shard_map/ppermute | solution.py:468
  2.7 14.2 %collective-permute-start.1 = (f32[32,256]{1,0:T(8,128)S(1)}, f32[32,256]{1,0:T(8,128)S(1)}, u32[]{:S(2)}, u32[]{:S(2)}) collective-permute-start(f32[32,256]{1,0:T(8,128)S(1)} %get-tuple-element.48), channel_id=1, source_target_pairs={{1,2},{2,1},{3,4},{4,3},{5,6},{6,5},{7,8},{8,7},{9,10},{10,9},{11,... | collective-permute-start | bytes 98312 | tf_op jit(solution)/shard_map/ppermute | solution.py:468
  7.3 9.6 %collective-permute-start.2 = (f32[32,256]{1,0:T(8,128)S(1)}, f32[32,256]{1,0:T(8,128)S(1)}, u32[]{:S(2)}, u32[]{:S(2)}) collective-permute-start(f32[32,256]{1,0:T(8,128)S(1)} %get-tuple-element.49), channel_id=1, source_target_pairs={{0,16},{16,0},{32,48},{48,32},{64,80},{80,64},{96,112},{112,96},{1... | collective-permute-start | bytes 98312 | tf_op jit(solution)/shard_map/ppermute | solution.py:468
  13.6 3.3 %collective-permute-start.3 = (f32[32,256]{1,0:T(8,128)S(1)}, f32[32,256]{1,0:T(8,128)S(1)}, u32[]{:S(2)}, u32[]{:S(2)}) collective-permute-start(f32[32,256]{1,0:T(8,128)S(1)} %get-tuple-element.50), channel_id=1, source_target_pairs={{0,1},{1,0},{2,3},{3,2},{4,5},{5,4},{6,7},{7,6},{8,9},{9,8},{10,11... | collective-permute-start | bytes 98312 | tf_op jit(solution)/shard_map/ppermute | solution.py:468
  16.9 42.6 %copy-start = (f32[1,1,768,768]{3,2,1,0:T(8,128)S(1)}, f32[1,1,768,768]{3,2,1,0:T(8,128)}, u32[]{:S(2)}) copy-start(f32[1,1,768,768]{3,2,1,0:T(8,128)} %param.9) | copy-start | bytes 7077892
